TPU v7x, 1024 devices: a whole 8x8x8 slice. The times are simulated.
1024 devices in a mesh: blk: 64 (over z, x), pair: 16 (over y, core).
Axes of the slice: x: 8, y: 8, z: 8, core: 2. Of those that a mesh axis runs over, the one named last changes fastest.
Arguments:
- centroids: float32 [3, 65536], P(None, 'blk'), may hold values from -6 to 6
- normals: float32 [3, 65536], P(None, 'blk'), may hold values from -4 to 4
- areas: float32 [65536], P('blk'), may hold values from 0.3 to 3
- cotangent: float32 [], replicated, may hold values from 6.1035156e-05 to 0.00024414062
- pair_code: int32 [64, 16, 64, 1], P('blk', 'pair'), may hold values from -1 to 15, as said below
- corner_vertex: int32 [3, 73728], P(None, 'blk'), may hold values from -1 to 511, as said below
Outputs:
- vertex_grad: float32 [3, 32768], P(None, 'blk')
- face_grad: float32 [4, 65536], P(None, 'blk')
Inputs may be any that keep to these rules, and one draw needn't show every extreme that they name: `pair_code`: an entry other than -1 at (q, p, b, c) is t * 4 + s with target block t of blk index b and source block s of blk index q, never the same block. `corner_vertex`: every corner of every face is named by exactly one entry other than -1 over all windows, in the window of the blk index that owns its vertex.
All inputs are finite; a program needn't handle non-finite values.
Results may differ from a plain program's by a relative error of at most 0.0003.
Values sent between devices are 32-bit elements; how exact they have to be, the bound alone decides.
No kernel may reach another device: no remote copies, remote signals or barrier semaphores. Data moves between devices by JAX's collectives and lax.ppermute only.
A program may use at most 32 MiB of HBM per device.

v0:
```python
import jax
import jax.numpy as jnp
from jax import lax
from jax.sharding import PartitionSpec as P

BLOCK = 256
FB_DEV = 4
HALO_FACES = 64


soften = 1.0
tile_group = 4


def extended_2(cells, sides, width):
    for axis, dim in sides:
        count = lax.axis_size(axis)
        head = lax.slice_in_dim(cells, 0, width, axis=dim)
        tail = lax.slice_in_dim(cells, cells.shape[dim] - width, cells.shape[dim], axis=dim)
        cells = jnp.concatenate(
            [
                lax.ppermute(tail, axis, [(i, (i + 1) % count) for i in range(count)]),
                cells,
                lax.ppermute(head, axis, [((i + 1) % count, i) for i in range(count)]),
            ],
            axis=dim,
        )
    return cells


def pair_terms(center_blocks, normal_blocks, area_blocks, sources, targets, cotangent):
    slot_count = targets.shape[0]
    block_width = center_blocks.shape[2]
    blocks = center_blocks.shape[1]
    active = targets >= 0
    active_count = jnp.sum(active.astype(jnp.int32))
    ordering = jnp.argsort(jnp.where(active, 0, 1).astype(jnp.int32), stable=True)
    rounds = (active_count + tile_group - 1) // tile_group
    target_init = jnp.zeros((7, blocks, block_width), jnp.float32)
    source_init = jnp.zeros((4, slot_count, block_width), jnp.float32)

    def one_round(round_index, totals):
        target_sum, source_sum = totals
        picked = lax.dynamic_slice_in_dim(
            ordering, (round_index * tile_group).astype(jnp.int32), tile_group
        )
        chosen = targets[picked]
        weight_on = (chosen >= 0).astype(jnp.float32)
        target_block = jnp.maximum(chosen, 0).astype(jnp.int32)
        source_rows = sources[:, picked]
        target_center = center_blocks[:, target_block]
        target_normal = normal_blocks[:, target_block]
        target_area = area_blocks[target_block]
        offsets = target_center[:, :, :, None] - source_rows[0:3, :, None, :]
        projected = jnp.sum(target_normal[:, :, :, None] * offsets, axis=0)
        distance = jnp.sum(offsets * offsets, axis=0) + soften
        numerator = projected * projected + soften
        inverse = 1.0 / (distance * distance)
        kernel = numerator * inverse
        weight = (
            cotangent
            * weight_on[:, None, None]
            * target_area[:, :, None]
            * source_rows[3][:, None, :]
        )
        pulling = 2.0 * weight * projected * inverse
        pushing = 4.0 * weight * numerator * inverse / distance
        forces = pulling[None] * target_normal[:, :, :, None] - pushing[None] * offsets
        energy_rate = cotangent * weight_on[:, None, None] * kernel
        target_part = jnp.concatenate(
            [
                jnp.sum(forces, axis=-1),
                jnp.sum(pulling[None] * offsets, axis=-1),
                jnp.sum(energy_rate * source_rows[3][:, None, :], axis=-1)[None],
            ],
            axis=0,
        )
        source_part = jnp.concatenate(
            [
                -jnp.sum(forces, axis=-2),
                jnp.sum(energy_rate * target_area[:, :, None], axis=-2)[None],
            ],
            axis=0,
        )
        pick_table = (target_block[:, None] == jnp.arange(blocks, dtype=jnp.int32)[None, :]).astype(
            jnp.float32
        ) * weight_on[:, None]
        target_sum = target_sum + jnp.einsum(
            "gf,kgb->kfb", pick_table, target_part, precision=lax.Precision.HIGHEST
        )
        source_sum = source_sum.at[:, picked].add(source_part)
        return (target_sum, source_sum)

    return lax.fori_loop(jnp.int32(0), rounds, one_round, (target_init, source_init))


def shards(centroids, normals, areas, cotangent, pair_code, corner_vertex):
    block_width = BLOCK
    blocks = FB_DEV
    devices = lax.axis_size("blk")
    center_blocks = centroids.reshape(3, blocks, block_width)
    normal_blocks = normals.reshape(3, blocks, block_width)
    area_blocks = areas.reshape(blocks, block_width)
    all_centers, all_areas, all_codes = (
        lax.all_gather(centroids, "blk", axis=1, tiled=True),
        lax.all_gather(areas, "blk", axis=0, tiled=True),
        lax.all_gather(pair_code, "blk", axis=0, tiled=True),
    )
    myself = lax.axis_index("blk")
    incoming = lax.dynamic_index_in_dim(all_codes[:, 0], myself, 1, keepdims=False)
    live_in = incoming >= 0
    owner = jnp.arange(devices, dtype=jnp.int32)[:, None]
    global_block = (owner * blocks + jnp.where(live_in, incoming % blocks, 0)).reshape(-1)
    targets = jnp.where(live_in, incoming // blocks, -1).reshape(-1)
    source_rows = jnp.concatenate(
        [
            all_centers.reshape(3, devices * blocks, block_width)[:, global_block],
            all_areas.reshape(devices * blocks, block_width)[global_block][None],
        ],
        axis=0,
    )
    target_sum, source_sum = pair_terms(
        center_blocks, normal_blocks, area_blocks, source_rows, targets, cotangent
    )
    spread = (
        jnp.zeros((4, devices * blocks, block_width), jnp.float32)
        .at[:, global_block]
        .add(source_sum)
    )
    returned = lax.psum_scatter(spread, "blk", scatter_dimension=1, tiled=True)
    combined = target_sum.at[0:3].add(returned[0:3]).at[6].add(returned[3])
    summed = lax.psum(combined.reshape(7, blocks * block_width), "pair")
    extended = extended_2(summed[0:3], (("blk", 1),), HALO_FACES)
    columns = jnp.arange(blocks * block_width // 2, dtype=jnp.int32)[None, :]
    incidence = (
        (corner_vertex[0][:, None] == columns).astype(jnp.float32)
        + (corner_vertex[1][:, None] == columns).astype(jnp.float32)
        + (corner_vertex[2][:, None] == columns).astype(jnp.float32)
    )
    vertex_grad = jnp.dot(extended, incidence, precision=lax.Precision.HIGHEST) / 3.0
    return (vertex_grad, summed[3:7])


def solution(mesh):
    placed = (
        P(None, "blk"),
        P(None, "blk"),
        P("blk"),
        P(),
        P("blk", "pair", None, None),
        P(None, "blk"),
    )
    return jax.shard_map(
        shards,
        mesh=mesh,
        in_specs=placed,
        out_specs=(P(None, "blk"), P(None, "blk")),
        check_vma=False,
    )
```

profile of v0, /device:TPU:1, one launch (start us, length us, event | category | flops | bytes accessed | tf_op | source)
XLA Modules:
  0.0 533.1 jit_solution(5714161076953515178)
XLA Ops:
  7.2 46.4 %all_gather.9 = s32[64,1,64,1]{2,3,1,0:T(1,128)S(1)} all-gather(s32[1,1,64,1]{2,3,1,0:T(1,128)} %param.16), channel_id=1, replica_groups=mesh['blk'=64,'pair'=16] {'blk'}, dimensions={0}, use_global_device_ids=true | all-gather | bytes 16640 | tf_op jit(solution)/shard_map/all_gather | solution.py:107
  53.6 1.3 dynamic-slice_reduce_fusion
  56.3 34.5 %all_gather.11 = f32[65536]{0:T(1024)S(1)} all-gather(f32[1024]{0:T(1024)} %param.14), channel_id=1, replica_groups=mesh['blk'=64,'pair'=16] {'blk'}, dimensions={0}, use_global_device_ids=true | all-gather | bytes 266240 | tf_op jit(solution)/shard_map/all_gather | solution.py:106
  91.4 37.8 %all_gather.10 = f32[3,65536]{1,0:T(4,128)S(1)} all-gather(f32[3,1024]{1,0:T(4,128)} %param.12), channel_id=1, replica_groups=mesh['blk'=64,'pair'=16] {'blk'}, dimensions={1}, use_global_device_ids=true | all-gather | bytes 798720 | tf_op jit(solution)/shard_map/all_gather | solution.py:105
  130.9 2.1 sort.17
  133.1 105.0 %while.14 = (s32[]{:T(128)}, f32[7,4,256]{2,1,0:T(4,128)S(1)}, f32[4,64,256]{2,0,1:T(4,128)S(1)}, s32[]{:T(128)}, s32[64]{0:T(128)S(1)}, /*index=5*/s32[64]{0:T(...) while((s32[]{:T(128)}, f32[7,4,256]{2,1,0:T(4,128)S(1)}, ...), condition=%wide.region_11.12_spmd, body=%wide.region_2.11_spmd.sunk | while | flops 15048774 | bytes 11043363 | solution.py:94
  138.7 1.9 fusion.52
  147.4 1.9 fusion.52
  156.2 1.9 fusion.52
  164.9 1.9 fusion.52
  173.7 1.9 fusion.52
  182.4 1.9 fusion.52
  191.2 1.9 fusion.52
  199.9 1.9 fusion.52
  208.7 1.9 fusion.52
  217.4 1.9 fusion.52
  226.2 1.9 fusion.52
  234.9 1.9 fusion.52
  238.3 2.8 scatter_fusion.1
  244.2 221.1 %all-reduce.3.cloned.1.call-done = f32[4,256,256]{2,0,1:T(4,128)} async-done(((f32[4,256,256]{2,0,1:T(4,128)}), f32[4,256,256]{2,0,1:T(4,128)}) %all-reduce.3.cloned.1.call-update) | async-done | bytes 1048592
  466.9 47.2 %psum.7 = f32[7,1024]{1,0:T(8,128)S(1)} all-reduce(f32[7,1024]{1,0:T(8,128)S(1)} %bitcast.65), channel_id=1, replica_groups=mesh['blk'=64,'pair'=16] {'pair'}, use_global_device_ids=true, to_apply=%region_14.15 | all-reduce | flops 7168 | bytes 57344 | tf_op jit(solution)/shard_map/psum | solution.py:132
  514.2 2.5 collective-permute-start
  516.7 6.1 %collective-permute-start.1 = (f32[3,64]{1,0:T(4,128)S(1)}, f32[3,64]{1,0:T(4,128)S(1)}, u32[]{:S(2)}, u32[]{:S(2)}) collective-permute-start(f32[3,64]{1,0:T(4,128)S(1)} %get-tuple-element.126), channel_id=1, source_target_pairs={{16,0},{32,16},{48,32},{64,48},{80,64},{96,80},{112,96},{128,112},... | collective-permute-start | bytes 2312 | tf_op jit(solution)/shard_map/ppermute | solution.py:24
  523.6 2.6 fusion.33
  (337 shorter events, 88.7 us)
Async XLA Ops:
  7.2 458.1 %all-reduce.3.cloned.1.call-start = ((), (), s32[]{:S(2)}) async-start(), calls=%async_computation | async-start | bytes 2097152
  129.3 3.8 copy-start.1
  129.3 3.8 copy-start.2
  238.3 284.5 %copy-start.3 = (s32[3,1152]{1,0:T(4,128)S(1)}, s32[3,1152]{1,0:T(4,128)}, u32[]{:S(2)}) copy-start(s32[3,1152]{1,0:T(4,128)} %param.17) | copy-start | bytes 41476
  241.2 1.0 copy-start
  514.2 9.3 %collective-permute-start = (f32[3,64]{1,0:T(4,128)S(1)}, f32[3,64]{1,0:T(4,128)S(1)}, u32[]{:S(2)}, u32[]{:S(2)}) collective-permute-start(f32[3,64]{1,0:T(4,128)S(1)} %get-tuple-element.127), channel_id=1, source_target_pairs={{0,16},{16,32},{32,48},{48,64},{64,80},{80,96},{96,112},{112,128},... | collective-permute-start | bytes 2312 | tf_op jit(solution)/shard_map/ppermute | solution.py:22
  516.7 6.8 %collective-permute-start.1 = (f32[3,64]{1,0:T(4,128)S(1)}, f32[3,64]{1,0:T(4,128)S(1)}, u32[]{:S(2)}, u32[]{:S(2)}) collective-permute-start(f32[3,64]{1,0:T(4,128)S(1)} %get-tuple-element.126), channel_id=1, source_target_pairs={{16,0},{32,16},{48,32},{64,48},{80,64},{96,80},{112,96},{128,112},... | collective-permute-start | bytes 2312 | tf_op jit(solution)/shard_map/ppermute | solution.py:24
Sparse Core Ops, SparseCore 0:
  242.3 222.8 all-reduce.2
where the time goes:
time: 536 us; the launch traced here: 533 us
  waiting for transfers between devices  221 us (41%)
  blocking collectives  166 us (31%)
  other arithmetic  73.1 us (14%)
  local copies, waits for them, and re-layouts  42.5 us (8%)
  between operations  15.6 us (3%)
  starting transfers between devices  8.63 us (2%)
    unnamed x2, waiting for transfers between devices  221 us
    psum x1, blocking collectives, shards(): summed = lax.psum(combined.reshape(7, blocks * block_width), 'pair')  47.2 us
    all_gather x1, blocking collectives, shards(): lax.all_gather(pair_code, 'blk', axis=0, tiled=True)  46.4 us
    all_gather x1, blocking collectives, shards(): lax.all_gather(centroids, 'blk', axis=1, tiled=True)  37.8 us
    all_gather x1, blocking collectives, shards(): lax.all_gather(areas, 'blk', axis=0, tiled=True)  34.5 us
    reduce_sum x12, other arithmetic, one_round(): jnp.sum(forces, axis=-2)  23 us
    reduce_sum x12, other arithmetic, one_round(): distance = jnp.sum(offsets * offsets, axis=0) + soften  13.4 us
  transfers between devices with their start and end apart: 3, of which 1 were waited for; matrix products, arithmetic and copies ran while one was open for 0% of the time, Pallas kernels for 0%

commit v1 on v0

v1 whole, which is shorter than its diff:
```python
import functools

import jax
import jax.numpy as jnp
from jax import lax
from jax.experimental import pallas as pl
from jax.experimental.pallas import tpu as pltpu
from jax.sharding import PartitionSpec as P

BLOCK = 256
FB_DEV = 4
HALO_FACES = 64
CODES = FB_DEV * FB_DEV
ROWS = 32
F32 = jnp.float32
VMEM = pl.BlockSpec(memory_space=pltpu.VMEM)
SMEM = pl.BlockSpec(memory_space=pltpu.SMEM)


def fold(values):
    return jnp.sum(values.reshape(ROWS // 8, 8, BLOCK), axis=0)


def reciprocal(values):
    guess = pl.reciprocal(values, approx=True)
    return guess * (2.0 - values * guess)


def cell(own, partner_ref, block, count, as_target):
    def step(at, totals):
        rows = partner_ref[block, pl.ds(pl.multiple_of(at * ROWS, ROWS), ROWS), :]
        column = [rows[:, c : c + 1] for c in range(7)]
        offset = [own[c] - column[c] for c in range(3)]
        normal = own[3:6] if as_target else column[3:6]
        projected = normal[0] * offset[0] + normal[1] * offset[1] + normal[2] * offset[2]
        distance = offset[0] * offset[0] + offset[1] * offset[1] + (offset[2] * offset[2] + 1.0)
        inverse = reciprocal(distance)
        weight = inverse * inverse * (column[6] * count)
        kernel = (projected * projected + 1.0) * weight
        pulling = projected * weight
        pushing = kernel * inverse
        terms = [kernel] + [pushing * offset[c] for c in range(3)]
        if as_target:
            terms += [pulling] + [pulling * offset[c] for c in range(3)]
        else:
            terms += [pulling * normal[c] for c in range(3)]
        return tuple(t + fold(v) for t, v in zip(totals, terms))

    zero = jnp.zeros((8, BLOCK), F32)
    return lax.fori_loop(0, BLOCK // ROWS, step, (zero,) * (8 if as_target else 7), unroll=2)


def pair_kernel(as_target, own_blocks, group, codes_ref, scale_ref, own_ref, *refs):
    partners, (base_ref, out_ref, cols_ref, acc_ref, count_ref) = refs[:group], refs[group:]
    shares = codes_ref.shape[1]
    slots = group * CODES

    def clear(i, carry):
        count_ref[i] = 0
        return carry

    lax.fori_loop(0, slots, clear, 0)

    def tally(i, carry):
        code = codes_ref[i // shares, i % shares]

        @pl.when(code >= 0)
        def _():
            at = (i // shares) * CODES + code
            count_ref[at] = count_ref[at] + 1

        return carry

    lax.fori_loop(0, group * shares, tally, 0)

    for k in range(group):
        for s in range(FB_DEV):
            cols_ref[k * FB_DEV + s, :, 0:8] = partners[k][:, s * BLOCK : (s + 1) * BLOCK].T
    acc_ref[...] = jnp.zeros_like(acc_ref)

    def visit(i, carry):
        count = count_ref[i]
        code = i % CODES
        first, second = code // FB_DEV, code % FB_DEV
        mine, other = (first, second) if as_target else (second, first)
        wanted = count > 0
        if len(own_blocks) < FB_DEV:
            wanted = jnp.logical_and(wanted, functools.reduce(jnp.logical_or, [mine == o for o in own_blocks]))

        @pl.when(wanted)
        def _():
            columns = pl.ds(pl.multiple_of(mine * BLOCK, BLOCK), BLOCK)
            own = [own_ref[c : c + 1, columns] for c in range(6)]
            sums = cell(own, cols_ref, (i // CODES) * FB_DEV + other, count.astype(F32), as_target)
            for f, value in enumerate(sums):
                acc_ref[f, :, columns] += value

        return carry

    lax.fori_loop(0, slots, visit, 0)

    scale = scale_ref[0, 0]
    for at, o in enumerate(own_blocks):
        columns = slice(o * BLOCK, (o + 1) * BLOCK)
        sums = [jnp.sum(acc_ref[f, :, columns], axis=0, keepdims=True) for f in range(8 if as_target else 7)]
        weight = scale * own_ref[6:7, columns]
        target = slice(at * BLOCK, (at + 1) * BLOCK)
        for c in range(3):
            lever = own_ref[3 + c : 4 + c, columns] * sums[4] if as_target else sums[4 + c]
            center = weight * (2.0 * lever - 4.0 * sums[1 + c])
            normal = 2.0 * weight * sums[5 + c] if as_target else jnp.zeros_like(weight)
            if as_target:
                center = center + base_ref[c : c + 1, columns]
            out_ref[c : c + 1, target] = center
            out_ref[3 + c : 4 + c, target] = normal
        area = scale * sums[0]
        if as_target:
            area = area + base_ref[6:7, columns]
        out_ref[6:7, target] = area
        out_ref[7:8, target] = jnp.zeros_like(area)


def pair_sums(as_target, own_blocks, codes, scale, own, partners, base, name):
    group = len(partners)
    cells = group * CODES * len(own_blocks) // FB_DEV // 3
    return pl.pallas_call(
        functools.partial(pair_kernel, as_target, own_blocks, group),
        out_shape=jax.ShapeDtypeStruct((8, len(own_blocks) * BLOCK), F32),
        in_specs=[SMEM, SMEM] + [VMEM] * (group + 2),
        out_specs=VMEM,
        scratch_shapes=[
            pltpu.VMEM((group * FB_DEV, BLOCK, 128), F32),
            pltpu.VMEM((8, 8, FB_DEV * BLOCK), F32),
            pltpu.SMEM((group * CODES,), jnp.int32),
        ],
        compiler_params=pltpu.CompilerParams(vmem_limit_bytes=24 * 1024 * 1024),
        cost_estimate=pl.CostEstimate(
            flops=cells * BLOCK * BLOCK * 40, bytes_accessed=1 << 18, transcendentals=cells * BLOCK * BLOCK
        ),
        name=name,
    )(codes, scale, own, *partners, base)


def incidence_kernel(corner_ref, out_ref):
    verts, faces = out_ref.shape
    vertex = lax.broadcasted_iota(jnp.int32, (verts, 128), 0)
    for e in range(0, faces, 128):
        total = jnp.zeros((verts, 128), F32)
        for k in range(3):
            total = total + jnp.where(corner_ref[k : k + 1, e : e + 128] == vertex, 1.0, 0.0)
        out_ref[:, e : e + 128] = total.astype(jnp.bfloat16)


def incidence_table(corner, verts):
    faces = corner.shape[1]
    return pl.pallas_call(
        incidence_kernel,
        out_shape=jax.ShapeDtypeStruct((verts, faces), jnp.bfloat16),
        in_specs=[VMEM],
        out_specs=VMEM,
        compiler_params=pltpu.CompilerParams(vmem_limit_bytes=16 * 1024 * 1024),
        cost_estimate=pl.CostEstimate(flops=verts * faces * 9, bytes_accessed=verts * faces * 2, transcendentals=0),
        name="incidence",
    )(corner)


def thirds(values):
    high = values.astype(jnp.bfloat16)
    rest = values - high.astype(F32)
    middle = rest.astype(jnp.bfloat16)
    low = (rest - middle.astype(F32)).astype(jnp.bfloat16)
    return [high, middle, low]


def finish_kernel(parts_ref, table_ref, vertex_ref, face_ref):
    total = parts_ref[0]
    for i in range(1, parts_ref.shape[0]):
        total = total + parts_ref[i]
    faces = total.shape[1]
    width = 2 * HALO_FACES
    face_ref[...] = total[3:7]
    edge = jnp.concatenate([total[7:8, c * width : (c + 1) * width] for c in range(3)], axis=0)
    contract = (((1,), (1,)), ((), ()))
    out = jnp.zeros((3, vertex_ref.shape[1]), F32)
    for high, side in zip(thirds(total[0:3]), thirds(edge)):
        out = out + lax.dot_general(high, table_ref[:, 0:faces], contract, preferred_element_type=F32)
        out = out + lax.dot_general(side, table_ref[:, faces:], contract, preferred_element_type=F32)
    vertex_ref[...] = out / 3.0


def finish(parts, table):
    verts, faces = table.shape[0], parts.shape[2]
    return pl.pallas_call(
        finish_kernel,
        out_shape=(jax.ShapeDtypeStruct((3, verts), F32), jax.ShapeDtypeStruct((4, faces), F32)),
        in_specs=[VMEM, VMEM],
        out_specs=(VMEM, VMEM),
        compiler_params=pltpu.CompilerParams(vmem_limit_bytes=16 * 1024 * 1024),
        name="finish",
    )(parts, table)


def shards(centroids, normals, areas, cotangent, pair_code, corner_vertex):
    count, shares = lax.axis_size("blk"), lax.axis_size("pair")
    group = count // shares
    both = ("blk", "pair")
    blk = lax.axis_index("blk")
    faces = centroids.shape[1]

    def route(k):
        pairs = []
        for b in range(count):
            for p in range(shares):
                q = group * p + (b + k) % group
                pairs.append((q * shares + b // group, b * shares + p))
        return pairs

    own = jnp.concatenate([centroids, normals, areas[None], jnp.zeros((1, faces), F32)], axis=0)
    partners = [lax.ppermute(own, both, route(k)) for k in range(group)]
    held = lax.all_to_all(pair_code.reshape(shares, group), "pair", 0, 0, tiled=True).T
    held_twice = jnp.concatenate([held, held], axis=0)
    lane = blk % group
    codes_out = lax.dynamic_slice_in_dim(held_twice, lane, group, axis=0)
    codes_in = jnp.concatenate(
        [
            lax.ppermute(lax.dynamic_slice_in_dim(held, (blk + group - k) % group, 1, axis=0), both, route(k))
            for k in range(group)
        ],
        axis=0,
    )
    scale = cotangent.reshape(1, 1)
    corner = jnp.concatenate(
        [corner_vertex[:, HALO_FACES:-HALO_FACES], corner_vertex[:, :HALO_FACES], corner_vertex[:, -HALO_FACES:]], axis=1
    )
    table = incidence_table(corner, faces // 2)

    sent = pair_sums(False, (0, 1, 2, 3), codes_out, scale, own, partners, own, "source_role")
    outer = pair_sums(True, (0, 3), codes_in, scale, own, partners, sent, "target_role_outer")
    head, tail = outer[0:3, :HALO_FACES], outer[0:3, -HALO_FACES:]
    forward = [(i, (i + 1) % count) for i in range(count)]
    left = lax.ppermute(tail, "blk", forward)
    right = lax.ppermute(head, "blk", [(j, i) for i, j in forward])
    inner = pair_sums(True, (1, 2), codes_in, scale, own, partners, sent, "target_role_inner")
    edge = jnp.concatenate([left, right], axis=1).reshape(1, -1)
    edge = jnp.pad(edge, ((0, 0), (0, faces - edge.shape[1])))
    part = jnp.concatenate([outer[:, :BLOCK], inner, outer[:, BLOCK:]], axis=1)
    part = jnp.concatenate([part[:7], edge], axis=0)
    parts = lax.all_gather(part, "pair")
    return finish(parts, table)


def solution(mesh):
    placed = (
        P(None, "blk"),
        P(None, "blk"),
        P("blk"),
        P(),
        P("blk", "pair", None, None),
        P(None, "blk"),
    )
    return jax.shard_map(
        shards,
        mesh=mesh,
        in_specs=placed,
        out_specs=(P(None, "blk"), P(None, "blk")),
        check_vma=False,
    )
```

time: 536 us -> 177 us (0.33)
  waiting for transfers between devices: 221 us -> 10 us
  blocking collectives: 166 us -> 37.4 us
  other arithmetic: 73.1 us -> 2.25 us
  starting transfers between devices: 8.63 us -> 71.8 us
  Pallas kernels: 0 us -> 47.9 us
  local copies, waits for them, and re-layouts: 42.5 us -> 4.42 us
  between operations: 15.6 us -> 1.49 us
    unnamed x2 -> x0, waiting for transfers between devices: 221 us -> none
    all_gather x3 -> x1, blocking collectives: 119 us -> 37.4 us  [shards(): parts = lax.all_gather(part, 'pair')]
    pallas_call x0 -> x5, Pallas kernels: none -> 47.9 us  [the longest x3 45.5 us: pair_sums(): pl.pallas_call(functools.partial(pair_kernel, as_target, own_blocks, grou...]
    psum x1 -> x0, blocking collectives: 47.2 us -> none  [shards(): summed = lax.psum(combined.reshape(7, blocks * block_width), 'pair')]
    reduce_sum x37 -> x0, other arithmetic: 41.6 us -> none  [the longest x12 23 us: one_round(): jnp.sum(forces, axis=-2)]
    gather x86 -> x0, local copies, waits for them, and re-layouts: 36.6 us -> none  [the longest x12 7.65 us: one_round(): chosen = targets[picked]]
    ppermute x2 -> x10, starting transfers between devices: 8.59 us -> 43.4 us  [the longest x4 18.8 us: shards(): partners = [lax.ppermute(own, both, route(k)) for k in range(group)]]
    all_to_all x0 -> x1, starting transfers between devices: none -> 28.5 us  [shards(): lax.all_to_all(pair_code.reshape(shares, group), 'pair', 0, 0, tiled=True)]
  transfers between devices with their start and end apart: 3 -> 11, of which waited for: 1 -> 4; matrix products, arithmetic and copies ran while one was open for 0% -> 3% of each run, Pallas kernels for 0% -> 7%
where the time goes in v1:
time: 177 us; the launch traced here: 175 us
  starting transfers between devices  71.8 us (41%)
  Pallas kernels  47.9 us (27%)
  blocking collectives  37.4 us (21%)
  waiting for transfers between devices  10 us (6%)
  local copies, waits for them, and re-layouts  4.42 us (2%)
  other arithmetic  2.25 us (1%)
    pallas_call x3, Pallas kernels, pair_sums(): pl.pallas_call(functools.partial(pair_kernel, as_target, own_blocks, grou...  45.5 us
    all_gather x1, blocking collectives, shards(): parts = lax.all_gather(part, 'pair')  37.4 us
    all_to_all x1, starting transfers between devices, shards(): lax.all_to_all(pair_code.reshape(shares, group), 'pair', 0, 0, tiled=True)  28.5 us
    ppermute x4, starting transfers between devices, shards(): partners = [lax.ppermute(own, both, route(k)) for k in range(group)]  18.8 us
    ppermute x4, starting transfers between devices, shards(): lax.ppermute(lax.dynamic_slice_in_dim(held, (blk + group - k) % group, 1,...  16 us
    ppermute x1, starting transfers between devices, shards(): right = lax.ppermute(head, 'blk', [(j, i) for i, j in forward])  6.68 us
    ppermute x4, waiting for transfers between devices, shards(): partners = [lax.ppermute(own, both, route(k)) for k in range(group)]  4.92 us
    all_to_all x1, waiting for transfers between devices, shards(): lax.all_to_all(pair_code.reshape(shares, group), 'pair', 0, 0, tiled=True)  3.84 us
  transfers between devices with their start and end apart: 11, of which 4 were waited for; matrix products, arithmetic and copies ran while one was open for 3% of the time, Pallas kernels for 7%

profile of v1, /device:TPU:1, one launch (start us, length us, event | category | flops | bytes accessed | tf_op | source)
XLA Modules:
  0.0 175.3 jit_solution(8127293196278754059)
XLA Ops:
  0.7 0.8 maximum_maximum_fusion.own_ref.refs_4_
  1.5 7.6 %collective-permute-start.7 = (f32[8,1024]{1,0:T(8,128)S(1)}, f32[8,1024]{1,0:T(8,128)S(1)}, u32[]{:S(2)}, u32[]{:S(2)}) collective-permute-start(f32[8,1024]{1,0:T(8,128)S(1)} %maximum_maximum_fusion.own_ref.refs_4_), channel_id=1, source_target_pairs={{48,0},{112,1},{176,2},{240,3},{304,4},{368,5},{432,6},{496,7},{56... | collective-permute-start | bytes 98312 | tf_op jit(solution)/shard_map/ppermute | solution.py:219
  9.2 2.8 %collective-permute-start.6 = (f32[8,1024]{1,0:T(8,128)S(1)}, f32[8,1024]{1,0:T(8,128)S(1)}, u32[]{:S(2)}, u32[]{:S(2)}) collective-permute-start(f32[8,1024]{1,0:T(8,128)S(1)} %maximum_maximum_fusion.own_ref.refs_4_), channel_id=1, source_target_pairs={{32,0},{96,1},{160,2},{224,3},{288,4},{352,5},{416,6},{480,7},{544... | collective-permute-start | bytes 98312 | tf_op jit(solution)/shard_map/ppermute | solution.py:219
  11.9 4.0 %collective-permute-start.5 = (f32[8,1024]{1,0:T(8,128)S(1)}, f32[8,1024]{1,0:T(8,128)S(1)}, u32[]{:S(2)}, u32[]{:S(2)}) collective-permute-start(f32[8,1024]{1,0:T(8,128)S(1)} %maximum_maximum_fusion.own_ref.refs_4_), channel_id=1, source_target_pairs={{16,0},{80,1},{144,2},{208,3},{272,4},{336,5},{400,6},{464,7},{528... | collective-permute-start | bytes 98312 | tf_op jit(solution)/shard_map/ppermute | solution.py:219
  16.5 1.3 reduce.11
  18.5 28.5 %all-to-all-start = ((s32[16,1,4]{2,1,0:T(1,128)}), s32[16,1,4]{2,1,0:T(1,128)S(1)}, u32[]{:S(2)}, u32[]{:S(2)}) async-start(s32[16,1,4]{2,1,0:T(1,128)} %bitcast), calls=%async_computation | async-start | bytes 16384 | tf_op jit(solution)/shard_map/all_to_all | solution.py:220
  47.0 0.8 fusion
  47.7 0.8 slice.29
  50.1 3.8 %all-to-all-done = s32[16,1,4]{2,1,0:T(1,128)S(1)} async-done(((s32[16,1,4]{2,1,0:T(1,128)}), s32[16,1,4]{2,1,0:T(1,128)S(1)}, u32[]{:S(2)}, u32[]{:S(2)}) %all-to-all-start) | async-done | bytes 288 | tf_op jit(solution)/shard_map/all_to_all | solution.py:220
  54.0 1.3 dynamic-slice_reduce_fusion.3
  55.3 5.1 %collective-permute-start.3 = (s32[1,16]{1,0:T(1,128)S(1)}, s32[1,16]{1,0:T(1,128)S(1)}, u32[]{:S(2)}, u32[]{:S(2)}) collective-permute-start(s32[1,16]{1,0:T(1,128)S(1)} %bitcast.29), channel_id=1, source_target_pairs={{48,0},{112,1},{176,2},{240,3},{304,4},{368,5},{432,6},{496,7},{56... | collective-permute-start | bytes 200 | tf_op jit(solution)/shard_map/ppermute | solution.py:226
  60.4 4.4 %collective-permute-start = (s32[1,16]{1,0:T(1,128)S(1)}, s32[1,16]{1,0:T(1,128)S(1)}, u32[]{:S(2)}, u32[]{:S(2)}) collective-permute-start(s32[1,16]{1,0:T(1,128)S(1)} %bitcast.28), channel_id=1, source_target_pairs={{0,0},{64,1},{128,2},{192,3},{256,4},{320,5},{384,6},{448,7},{512,... | collective-permute-start | bytes 200 | tf_op jit(solution)/shard_map/ppermute | solution.py:226
  64.9 3.2 %collective-permute-start.2 = (s32[1,16]{1,0:T(1,128)S(1)}, s32[1,16]{1,0:T(1,128)S(1)}, u32[]{:S(2)}, u32[]{:S(2)}) collective-permute-start(s32[1,16]{1,0:T(1,128)S(1)} %bitcast.27), channel_id=1, source_target_pairs={{32,0},{96,1},{160,2},{224,3},{288,4},{352,5},{416,6},{480,7},{544... | collective-permute-start | bytes 200 | tf_op jit(solution)/shard_map/ppermute | solution.py:226
  68.0 1.1 collective-permute-done
  69.2 3.3 %collective-permute-start.1 = (s32[1,16]{1,0:T(1,128)S(1)}, s32[1,16]{1,0:T(1,128)S(1)}, u32[]{:S(2)}, u32[]{:S(2)}) collective-permute-start(s32[1,16]{1,0:T(1,128)S(1)} %bitcast.26), channel_id=1, source_target_pairs={{16,0},{80,1},{144,2},{208,3},{272,4},{336,5},{400,6},{464,7},{528... | collective-permute-start | bytes 200 | tf_op jit(solution)/shard_map/ppermute | solution.py:226
  72.5 4.4 %collective-permute-start.4 = (f32[8,1024]{1,0:T(8,128)S(1)}, f32[8,1024]{1,0:T(8,128)S(1)}, u32[]{:S(2)}, u32[]{:S(2)}) collective-permute-start(f32[8,1024]{1,0:T(8,128)S(1)} %maximum_maximum_fusion.own_ref.refs_4_), channel_id=1, source_target_pairs={{0,0},{64,1},{128,2},{192,3},{256,4},{320,5},{384,6},{448,7},{512,... | collective-permute-start | bytes 98312 | tf_op jit(solution)/shard_map/ppermute | solution.py:219
  77.1 4.9 %collective-permute-done.4.refs_0_ = f32[8,1024]{1,0:T(8,128)S(1)} collective-permute-done((f32[8,1024]{1,0:T(8,128)S(1)}, f32[8,1024]{1,0:T(8,128)S(1)}, u32[]{:S(2)}, u32[]{:S(2)}) %collective-permute-start.4) | collective-permute-done | bytes 32800 | tf_op jit(solution)/shard_map/ppermute | solution.py:219
  82.0 21.5 %source_role.1.refs_4_ = f32[8,1024]{1,0:T(8,128)S(1)} custom-call(s32[4,16]{1,0:T(4,128)S(1)} %constant_dynamic-slice_fusion.codes_ref, f32[1,1]{1,0:T(1,128)} %bitcast.19.scale_ref, f32[8,1024]{1,0:T(8,128)S(1)} %maximum_maximum_fusion.own_ref.refs_4_, f32[8,1024]{1,0:T(8,128)S(1)} %collective-permute-done.4.refs_0_, ...), custom_call_target="tpu_custom_call" | custom-call | flops 55050240 | bytes 262144 | tf_op jit(solution)/shard_map/source_role/pallas_call | solution.py:126
  103.5 13.3 %target_role_outer.1 = f32[8,512]{1,0:T(8,128)S(1)} custom-call(s32[4,16]{1,0:T(4,128)S(1)} %pad_add_fusion.1.codes_ref, f32[1,1]{1,0:T(1,128)} %bitcast.20.scale_ref, f32[8,1024]{1,0:T(8,128)S(1)} %maximum_maximum_fusion.own_ref.refs_4_, f32[8,1024]{1,0:T(8,128)S(1)} %collective-permute-done.4.refs_0_, f32[8,1024]{1,0:T(8,128)S(1)} %collective-permute-done.5.refs_1_, ...), custom_call_target="tpu_custom_call" | custom-call | flops 26214400 | bytes 262144 | tf_op jit(solution)/shard_map/target_role_outer/pallas_call | solution.py:126
  116.9 1.9 %collective-permute-start.8 = (f32[3,64]{1,0:T(4,128)S(1)}, f32[3,64]{1,0:T(4,128)S(1)}, u32[]{:S(2)}, u32[]{:S(2)}) collective-permute-start(f32[3,64]{1,0:T(4,128)S(1)} %get-tuple-element.10), channel_id=1, source_target_pairs={{0,16},{16,32},{32,48},{48,64},{64,80},{80,96},{96,112},{112,128},... | collective-permute-start | bytes 2312 | tf_op jit(solution)/shard_map/ppermute | solution.py:241
  118.8 6.7 %collective-permute-start.9 = (f32[3,64]{1,0:T(4,128)S(1)}, f32[3,64]{1,0:T(4,128)S(1)}, u32[]{:S(2)}, u32[]{:S(2)}) collective-permute-start(f32[3,64]{1,0:T(4,128)S(1)} %get-tuple-element.11), channel_id=1, source_target_pairs={{16,0},{32,16},{48,32},{64,48},{80,64},{96,80},{112,96},{128,112},... | collective-permute-start | bytes 2312 | tf_op jit(solution)/shard_map/ppermute | solution.py:242
  125.5 10.7 %target_role_inner.1 = f32[8,512]{1,0:T(8,128)S(1)} custom-call(s32[4,16]{1,0:T(4,128)S(1)} %pad_add_fusion.1.codes_ref, f32[1,1]{1,0:T(1,128)} %bitcast.21.scale_ref, f32[8,1024]{1,0:T(8,128)S(1)} %maximum_maximum_fusion.own_ref.refs_4_, f32[8,1024]{1,0:T(8,128)S(1)} %collective-permute-done.4.refs_0_, f32[8,1024]{1,0:T(8,128)S(1)} %collective-permute-done.5.refs_1_, ...), custom_call_target="tpu_custom_call" | custom-call | flops 26214400 | bytes 262144 | tf_op jit(solution)/shard_map/target_role_inner/pallas_call | solution.py:126
  136.3 37.4 %all-gather = f32[128,1024]{1,0:T(8,128)S(1)} all-gather(f32[8,1024]{1,0:T(8,128)S(1)} %select_maximum_fusion), channel_id=2, replica_groups=mesh['blk'=64,'pair'=16] {'pair'}, dimensions={0}, use_global_device_ids=true | all-gather | bytes 557056 | tf_op jit(solution)/shard_map/all_gather | solution.py:248
  173.6 1.6 finish.1
  (22 shorter events, 2.6 us)
Async XLA Ops:
  1.5 75.5 %collective-permute-start.7 = (f32[8,1024]{1,0:T(8,128)S(1)}, f32[8,1024]{1,0:T(8,128)S(1)}, u32[]{:S(2)}, u32[]{:S(2)}) collective-permute-start(f32[8,1024]{1,0:T(8,128)S(1)} %maximum_maximum_fusion.own_ref.refs_4_), channel_id=1, source_target_pairs={{48,0},{112,1},{176,2},{240,3},{304,4},{368,5},{432,6},{496,7},{56... | collective-permute-start | bytes 98312 | tf_op jit(solution)/shard_map/ppermute | solution.py:219
  9.2 67.9 %collective-permute-start.6 = (f32[8,1024]{1,0:T(8,128)S(1)}, f32[8,1024]{1,0:T(8,128)S(1)}, u32[]{:S(2)}, u32[]{:S(2)}) collective-permute-start(f32[8,1024]{1,0:T(8,128)S(1)} %maximum_maximum_fusion.own_ref.refs_4_), channel_id=1, source_target_pairs={{32,0},{96,1},{160,2},{224,3},{288,4},{352,5},{416,6},{480,7},{544... | collective-permute-start | bytes 98312 | tf_op jit(solution)/shard_map/ppermute | solution.py:219
  11.9 65.1 %collective-permute-start.5 = (f32[8,1024]{1,0:T(8,128)S(1)}, f32[8,1024]{1,0:T(8,128)S(1)}, u32[]{:S(2)}, u32[]{:S(2)}) collective-permute-start(f32[8,1024]{1,0:T(8,128)S(1)} %maximum_maximum_fusion.own_ref.refs_4_), channel_id=1, source_target_pairs={{16,0},{80,1},{144,2},{208,3},{272,4},{336,5},{400,6},{464,7},{528... | collective-permute-start | bytes 98312 | tf_op jit(solution)/shard_map/ppermute | solution.py:219
  18.5 35.4 %all-to-all-start = ((s32[16,1,4]{2,1,0:T(1,128)}), s32[16,1,4]{2,1,0:T(1,128)S(1)}, u32[]{:S(2)}, u32[]{:S(2)}) async-start(s32[16,1,4]{2,1,0:T(1,128)} %bitcast), calls=%async_computation | async-start | bytes 16384 | tf_op jit(solution)/shard_map/all_to_all | solution.py:220
  55.3 9.5 %collective-permute-start.3 = (s32[1,16]{1,0:T(1,128)S(1)}, s32[1,16]{1,0:T(1,128)S(1)}, u32[]{:S(2)}, u32[]{:S(2)}) collective-permute-start(s32[1,16]{1,0:T(1,128)S(1)} %bitcast.29), channel_id=1, source_target_pairs={{48,0},{112,1},{176,2},{240,3},{304,4},{368,5},{432,6},{496,7},{56... | collective-permute-start | bytes 200 | tf_op jit(solution)/shard_map/ppermute | solution.py:226
  60.4 8.8 %collective-permute-start = (s32[1,16]{1,0:T(1,128)S(1)}, s32[1,16]{1,0:T(1,128)S(1)}, u32[]{:S(2)}, u32[]{:S(2)}) collective-permute-start(s32[1,16]{1,0:T(1,128)S(1)} %bitcast.28), channel_id=1, source_target_pairs={{0,0},{64,1},{128,2},{192,3},{256,4},{320,5},{384,6},{448,7},{512,... | collective-permute-start | bytes 200 | tf_op jit(solution)/shard_map/ppermute | solution.py:226
  64.9 7.6 %collective-permute-start.2 = (s32[1,16]{1,0:T(1,128)S(1)}, s32[1,16]{1,0:T(1,128)S(1)}, u32[]{:S(2)}, u32[]{:S(2)}) collective-permute-start(s32[1,16]{1,0:T(1,128)S(1)} %bitcast.27), channel_id=1, source_target_pairs={{32,0},{96,1},{160,2},{224,3},{288,4},{352,5},{416,6},{480,7},{544... | collective-permute-start | bytes 200 | tf_op jit(solution)/shard_map/ppermute | solution.py:226
  69.2 7.9 %collective-permute-start.1 = (s32[1,16]{1,0:T(1,128)S(1)}, s32[1,16]{1,0:T(1,128)S(1)}, u32[]{:S(2)}, u32[]{:S(2)}) collective-permute-start(s32[1,16]{1,0:T(1,128)S(1)} %bitcast.26), channel_id=1, source_target_pairs={{16,0},{80,1},{144,2},{208,3},{272,4},{336,5},{400,6},{464,7},{528... | collective-permute-start | bytes 200 | tf_op jit(solution)/shard_map/ppermute | solution.py:226
  72.5 9.5 %collective-permute-start.4 = (f32[8,1024]{1,0:T(8,128)S(1)}, f32[8,1024]{1,0:T(8,128)S(1)}, u32[]{:S(2)}, u32[]{:S(2)}) collective-permute-start(f32[8,1024]{1,0:T(8,128)S(1)} %maximum_maximum_fusion.own_ref.refs_4_), channel_id=1, source_target_pairs={{0,0},{64,1},{128,2},{192,3},{256,4},{320,5},{384,6},{448,7},{512,... | collective-permute-start | bytes 98312 | tf_op jit(solution)/shard_map/ppermute | solution.py:219
  116.9 19.3 %collective-permute-start.8 = (f32[3,64]{1,0:T(4,128)S(1)}, f32[3,64]{1,0:T(4,128)S(1)}, u32[]{:S(2)}, u32[]{:S(2)}) collective-permute-start(f32[3,64]{1,0:T(4,128)S(1)} %get-tuple-element.10), channel_id=1, source_target_pairs={{0,16},{16,32},{32,48},{48,64},{64,80},{80,96},{96,112},{112,128},... | collective-permute-start | bytes 2312 | tf_op jit(solution)/shard_map/ppermute | solution.py:241
  118.8 17.4 %collective-permute-start.9 = (f32[3,64]{1,0:T(4,128)S(1)}, f32[3,64]{1,0:T(4,128)S(1)}, u32[]{:S(2)}, u32[]{:S(2)}) collective-permute-start(f32[3,64]{1,0:T(4,128)S(1)} %get-tuple-element.11), channel_id=1, source_target_pairs={{16,0},{32,16},{48,32},{64,48},{80,64},{96,80},{112,96},{128,112},... | collective-permute-start | bytes 2312 | tf_op jit(solution)/shard_map/ppermute | solution.py:242

commit v2 on v1

v2 whole, which is shorter than its diff:
```python
import functools

import jax
import jax.numpy as jnp
from jax import lax
from jax.experimental import pallas as pl
from jax.experimental.pallas import tpu as pltpu
from jax.sharding import PartitionSpec as P

BLOCK = 256
FB_DEV = 4
HALO_FACES = 64
CODES = FB_DEV * FB_DEV
DEPTH = 64
CELLS = 2
LEFT = (0, 0, 1, 1, 0, 2)
RIGHT = (0, 1, 0, 1, 2, 0)
ONES = (0, 1, 4)
F32 = jnp.float32
BF16 = jnp.bfloat16
VMEM = pl.BlockSpec(memory_space=pltpu.VMEM)
SMEM = pl.BlockSpec(memory_space=pltpu.SMEM)
dot = functools.partial(jnp.dot, preferred_element_type=F32)


def thirds(values):
    high = values.astype(BF16).astype(F32)
    rest = values - high
    middle = rest.astype(BF16).astype(F32)
    return [high, middle, (rest - middle).astype(BF16).astype(F32)]


def square(x):
    return jnp.sum(x[0:3] * x[0:3], axis=0, keepdims=True)


def lever(x):
    return jnp.sum(x[0:3] * x[3:6], axis=0, keepdims=True)


def partner_features(partners, left_ref, feat_ref):
    width = FB_DEV * BLOCK
    row = lax.broadcasted_iota(jnp.int32, (8, width), 0)
    for k, partner in enumerate(partners):
        x = partner[...]
        area = x[6:7]
        x = jnp.where(row >= 6, 1.0, x)
        split = thirds(x)
        extra = thirds(square(x)) + thirds(lever(x)) + [jnp.zeros((10, width), F32)]
        left = jnp.concatenate([split[i] for i in LEFT] + extra, axis=0)
        feat = jnp.concatenate(thirds(x * area) + [jnp.zeros((8, width), F32)], axis=0).astype(BF16)
        for s in range(FB_DEV):
            columns = slice(s * BLOCK, (s + 1) * BLOCK)
            left_ref[k * FB_DEV + s] = left[:, columns].T.astype(BF16)
            feat_ref[k * FB_DEV + s] = feat[:, columns]


def own_features(own_ref, own_blocks, right_ref):
    row = lax.broadcasted_iota(jnp.int32, (8, BLOCK), 0)
    zero = jnp.zeros((8, BLOCK), F32)
    first, second = row < 3, jnp.logical_and(row >= 3, row < 6)
    for a, o in enumerate(own_blocks):
        x = own_ref[:, o * BLOCK : (o + 1) * BLOCK]
        center = thirds(-2.0 * x)
        swapped = thirds(jnp.concatenate([x[3:6], x[0:3], x[6:8]], axis=0))
        distance, level = thirds(square(x) + 1.0), thirds(lever(x))
        sides = (
            [jnp.where(first, center[i], zero) for i in RIGHT],
            [jnp.where(first, -swapped[i], zero) for i in RIGHT],
            [jnp.where(second, swapped[i], zero) for i in RIGHT],
        )
        for i, g in enumerate(ONES):
            sides[0][g] = jnp.where(row == 7, distance[i], sides[0][g])
            sides[1][g] = jnp.where(row == 7, level[i], sides[1][g])
        tails = (jnp.where(first, 1.0, zero), zero, jnp.where(second, -1.0, zero))
        for m in range(3):
            right_ref[a, m] = jnp.concatenate(sides[m] + [tails[m], zero], axis=0).astype(BF16)


def list_cells(own_blocks, group, place_ref, count_ref, list_ref):
    slots = group * CODES
    lane = place_ref[0, 0]

    def step(i, found):
        role, j = i // slots, i % slots
        k, code = j // CODES, j % CODES
        line = jnp.where(role == 0, k, group)
        member = jnp.where(role == 0, lane, (lane + k) % group)
        count = count_ref[line, member * CODES + code].astype(jnp.int32)
        first, second = code // FB_DEV, code % FB_DEV
        mine, other = jnp.where(role == 0, first, second), jnp.where(role == 0, second, first)
        at, held = jnp.int32(0), jnp.bool_(False)
        for a, o in enumerate(own_blocks):
            at, held = jnp.where(mine == o, a, at), jnp.logical_or(held, mine == o)
        list_ref[found] = count * 65536 + role * 4096 + at * 256 + k * FB_DEV + other
        return found + jnp.logical_and(count > 0, held).astype(jnp.int32)

    found = lax.fori_loop(0, 2 * slots, step, jnp.int32(0), unroll=4)
    for u in range(CELLS):
        list_ref[found + u] = 0
    return found


def weighted(feat, values):
    high = values.astype(BF16)
    return dot(feat, high) + dot(feat, (values - high.astype(F32)).astype(BF16))


def cell(entry, left_ref, feat_ref, right_ref):
    count, role, at, x = entry // 65536, (entry // 4096) % 16, (entry // 256) % 16, entry % 256
    left, feat = left_ref[x], feat_ref[x]
    inverse = pl.reciprocal(dot(left, right_ref[at, 0]), approx=True)
    projected = dot(left, right_ref[at, 1 + role])
    scaled = inverse * inverse
    kernel = (projected * projected + 1.0) * scaled
    sums = [weighted(feat, v) for v in (kernel, kernel * inverse, projected * scaled)]
    return at, role, [count.astype(F32) * s for s in sums]


def pair_body(own_blocks, group, place_ref, count_ref, scale_ref, own_ref, left_ref, feat_ref, out_ref, right_ref, acc_ref, list_ref):
    found = list_cells(own_blocks, group, place_ref, count_ref, list_ref)
    own_features(own_ref, own_blocks, right_ref)
    acc_ref[...] = jnp.zeros_like(acc_ref)

    def visit(i, carry):
        results = [cell(list_ref[i * CELLS + u], left_ref, feat_ref, right_ref) for u in range(CELLS)]
        for at, role, sums in results:
            acc_ref[at, 0] += sums[0]
            acc_ref[at, 1] += sums[1]
            acc_ref[at, 2 + role] += sums[2]
        return carry

    lax.fori_loop(0, (found + CELLS - 1) // CELLS, visit, 0)

    scale = scale_ref[0, 0]
    for a, o in enumerate(own_blocks):
        kernel, pushing, target, source = (acc_ref[a, m, 0:8] + acc_ref[a, m, 8:16] + acc_ref[a, m, 16:24] for m in range(4))
        x = own_ref[:, o * BLOCK : (o + 1) * BLOCK]
        center, normal = x[0:3], x[3:6]
        weight = scale * x[6:7]
        push = center * pushing[6:7] - pushing[0:3]
        pull = normal * target[6:7] + source[3:6]
        columns = slice(a * BLOCK, (a + 1) * BLOCK)
        out_ref[0:3, columns] = weight * (2.0 * pull - 4.0 * push)
        out_ref[3:6, columns] = 2.0 * weight * (center * target[6:7] - target[0:3])
        out_ref[6:7, columns] = scale * kernel[6:7]
        out_ref[7:8, columns] = jnp.zeros((1, BLOCK), F32)


def outer_kernel(own_blocks, group, place_ref, count_ref, scale_ref, own_ref, *refs):
    partners, (out_ref, left_ref, feat_ref, *scratch) = refs[:group], refs[group:]
    partner_features(partners, left_ref, feat_ref)
    pair_body(own_blocks, group, place_ref, count_ref, scale_ref, own_ref, left_ref, feat_ref, out_ref, *scratch)


def pair_call(body, own_blocks, group, outputs, operands, name):
    n = len(own_blocks)
    cells = 2 * group * CODES * n // FB_DEV // 3
    in_specs = [SMEM] * 3 + [VMEM] * (len(operands) - 3)
    return pl.pallas_call(
        functools.partial(body, own_blocks, group),
        out_shape=outputs,
        in_specs=in_specs,
        out_specs=jax.tree.map(lambda _: VMEM, outputs),
        scratch_shapes=[
            pltpu.VMEM((n, 3, DEPTH, BLOCK), BF16),
            pltpu.VMEM((n, 4, 32, BLOCK), F32),
            pltpu.SMEM((2 * group * CODES + 8,), jnp.int32),
        ],
        compiler_params=pltpu.CompilerParams(vmem_limit_bytes=24 * 1024 * 1024),
        cost_estimate=pl.CostEstimate(
            flops=cells * BLOCK * BLOCK * 500, bytes_accessed=1 << 21, transcendentals=cells * BLOCK * BLOCK
        ),
        name=name,
    )(*operands)


def incidence_kernel(corner_ref, out_ref):
    verts, faces = out_ref.shape
    vertex = lax.broadcasted_iota(jnp.int32, (verts, 128), 0)
    for e in range(0, faces, 128):
        total = jnp.zeros((verts, 128), F32)
        for k in range(3):
            total = total + jnp.where(corner_ref[k : k + 1, e : e + 128] == vertex, 1.0, 0.0)
        out_ref[:, e : e + 128] = total.astype(BF16)


def incidence_table(corner, verts):
    faces = corner.shape[1]
    return pl.pallas_call(
        incidence_kernel,
        out_shape=jax.ShapeDtypeStruct((verts, faces), BF16),
        in_specs=[VMEM],
        out_specs=VMEM,
        compiler_params=pltpu.CompilerParams(vmem_limit_bytes=16 * 1024 * 1024),
        cost_estimate=pl.CostEstimate(flops=verts * faces * 9, bytes_accessed=verts * faces * 2, transcendentals=0),
        name="incidence",
    )(corner)


def finish_kernel(parts_ref, table_ref, vertex_ref, face_ref):
    total = parts_ref[0]
    for i in range(1, parts_ref.shape[0]):
        total = total + parts_ref[i]
    faces = total.shape[1]
    width = 2 * HALO_FACES
    face_ref[...] = total[3:7]
    edge = jnp.concatenate([total[7:8, c * width : (c + 1) * width] for c in range(3)], axis=0)
    contract = (((1,), (1,)), ((), ()))
    out = jnp.zeros((3, vertex_ref.shape[1]), F32)
    for main, side in zip(thirds(total[0:3]), thirds(edge)):
        out = out + lax.dot_general(main.astype(BF16), table_ref[:, 0:faces], contract, preferred_element_type=F32)
        out = out + lax.dot_general(side.astype(BF16), table_ref[:, faces:], contract, preferred_element_type=F32)
    vertex_ref[...] = out / 3.0


def finish(parts, table):
    verts, faces = table.shape[0], parts.shape[2]
    return pl.pallas_call(
        finish_kernel,
        out_shape=(jax.ShapeDtypeStruct((3, verts), F32), jax.ShapeDtypeStruct((4, faces), F32)),
        in_specs=[VMEM, VMEM],
        out_specs=(VMEM, VMEM),
        compiler_params=pltpu.CompilerParams(vmem_limit_bytes=16 * 1024 * 1024),
        name="finish",
    )(parts, table)


def shards(centroids, normals, areas, cotangent, pair_code, corner_vertex):
    count, shares = lax.axis_size("blk"), lax.axis_size("pair")
    group = count // shares
    both = ("blk", "pair")
    faces = centroids.shape[1]

    def route(k):
        pairs = []
        for b in range(count):
            for p in range(shares):
                q = group * p + (b + k) % group
                pairs.append((q * shares + b // group, b * shares + p))
        return pairs

    held = lax.all_to_all(pair_code.reshape(shares, group), "pair", 0, 0, tiled=True)
    tally = jnp.sum((held[:, :, None] == jnp.arange(CODES, dtype=jnp.int32)).astype(F32), axis=0).reshape(1, group * CODES)
    tally_row = jnp.pad(tally, ((0, 0), (0, faces - group * CODES)))
    own = jnp.concatenate([centroids, normals, areas[None], tally_row], axis=0)
    partners = [lax.ppermute(own, both, route(k)) for k in range(group)]
    counts = jnp.concatenate([x[7:8, : group * CODES] for x in partners] + [tally], axis=0)
    place = (lax.axis_index("blk") % group).reshape(1, 1)
    scale = cotangent.reshape(1, 1)
    corner = jnp.concatenate(
        [corner_vertex[:, HALO_FACES:-HALO_FACES], corner_vertex[:, :HALO_FACES], corner_vertex[:, -HALO_FACES:]], axis=1
    )
    table = incidence_table(corner, faces // 2)

    half = jax.ShapeDtypeStruct((8, faces // 2), F32)
    left = jax.ShapeDtypeStruct((group * FB_DEV, BLOCK, DEPTH), BF16)
    feat = jax.ShapeDtypeStruct((group * FB_DEV, 32, BLOCK), BF16)
    outer, left, feat = pair_call(
        outer_kernel, (0, 3), group, (half, left, feat), (place, counts, scale, own, *partners), "outer_blocks"
    )
    head, tail = outer[0:3, :HALO_FACES], outer[0:3, -HALO_FACES:]
    forward = [(i, (i + 1) % count) for i in range(count)]
    before = lax.ppermute(tail, "blk", forward)
    after = lax.ppermute(head, "blk", [(j, i) for i, j in forward])
    inner = pair_call(pair_body, (1, 2), group, half, (place, counts, scale, own, left, feat), "inner_blocks")
    edge = jnp.concatenate([before, after], axis=1).reshape(1, -1)
    edge = jnp.pad(edge, ((0, 0), (0, faces - edge.shape[1])))
    part = jnp.concatenate([outer[:, :BLOCK], inner, outer[:, BLOCK:]], axis=1)
    part = jnp.concatenate([part[:7], edge], axis=0)
    parts = lax.all_gather(part, "pair")
    return finish(parts, table)


def solution(mesh):
    placed = (
        P(None, "blk"),
        P(None, "blk"),
        P("blk"),
        P(),
        P("blk", "pair", None, None),
        P(None, "blk"),
    )
    return jax.shard_map(
        shards,
        mesh=mesh,
        in_specs=placed,
        out_specs=(P(None, "blk"), P(None, "blk")),
        check_vma=False,
    )
```

time: 177 us -> 130 us (0.73)
  starting transfers between devices: 71.8 us -> 31.2 us
  blocking collectives: 37.4 us -> 56.6 us
  Pallas kernels: 47.9 us -> 31.1 us
  waiting for transfers between devices: 10 us -> 2.27 us
  local copies, waits for them, and re-layouts: 4.42 us -> 2.54 us
    all_to_all x1 -> x0, starting transfers between devices: 28.5 us -> none  [shards(): lax.all_to_all(pair_code.reshape(shares, group), 'pair', 0, 0, tiled=True)]
    all_to_all x0 -> x1, blocking collectives: none -> 23.6 us  [shards(): lax.all_to_all(pair_code.reshape(shares, group), 'pair', 0, 0, tiled=True)]
    pallas_call x3 -> x2, Pallas kernels: 45.5 us -> 28.7 us  [pair_call(): pl.pallas_call(functools.partial(body, own_blocks, group), out_shape=outp...]
    ppermute x4, starting transfers between devices: 18.8 us -> 12.4 us  [shards(): partners = [lax.ppermute(own, both, route(k)) for k in range(group)]]
    ppermute x6 -> x2, starting transfers between devices: 24.6 us -> 18.7 us  [the longest x1 12.3 us: shards(): after = lax.ppermute(head, 'blk', [(j, i) for i, j in forward])]
    all_gather x1, blocking collectives: 37.4 us -> 33 us  [shards(): parts = lax.all_gather(part, 'pair')]
    all_to_all x1 -> x0, waiting for transfers between devices: 3.84 us -> none  [shards(): lax.all_to_all(pair_code.reshape(shares, group), 'pair', 0, 0, tiled=True)]
    ppermute x4, waiting for transfers between devices: 4.92 us -> 2.26 us  [shards(): partners = [lax.ppermute(own, both, route(k)) for k in range(group)]]
  transfers between devices with their start and end apart: 11 -> 6, of which waited for: 4 -> 1; matrix products, arithmetic and copies ran while one was open for 3% -> 1% of each run, Pallas kernels for 7% -> 12%
where the time goes in v2:
time: 130 us; the launch traced here: 127 us
  blocking collectives  56.6 us (44%)
  starting transfers between devices  31.2 us (24%)
  Pallas kernels  31.1 us (24%)
  local copies, waits for them, and re-layouts  2.54 us (2%)
  other arithmetic  2.27 us (2%)
  waiting for transfers between devices  2.27 us (2%)
  between operations  1.43 us (1%)
    all_gather x1, blocking collectives, shards(): parts = lax.all_gather(part, 'pair')  33 us
    pallas_call x2, Pallas kernels, pair_call(): pl.pallas_call(functools.partial(body, own_blocks, group), out_shape=outp...  28.7 us
    all_to_all x1, blocking collectives, shards(): lax.all_to_all(pair_code.reshape(shares, group), 'pair', 0, 0, tiled=True)  23.6 us
    ppermute x4, starting transfers between devices, shards(): partners = [lax.ppermute(own, both, route(k)) for k in range(group)]  12.4 us
    ppermute x1, starting transfers between devices, shards(): after = lax.ppermute(head, 'blk', [(j, i) for i, j in forward])  12.3 us
    ppermute x1, starting transfers between devices, shards(): before = lax.ppermute(tail, 'blk', forward)  6.44 us
  transfers between devices with their start and end apart: 6, of which 1 were waited for; matrix products, arithmetic and copies ran while one was open for 1% of the time, Pallas kernels for 12%

profile of v2, /device:TPU:1, one launch (start us, length us, event | category | flops | bytes accessed | tf_op | source)
XLA Modules:
  0.0 127.4 jit_solution(12564999113587748715)
XLA Ops:
  0.6 0.5 broadcast.22
  1.1 1.3 %reduce.3 = s32[64]{0:T(128)S(1)} reduce(s32[1,1,64,1]{2,3,1,0:T(1,128)} %param.10, s32[]{:T(128)} %broadcast.22), dimensions={0,1,3}, to_apply=%param.10.reduce_sub_computation.3 | reduce | bytes 516 | tf_op args[4]
  2.5 0.1 all_to_all.6
  2.5 23.6 %all_to_all.9 = s32[16,1,4]{2,1,0:T(1,128)S(1)} all-to-all(s32[16,1,4]{2,1,0:T(1,128)S(1)} %bitcast.16), channel_id=1, replica_groups=mesh['blk'=64,'pair'=16] {'pair'}, dimensions={0} | all-to-all | bytes 512 | tf_op jit(solution)/shard_map/all_to_all | solution.py:243
  26.1 0.1 copy.16
  26.2 0.1 convert_reduce_fusion
  26.3 0.1 reshape.23
  26.4 0.8 select_maximum_fusion.3.own_ref
  27.2 1.9 %collective-permute-start = (f32[8,1024]{1,0:T(8,128)S(1)}, f32[8,1024]{1,0:T(8,128)S(1)}, u32[]{:S(2)}, u32[]{:S(2)}) collective-permute-start(f32[8,1024]{1,0:T(8,128)S(1)} %select_maximum_fusion.3.own_ref), channel_id=1, source_target_pairs={{0,0},{64,1},{128,2},{192,3},{256,4},{320,5},{384,6},{448,7},{512,... | collective-permute-start | bytes 98312 | tf_op jit(solution)/shard_map/ppermute | solution.py:247
  29.1 1.9 %collective-permute-start.1 = (f32[8,1024]{1,0:T(8,128)S(1)}, f32[8,1024]{1,0:T(8,128)S(1)}, u32[]{:S(2)}, u32[]{:S(2)}) collective-permute-start(f32[8,1024]{1,0:T(8,128)S(1)} %select_maximum_fusion.3.own_ref), channel_id=1, source_target_pairs={{16,0},{80,1},{144,2},{208,3},{272,4},{336,5},{400,6},{464,7},{528... | collective-permute-start | bytes 98312 | tf_op jit(solution)/shard_map/ppermute | solution.py:247
  31.0 3.8 %collective-permute-start.2 = (f32[8,1024]{1,0:T(8,128)S(1)}, f32[8,1024]{1,0:T(8,128)S(1)}, u32[]{:S(2)}, u32[]{:S(2)}) collective-permute-start(f32[8,1024]{1,0:T(8,128)S(1)} %select_maximum_fusion.3.own_ref), channel_id=1, source_target_pairs={{32,0},{96,1},{160,2},{224,3},{288,4},{352,5},{416,6},{480,7},{544... | collective-permute-start | bytes 98312 | tf_op jit(solution)/shard_map/ppermute | solution.py:247
  34.8 4.8 %collective-permute-start.3 = (f32[8,1024]{1,0:T(8,128)S(1)}, f32[8,1024]{1,0:T(8,128)S(1)}, u32[]{:S(2)}, u32[]{:S(2)}) collective-permute-start(f32[8,1024]{1,0:T(8,128)S(1)} %select_maximum_fusion.3.own_ref), channel_id=1, source_target_pairs={{48,0},{112,1},{176,2},{240,3},{304,4},{368,5},{432,6},{496,7},{56... | collective-permute-start | bytes 98312 | tf_op jit(solution)/shard_map/ppermute | solution.py:247
  39.6 0.8 fusion
  40.4 0.8 slice.45
  41.9 0.1 concatenate.23.corner_ref
  42.0 0.8 incidence.1.table_ref
  42.8 2.3 %collective-permute-done.3.refs_3_ = f32[8,1024]{1,0:T(8,128)S(1)} collective-permute-done((f32[8,1024]{1,0:T(8,128)S(1)}, f32[8,1024]{1,0:T(8,128)S(1)}, u32[]{:S(2)}, u32[]{:S(2)}) %collective-permute-start.3) | collective-permute-done | bytes 32800 | tf_op jit(solution)/shard_map/ppermute | solution.py:247
  45.1 13.7 %outer_blocks.1 = (f32[8,512]{1,0:T(8,128)S(1)}, bf16[16,256,64]{2,1,0:T(8,128)(2,1)S(1)}, bf16[16,32,256]{2,1,0:T(8,128)(2,1)S(1)}) custom-call(s32[1,1]{1,0:T(1,128)} %bitcast.place_ref, f32[5,64]{1,0:T(8,128)S(1)} %concatenate.19.count_ref, f32[1,1]{1,0:T(1,128)} %bitcast.13.scale_ref, f32[8,1024]{1,0:T(8,128)S(1)} %select_maximum_fusion.3.own_ref, ...), custom_call_target="tpu_custom_call" | custom-call | flops 688128000 | bytes 2097152 | tf_op jit(solution)/shard_map/outer_blocks/pallas_call | solution.py:160
  58.9 6.4 %collective-permute-start.4 = (f32[3,64]{1,0:T(4,128)S(1)}, f32[3,64]{1,0:T(4,128)S(1)}, u32[]{:S(2)}, u32[]{:S(2)}) collective-permute-start(f32[3,64]{1,0:T(4,128)S(1)} %get-tuple-element.12), channel_id=1, source_target_pairs={{0,16},{16,32},{32,48},{48,64},{64,80},{80,96},{96,112},{112,128},... | collective-permute-start | bytes 2312 | tf_op jit(solution)/shard_map/ppermute | solution.py:264
  65.3 12.3 %collective-permute-start.5 = (f32[3,64]{1,0:T(4,128)S(1)}, f32[3,64]{1,0:T(4,128)S(1)}, u32[]{:S(2)}, u32[]{:S(2)}) collective-permute-start(f32[3,64]{1,0:T(4,128)S(1)} %get-tuple-element.13), channel_id=1, source_target_pairs={{16,0},{32,16},{48,32},{64,48},{80,64},{96,80},{112,96},{128,112},... | collective-permute-start | bytes 2312 | tf_op jit(solution)/shard_map/ppermute | solution.py:265
  77.6 15.0 %inner_blocks.1 = f32[8,512]{1,0:T(8,128)S(1)} custom-call(s32[1,1]{1,0:T(1,128)} %bitcast.place_ref, f32[5,64]{1,0:T(8,128)S(1)} %concatenate.19.count_ref, f32[1,1]{1,0:T(1,128)} %bitcast.14.scale_ref, f32[8,1024]{1,0:T(8,128)S(1)} %select_maximum_fusion.3.own_ref, bf16[16,256,64]{2,1,0:T(8,128)(2,1)S(1)} %get-tuple-element.6.left_ref, ...), custom_call_target="tpu_custom_call" | custom-call | flops 688128000 | bytes 2097152 | tf_op jit(solution)/shard_map/inner_blocks/pallas_call | solution.py:160
  92.7 0.1 maximum_bitcast_fusion
  92.8 33.0 %all-gather = f32[128,1024]{1,0:T(8,128)S(1)} all-gather(f32[8,1024]{1,0:T(8,128)S(1)} %select_maximum_fusion), channel_id=2, replica_groups=mesh['blk'=64,'pair'=16] {'pair'}, dimensions={0}, use_global_device_ids=true | all-gather | bytes 557056 | tf_op jit(solution)/shard_map/all_gather | solution.py:271
  125.8 1.6 %finish.1 = (f32[3,512]{1,0:T(4,128)}, f32[4,1024]{1,0:T(4,128)}) custom-call(f32[16,8,1024]{2,1,0:T(8,128)S(1)} %bitcast.15, bf16[512,1152]{1,0:T(8,128)(2,1)S(1)} %incidence.1.table_ref), custom_call_target="tpu_custom_call" | custom-call | tf_op jit(solution)/shard_map/finish/pallas_call | solution.py:219
  (14 shorter events, 0.1 us)
Async XLA Ops:
  27.2 15.5 %collective-permute-start = (f32[8,1024]{1,0:T(8,128)S(1)}, f32[8,1024]{1,0:T(8,128)S(1)}, u32[]{:S(2)}, u32[]{:S(2)}) collective-permute-start(f32[8,1024]{1,0:T(8,128)S(1)} %select_maximum_fusion.3.own_ref), channel_id=1, source_target_pairs={{0,0},{64,1},{128,2},{192,3},{256,4},{320,5},{384,6},{448,7},{512,... | collective-permute-start | bytes 98312 | tf_op jit(solution)/shard_map/ppermute | solution.py:247
  29.1 13.6 %collective-permute-start.1 = (f32[8,1024]{1,0:T(8,128)S(1)}, f32[8,1024]{1,0:T(8,128)S(1)}, u32[]{:S(2)}, u32[]{:S(2)}) collective-permute-start(f32[8,1024]{1,0:T(8,128)S(1)} %select_maximum_fusion.3.own_ref), channel_id=1, source_target_pairs={{16,0},{80,1},{144,2},{208,3},{272,4},{336,5},{400,6},{464,7},{528... | collective-permute-start | bytes 98312 | tf_op jit(solution)/shard_map/ppermute | solution.py:247
  31.0 11.7 %collective-permute-start.2 = (f32[8,1024]{1,0:T(8,128)S(1)}, f32[8,1024]{1,0:T(8,128)S(1)}, u32[]{:S(2)}, u32[]{:S(2)}) collective-permute-start(f32[8,1024]{1,0:T(8,128)S(1)} %select_maximum_fusion.3.own_ref), channel_id=1, source_target_pairs={{32,0},{96,1},{160,2},{224,3},{288,4},{352,5},{416,6},{480,7},{544... | collective-permute-start | bytes 98312 | tf_op jit(solution)/shard_map/ppermute | solution.py:247
  34.8 10.2 %collective-permute-start.3 = (f32[8,1024]{1,0:T(8,128)S(1)}, f32[8,1024]{1,0:T(8,128)S(1)}, u32[]{:S(2)}, u32[]{:S(2)}) collective-permute-start(f32[8,1024]{1,0:T(8,128)S(1)} %select_maximum_fusion.3.own_ref), channel_id=1, source_target_pairs={{48,0},{112,1},{176,2},{240,3},{304,4},{368,5},{432,6},{496,7},{56... | collective-permute-start | bytes 98312 | tf_op jit(solution)/shard_map/ppermute | solution.py:247
  58.9 33.8 %collective-permute-start.4 = (f32[3,64]{1,0:T(4,128)S(1)}, f32[3,64]{1,0:T(4,128)S(1)}, u32[]{:S(2)}, u32[]{:S(2)}) collective-permute-start(f32[3,64]{1,0:T(4,128)S(1)} %get-tuple-element.12), channel_id=1, source_target_pairs={{0,16},{16,32},{32,48},{48,64},{64,80},{80,96},{96,112},{112,128},... | collective-permute-start | bytes 2312 | tf_op jit(solution)/shard_map/ppermute | solution.py:264
  65.3 27.4 %collective-permute-start.5 = (f32[3,64]{1,0:T(4,128)S(1)}, f32[3,64]{1,0:T(4,128)S(1)}, u32[]{:S(2)}, u32[]{:S(2)}) collective-permute-start(f32[3,64]{1,0:T(4,128)S(1)} %get-tuple-element.13), channel_id=1, source_target_pairs={{16,0},{32,16},{48,32},{64,48},{80,64},{96,80},{112,96},{128,112},... | collective-permute-start | bytes 2312 | tf_op jit(solution)/shard_map/ppermute | solution.py:265

commit v3 on v2

--- a/solution.py
+++ b/solution.py
@@ -12,7 +12,6 @@
 HALO_FACES = 64
 CODES = FB_DEV * FB_DEV
 DEPTH = 64
-CELLS = 2
 LEFT = (0, 0, 1, 1, 0, 2)
 RIGHT = (0, 1, 0, 1, 2, 0)
 ONES = (0, 1, 4)
@@ -38,11 +37,11 @@
     return jnp.sum(x[0:3] * x[3:6], axis=0, keepdims=True)
 
 
-def partner_features(partners, left_ref, feat_ref):
+def partner_features(group, first, rows_ref, left_ref, feat_ref):
     width = FB_DEV * BLOCK
     row = lax.broadcasted_iota(jnp.int32, (8, width), 0)
-    for k, partner in enumerate(partners):
-        x = partner[...]
+    for k in range(group):
+        x = rows_ref[first + k]
         area = x[6:7]
         x = jnp.where(row >= 6, 1.0, x)
         split = thirds(x)
@@ -78,59 +77,77 @@
 
 
 def list_cells(own_blocks, group, place_ref, count_ref, list_ref):
-    slots = group * CODES
-    lane = place_ref[0, 0]
-
-    def step(i, found):
-        role, j = i // slots, i % slots
-        k, code = j // CODES, j % CODES
-        line = jnp.where(role == 0, k, group)
-        member = jnp.where(role == 0, lane, (lane + k) % group)
-        count = count_ref[line, member * CODES + code].astype(jnp.int32)
-        first, second = code // FB_DEV, code % FB_DEV
-        mine, other = jnp.where(role == 0, first, second), jnp.where(role == 0, second, first)
-        at, held = jnp.int32(0), jnp.bool_(False)
-        for a, o in enumerate(own_blocks):
-            at, held = jnp.where(mine == o, a, at), jnp.logical_or(held, mine == o)
-        list_ref[found] = count * 65536 + role * 4096 + at * 256 + k * FB_DEV + other
-        return found + jnp.logical_and(count > 0, held).astype(jnp.int32)
-
-    found = lax.fori_loop(0, 2 * slots, step, jnp.int32(0), unroll=4)
-    for u in range(CELLS):
-        list_ref[found + u] = 0
+    n = len(own_blocks)
+    lane, core = place_ref[0, 0], place_ref[0, 1]
+    last = count_ref.shape[0] - 1
+    list_ref[0] = 0
+
+    def step(j, found):
+        k, a, other = j // (n * FB_DEV), (j // FB_DEV) % n, j % FB_DEV
+        mine = sum(jnp.where(a == i, o, 0) for i, o in enumerate(own_blocks))
+        partner = core * group + k
+        place = a * 256 + k * FB_DEV + other
+        target = count_ref[partner, lane * CODES + mine * FB_DEV + other].astype(jnp.int32)
+        list_ref[found + 1] = target * 65536 + place
+        found = found + (target > 0).astype(jnp.int32)
+        source = count_ref[last, partner * CODES + other * FB_DEV + mine].astype(jnp.int32)
+        list_ref[found + 1] = source * 65536 + 4096 + place
+        return found + (source > 0).astype(jnp.int32)
+
+    found = lax.fori_loop(0, group * n * FB_DEV, step, jnp.int32(0), unroll=4)
+    for u in range(3):
+        list_ref[found + 1 + u] = 0
     return found
 
 
-def weighted(feat, values):
-    high = values.astype(BF16)
-    return dot(feat, high) + dot(feat, (values - high.astype(F32)).astype(BF16))
-
-
-def cell(entry, left_ref, feat_ref, right_ref):
-    count, role, at, x = entry // 65536, (entry // 4096) % 16, (entry // 256) % 16, entry % 256
-    left, feat = left_ref[x], feat_ref[x]
-    inverse = pl.reciprocal(dot(left, right_ref[at, 0]), approx=True)
-    projected = dot(left, right_ref[at, 1 + role])
+def unpack(entry):
+    return entry // 65536, (entry // 4096) % 16, (entry // 256) % 16, entry % 256
+
+
+def products(entry, left_ref, right_ref, out_ref):
+    _, role, at, x = unpack(entry)
+    left = left_ref[x]
+    out_ref[0] = dot(left, right_ref[at, 0])
+    out_ref[1] = dot(left, right_ref[at, 1 + role])
+
+
+def weights(in_ref, out_ref):
+    inverse = pl.reciprocal(in_ref[0], approx=True)
+    projected = in_ref[1]
     scaled = inverse * inverse
     kernel = (projected * projected + 1.0) * scaled
-    sums = [weighted(feat, v) for v in (kernel, kernel * inverse, projected * scaled)]
-    return at, role, [count.astype(F32) * s for s in sums]
-
-
-def pair_body(own_blocks, group, place_ref, count_ref, scale_ref, own_ref, left_ref, feat_ref, out_ref, right_ref, acc_ref, list_ref):
+    for m, values in enumerate((kernel, kernel * inverse, projected * scaled)):
+        high = values.astype(BF16)
+        out_ref[m, 0] = high
+        out_ref[m, 1] = (values - high.astype(F32)).astype(BF16)
+
+
+def reduce_cell(entry, feat_ref, in_ref, acc_ref):
+    count, role, at, x = unpack(entry)
+    feat = feat_ref[x]
+    for m, place in enumerate((0, 1, 2 + role)):
+        acc_ref[at, place] += count.astype(F32) * (dot(feat, in_ref[m, 0]) + dot(feat, in_ref[m, 1]))
+
+
+def pair_body(own_blocks, group, place_ref, count_ref, scale_ref, own_ref, left_ref, feat_ref, out_ref, right_ref, acc_ref, list_ref, *stages):
+    product_refs, weight_refs = stages[:2], stages[2:]
     found = list_cells(own_blocks, group, place_ref, count_ref, list_ref)
     own_features(own_ref, own_blocks, right_ref)
     acc_ref[...] = jnp.zeros_like(acc_ref)
+    weight_refs[1][...] = jnp.zeros_like(weight_refs[1])
+    products(list_ref[1], left_ref, right_ref, product_refs[0])
 
     def visit(i, carry):
-        results = [cell(list_ref[i * CELLS + u], left_ref, feat_ref, right_ref) for u in range(CELLS)]
-        for at, role, sums in results:
-            acc_ref[at, 0] += sums[0]
-            acc_ref[at, 1] += sums[1]
-            acc_ref[at, 2 + role] += sums[2]
+        for u in range(2):
+            now, later = u, 1 - u
+            reduce_cell(list_ref[2 * i + u], feat_ref, weight_refs[later], acc_ref)
+            weights(product_refs[now], weight_refs[now])
+            products(list_ref[2 * i + u + 2], left_ref, right_ref, product_refs[later])
         return carry
 
-    lax.fori_loop(0, (found + CELLS - 1) // CELLS, visit, 0)
+    rounds = (found + 1) // 2
+    lax.fori_loop(0, rounds, visit, 0)
+    reduce_cell(list_ref[2 * rounds], feat_ref, weight_refs[1], acc_ref)
 
     scale = scale_ref[0, 0]
     for a, o in enumerate(own_blocks):
@@ -147,9 +164,8 @@
         out_ref[7:8, columns] = jnp.zeros((1, BLOCK), F32)
 
 
-def outer_kernel(own_blocks, group, place_ref, count_ref, scale_ref, own_ref, *refs):
-    partners, (out_ref, left_ref, feat_ref, *scratch) = refs[:group], refs[group:]
-    partner_features(partners, left_ref, feat_ref)
+def outer_kernel(own_blocks, group, place_ref, count_ref, scale_ref, own_ref, rows_ref, out_ref, left_ref, feat_ref, *scratch):
+    partner_features(group, place_ref[0, 1] * group, rows_ref, left_ref, feat_ref)
     pair_body(own_blocks, group, place_ref, count_ref, scale_ref, own_ref, left_ref, feat_ref, out_ref, *scratch)
 
 
@@ -166,7 +182,9 @@
             pltpu.VMEM((n, 3, DEPTH, BLOCK), BF16),
             pltpu.VMEM((n, 4, 32, BLOCK), F32),
             pltpu.SMEM((2 * group * CODES + 8,), jnp.int32),
-        ],
+        ]
+        + [pltpu.VMEM((2, BLOCK, BLOCK), F32)] * 2
+        + [pltpu.VMEM((3, 2, BLOCK, BLOCK), BF16)] * 2,
         compiler_params=pltpu.CompilerParams(vmem_limit_bytes=24 * 1024 * 1024),
         cost_estimate=pl.CostEstimate(
             flops=cells * BLOCK * BLOCK * 500, bytes_accessed=1 << 21, transcendentals=cells * BLOCK * BLOCK
@@ -228,25 +246,31 @@
 
 def shards(centroids, normals, areas, cotangent, pair_code, corner_vertex):
     count, shares = lax.axis_size("blk"), lax.axis_size("pair")
-    group = count // shares
+    side = shares // 2
+    group = side // 2
     both = ("blk", "pair")
     faces = centroids.shape[1]
-
-    def route(k):
-        pairs = []
-        for b in range(count):
-            for p in range(shares):
-                q = group * p + (b + k) % group
-                pairs.append((q * shares + b // group, b * shares + p))
-        return pairs
-
-    held = lax.all_to_all(pair_code.reshape(shares, group), "pair", 0, 0, tiled=True)
-    tally = jnp.sum((held[:, :, None] == jnp.arange(CODES, dtype=jnp.int32)).astype(F32), axis=0).reshape(1, group * CODES)
-    tally_row = jnp.pad(tally, ((0, 0), (0, faces - group * CODES)))
+    assert count == side * side
+    z, x = lax.axis_index("blk") // side, lax.axis_index("blk") % side
+    core = lax.axis_index("pair") % 2
+
+    def at(z, x, y, c):
+        return (z * side + x) * shares + y * 2 + c
+
+    every = range(side)
+    swap = [(at(y, x, z, c), at(z, x, y, c)) for z in every for x in every for y in every for c in range(2)]
+    along = [[z * side + x for x in every] for z in every]
+
+    code = jnp.repeat(pair_code.reshape(side, 1, side), 2, axis=1).reshape(shares, side)
+    held = lax.all_to_all(code, "pair", 0, 0, tiled=True)
+    tally = jnp.sum((held[:, :, None] == jnp.arange(CODES, dtype=jnp.int32)).astype(F32), axis=0).reshape(1, side * CODES)
+    tally_row = jnp.pad(tally, ((0, 0), (0, faces - side * CODES)))
     own = jnp.concatenate([centroids, normals, areas[None], tally_row], axis=0)
-    partners = [lax.ppermute(own, both, route(k)) for k in range(group)]
-    counts = jnp.concatenate([x[7:8, : group * CODES] for x in partners] + [tally], axis=0)
-    place = (lax.axis_index("blk") % group).reshape(1, 1)
+    swapped = lax.ppermute(own, both, swap)
+    copies = jnp.broadcast_to(swapped[None], (side, 8, faces))
+    rows = lax.all_to_all(copies, "blk", 0, 0, axis_index_groups=along)
+    counts = jnp.concatenate([rows[:, 7, : side * CODES], tally], axis=0)
+    place = jnp.stack([x, core]).reshape(1, 2)
     scale = cotangent.reshape(1, 1)
     corner = jnp.concatenate(
         [corner_vertex[:, HALO_FACES:-HALO_FACES], corner_vertex[:, :HALO_FACES], corner_vertex[:, -HALO_FACES:]], axis=1
@@ -257,7 +281,7 @@
     left = jax.ShapeDtypeStruct((group * FB_DEV, BLOCK, DEPTH), BF16)
     feat = jax.ShapeDtypeStruct((group * FB_DEV, 32, BLOCK), BF16)
     outer, left, feat = pair_call(
-        outer_kernel, (0, 3), group, (half, left, feat), (place, counts, scale, own, *partners), "outer_blocks"
+        outer_kernel, (0, 3), group, (half, left, feat), (place, counts, scale, own, rows), "outer_blocks"
     )
     head, tail = outer[0:3, :HALO_FACES], outer[0:3, -HALO_FACES:]
     forward = [(i, (i + 1) % count) for i in range(count)]

time: 130 us -> 105 us (0.81); the launches traced: 127 us -> 105 us
  Pallas kernels: 31.1 us -> 16.7 us
  blocking collectives: 56.6 us -> 48 us
  starting transfers between devices: 31.2 us -> 25.5 us
  waiting for transfers between devices: 2.27 us -> 7.73 us
    pallas_call x2, Pallas kernels: 28.7 us -> 14.3 us  [pair_call(): pl.pallas_call(functools.partial(body, own_blocks, group), out_shape=outp...]
    ppermute x4 -> x1, starting transfers between devices: 12.4 us -> 0.66 us  [shards(): swapped = lax.ppermute(own, both, swap)]
    all_gather x1, blocking collectives: 33 us -> 24.4 us  [shards(): parts = lax.all_gather(part, 'pair')]
    all_to_all x0 -> x1, waiting for transfers between devices: none -> 7.72 us  [shards(): rows = lax.all_to_all(copies, 'blk', 0, 0, axis_index_groups=along)]
    ppermute x1, starting transfers between devices: 12.3 us -> 19.5 us  [shards(): after = lax.ppermute(head, 'blk', [(j, i) for i, j in forward])]
    ppermute x1, starting transfers between devices: 6.44 us -> 1.91 us  [shards(): before = lax.ppermute(tail, 'blk', forward)]
    all_to_all x0 -> x1, starting transfers between devices: none -> 3.41 us  [shards(): rows = lax.all_to_all(copies, 'blk', 0, 0, axis_index_groups=along)]
    ppermute x4 -> x1, waiting for transfers between devices: 2.26 us -> 0.01 us  [shards(): swapped = lax.ppermute(own, both, swap)]
  transfers between devices with their start and end apart: 6 -> 4, of which waited for: 1 -> 1; matrix products, arithmetic and copies ran while one was open for 1% -> 2% of each run, Pallas kernels for 12% -> 7%
where the time goes in v3:
time: 105 us
  blocking collectives  48 us (46%)
  starting transfers between devices  25.5 us (24%)
  Pallas kernels  16.7 us (16%)
  waiting for transfers between devices  7.73 us (7%)
  local copies, waits for them, and re-layouts  3.14 us (3%)
  other arithmetic  2.35 us (2%)
  between operations  1.39 us (1%)
    all_gather x1, blocking collectives, shards(): parts = lax.all_gather(part, 'pair')  24.4 us
    all_to_all x1, blocking collectives, shards(): held = lax.all_to_all(code, 'pair', 0, 0, tiled=True)  23.6 us
    ppermute x1, starting transfers between devices, shards(): after = lax.ppermute(head, 'blk', [(j, i) for i, j in forward])  19.5 us
    pallas_call x2, Pallas kernels, pair_call(): pl.pallas_call(functools.partial(body, own_blocks, group), out_shape=outp...  14.3 us
    all_to_all x1, waiting for transfers between devices, shards(): rows = lax.all_to_all(copies, 'blk', 0, 0, axis_index_groups=along)  7.72 us
    all_to_all x1, starting transfers between devices, shards(): rows = lax.all_to_all(copies, 'blk', 0, 0, axis_index_groups=along)  3.41 us
  transfers between devices with their start and end apart: 4, of which 1 were waited for; matrix products, arithmetic and copies ran while one was open for 2% of the time, Pallas kernels for 7%

profile of v3, /device:TPU:1, one launch (start us, length us, event | category | flops | bytes accessed | tf_op | source)
XLA Modules:
  0.0 104.7 jit_solution(16802256108399343812)
XLA Ops:
  0.6 0.5 broadcast.25
  1.1 1.3 %reduce.3 = s32[64]{0:T(128)S(1)} reduce(s32[1,1,64,1]{2,3,1,0:T(1,128)} %param.10, s32[]{:T(128)} %broadcast.25), dimensions={0,1,3}, to_apply=%param.10.reduce_sub_computation.3 | reduce | bytes 516 | tf_op args[4]
  2.5 0.1 reshape.28
  2.5 23.6 %all_to_all.14 = s32[16,1,8]{2,1,0:T(1,128)S(1)} all-to-all(s32[16,1,8]{2,1,0:T(1,128)S(1)} %bitcast.24), channel_id=1, replica_groups=mesh['blk'=64,'pair'=16] {'pair'}, dimensions={0} | all-to-all | bytes 1024 | tf_op jit(solution)/shard_map/all_to_all | solution.py:265
  26.1 0.1 convert_reduce_fusion
  26.2 0.1 reshape.29
  26.3 0.8 select_maximum_fusion.3.own_ref
  27.1 0.7 collective-permute-start
  27.8 0.7 broadcast_in_dim.16
  28.5 3.4 %all-to-all-start.1 = ((f32[8,8,1024]{2,1,0:T(8,128)}), f32[8,8,1024]{2,1,0:T(8,128)S(1)}, u32[]{:S(2)}, u32[]{:S(2)}) async-start(f32[8,8,1024]{2,1,0:T(8,128)} %broadcast_in_dim.16), calls=%async_computation.1 | async-start | bytes 524288 | tf_op jit(solution)/shard_map/all_to_all | solution.py:271
  32.6 0.8 slice.33
  33.4 0.8 fusion
  34.1 0.1 concatenate.23.corner_ref
  34.2 0.8 incidence.1.table_ref
  35.0 0.1 add_bitcast_fusion.place_ref
  35.1 7.7 %all-to-all-done.1.rows_ref = f32[8,8,1024]{2,1,0:T(8,128)S(1)} async-done(((f32[8,8,1024]{2,1,0:T(8,128)}), f32[8,8,1024]{2,1,0:T(8,128)S(1)}, u32[]{:S(2)}, u32[]{:S(2)}) %all-to-all-start.1) | async-done | bytes 262176 | tf_op jit(solution)/shard_map/all_to_all | solution.py:271
  42.8 7.6 %outer_blocks.1 = (f32[8,512]{1,0:T(8,128)S(1)}, bf16[16,256,64]{2,1,0:T(8,128)(2,1)S(1)}, bf16[16,32,256]{2,1,0:T(8,128)(2,1)S(1)}) custom-call(s32[1,2]{1,0:T(1,128)S(1)} %add_bitcast_fusion.place_ref, f32[9,128]{1,0:T(8,128)S(1)} %pad_maximum_fusion.count_ref, f32[1,1]{1,0:T(1,128)} %bitcast.21.scale_ref, f32[8,1024]{1,0:T(8,128)S(1)} %select_maximum_fusion.3.own_ref, ...), custom_call_target="tpu_custom_call" | custom-call | flops 688128000 | bytes 2097152 | tf_op jit(solution)/shard_map/outer_blocks/pallas_call | solution.py:176
  50.4 0.1 fusion.2
  50.5 1.9 %collective-permute-start.1 = (f32[3,64]{1,0:T(4,128)S(1)}, f32[3,64]{1,0:T(4,128)S(1)}, u32[]{:S(2)}, u32[]{:S(2)}) collective-permute-start(f32[3,64]{1,0:T(4,128)S(1)} %get-tuple-element.12), channel_id=1, source_target_pairs={{0,16},{16,32},{32,48},{48,64},{64,80},{80,96},{96,112},{112,128},... | collective-permute-start | bytes 2312 | tf_op jit(solution)/shard_map/ppermute | solution.py:288
  52.4 19.5 %collective-permute-start.2 = (f32[3,64]{1,0:T(4,128)S(1)}, f32[3,64]{1,0:T(4,128)S(1)}, u32[]{:S(2)}, u32[]{:S(2)}) collective-permute-start(f32[3,64]{1,0:T(4,128)S(1)} %get-tuple-element.13), channel_id=1, source_target_pairs={{16,0},{32,16},{48,32},{64,48},{80,64},{96,80},{112,96},{128,112},... | collective-permute-start | bytes 2312 | tf_op jit(solution)/shard_map/ppermute | solution.py:289
  71.9 6.7 %inner_blocks.1 = f32[8,512]{1,0:T(8,128)S(1)} custom-call(s32[1,2]{1,0:T(1,128)S(1)} %add_bitcast_fusion.place_ref, f32[9,128]{1,0:T(8,128)S(1)} %pad_maximum_fusion.count_ref, f32[1,1]{1,0:T(1,128)} %bitcast.22.scale_ref, f32[8,1024]{1,0:T(8,128)S(1)} %select_maximum_fusion.3.own_ref, bf16[16,256,64]{2,1,0:T(8,128)(2,1)S(1)} %get-tuple-element.6.left_ref, ...), custom_call_target="tpu_custom_call" | custom-call | flops 688128000 | bytes 2097152 | tf_op jit(solution)/shard_map/inner_blocks/pallas_call | solution.py:176
  78.6 0.1 maximum_bitcast_fusion
  78.7 24.4 %all-gather = f32[128,1024]{1,0:T(8,128)S(1)} all-gather(f32[8,1024]{1,0:T(8,128)S(1)} %select_maximum_fusion), channel_id=2, replica_groups=mesh['blk'=64,'pair'=16] {'pair'}, dimensions={0}, use_global_device_ids=true | all-gather | bytes 557056 | tf_op jit(solution)/shard_map/all_gather | solution.py:295
  103.1 1.6 %finish.1 = (f32[3,512]{1,0:T(4,128)}, f32[4,1024]{1,0:T(4,128)}) custom-call(f32[16,8,1024]{2,1,0:T(8,128)S(1)} %bitcast.23, bf16[512,1152]{1,0:T(8,128)(2,1)S(1)} %incidence.1.table_ref), custom_call_target="tpu_custom_call" | custom-call | tf_op jit(solution)/shard_map/finish/pallas_call | solution.py:237
  (9 shorter events, 0.0 us)
Async XLA Ops:
  27.1 0.7 collective-permute-start
  28.5 14.3 %all-to-all-start.1 = ((f32[8,8,1024]{2,1,0:T(8,128)}), f32[8,8,1024]{2,1,0:T(8,128)S(1)}, u32[]{:S(2)}, u32[]{:S(2)}) async-start(f32[8,8,1024]{2,1,0:T(8,128)} %broadcast_in_dim.16), calls=%async_computation.1 | async-start | bytes 524288 | tf_op jit(solution)/shard_map/all_to_all | solution.py:271
  50.5 28.1 %collective-permute-start.1 = (f32[3,64]{1,0:T(4,128)S(1)}, f32[3,64]{1,0:T(4,128)S(1)}, u32[]{:S(2)}, u32[]{:S(2)}) collective-permute-start(f32[3,64]{1,0:T(4,128)S(1)} %get-tuple-element.12), channel_id=1, source_target_pairs={{0,16},{16,32},{32,48},{48,64},{64,80},{80,96},{96,112},{112,128},... | collective-permute-start | bytes 2312 | tf_op jit(solution)/shard_map/ppermute | solution.py:288
  52.4 26.2 %collective-permute-start.2 = (f32[3,64]{1,0:T(4,128)S(1)}, f32[3,64]{1,0:T(4,128)S(1)}, u32[]{:S(2)}, u32[]{:S(2)}) collective-permute-start(f32[3,64]{1,0:T(4,128)S(1)} %get-tuple-element.13), channel_id=1, source_target_pairs={{16,0},{32,16},{48,32},{64,48},{80,64},{96,80},{112,96},{128,112},... | collective-permute-start | bytes 2312 | tf_op jit(solution)/shard_map/ppermute | solution.py:289

commit v4 on v3

v4 whole, which is shorter than its diff:
```python
import functools

import jax
import jax.numpy as jnp
from jax import lax
from jax.experimental import pallas as pl
from jax.experimental.pallas import tpu as pltpu
from jax.sharding import PartitionSpec as P

BLOCK = 256
FB_DEV = 4
HALO_FACES = 64
CODES = FB_DEV * FB_DEV
DEPTH = 64
LEFT = (0, 0, 1, 1, 0, 2)
RIGHT = (0, 1, 0, 1, 2, 0)
ONES = (0, 1, 4)
F32 = jnp.float32
BF16 = jnp.bfloat16
VMEM = pl.BlockSpec(memory_space=pltpu.VMEM)
SMEM = pl.BlockSpec(memory_space=pltpu.SMEM)
dot = functools.partial(jnp.dot, preferred_element_type=F32)


def thirds(values):
    high = values.astype(BF16).astype(F32)
    rest = values - high
    middle = rest.astype(BF16).astype(F32)
    return [high, middle, (rest - middle).astype(BF16).astype(F32)]


def square(x):
    return jnp.sum(x[0:3] * x[0:3], axis=0, keepdims=True)


def lever(x):
    return jnp.sum(x[0:3] * x[3:6], axis=0, keepdims=True)


def partner_features(rows_ref, left_ref, feat_ref):
    width = FB_DEV * BLOCK
    row = lax.broadcasted_iota(jnp.int32, (8, width), 0)
    for k in range(rows_ref.shape[0]):
        x = rows_ref[k]
        area = x[6:7]
        x = jnp.where(row >= 6, 1.0, x)
        split = thirds(x)
        extra = thirds(square(x)) + thirds(lever(x)) + [jnp.zeros((10, width), F32)]
        left = jnp.concatenate([split[i] for i in LEFT] + extra, axis=0).astype(BF16)
        feat = jnp.concatenate(thirds(x * area) + [jnp.zeros((8, width), F32)], axis=0).astype(BF16)
        for s in range(FB_DEV):
            columns = slice(s * BLOCK, (s + 1) * BLOCK)
            left_ref[k * FB_DEV + s] = left[:, columns]
            feat_ref[k * FB_DEV + s] = feat[:, columns]


def own_features(x, right_ref):
    row = lax.broadcasted_iota(jnp.int32, (8, BLOCK), 0)
    zero = jnp.zeros((8, BLOCK), F32)
    first, second = row < 3, jnp.logical_and(row >= 3, row < 6)
    center = thirds(-2.0 * x)
    swapped = thirds(jnp.concatenate([x[3:6], x[0:3], x[6:8]], axis=0))
    distance, level = thirds(square(x) + 1.0), thirds(lever(x))
    sides = (
        [jnp.where(first, center[i], zero) for i in RIGHT],
        [jnp.where(first, -swapped[i], zero) for i in RIGHT],
        [jnp.where(second, swapped[i], zero) for i in RIGHT],
    )
    for i, g in enumerate(ONES):
        sides[0][g] = jnp.where(row == 7, distance[i], sides[0][g])
        sides[1][g] = jnp.where(row == 7, level[i], sides[1][g])
    tails = (jnp.where(first, 1.0, zero), zero, jnp.where(second, -1.0, zero))
    for m in range(3):
        right_ref[m] = jnp.concatenate(sides[m] + [tails[m], zero], axis=0).astype(BF16)


def list_cells(mine, lane, count_ref, list_ref):
    last = count_ref.shape[0] - 1
    list_ref[0] = 0

    def step(j, found):
        partner, other = j // FB_DEV, j % FB_DEV
        target = count_ref[partner, lane * CODES + mine * FB_DEV + other]
        list_ref[found + 1] = target * 65536 + j
        found = found + (target > 0).astype(jnp.int32)
        source = count_ref[last, partner * CODES + other * FB_DEV + mine]
        list_ref[found + 1] = source * 65536 + 256 + j
        return found + (source > 0).astype(jnp.int32)

    found = lax.fori_loop(0, last * FB_DEV, step, jnp.int32(0), unroll=8)
    for u in range(3):
        list_ref[found + 1 + u] = 0
    return found


def unpack(entry):
    return entry // 65536, (entry // 256) % 256, entry % 256


def products(entry, left_ref, right_ref, out_ref):
    _, role, x = unpack(entry)
    left = left_ref[x]
    over = (((0,), (0,)), ((), ()))
    out_ref[0] = lax.dot_general(left, right_ref[0], over, preferred_element_type=F32)
    out_ref[1] = lax.dot_general(left, right_ref[1 + role], over, preferred_element_type=F32)


def weights(entry, rows_ref, in_ref, out_ref, kernel_ref):
    count, _, x = unpack(entry)
    rows = rows_ref[x // FB_DEV, :, pl.ds(pl.multiple_of((x % FB_DEV) * BLOCK, BLOCK), BLOCK)]
    area = rows.T[:, 6:7]
    inverse = pl.reciprocal(in_ref[0], approx=True)
    projected = in_ref[1]
    scaled = inverse * inverse
    kernel = (projected * projected + 1.0) * scaled
    kernel_ref[...] += count.astype(F32) * jnp.sum((kernel * area).reshape(BLOCK // 8, 8, BLOCK), axis=0)
    for m, values in enumerate((kernel * inverse, projected * scaled)):
        high = values.astype(BF16)
        out_ref[m, 0] = high
        out_ref[m, 1] = (values - high.astype(F32)).astype(BF16)


def reduce_cell(entry, feat_ref, in_ref, acc_ref):
    count, role, x = unpack(entry)
    feat = feat_ref[x]
    for m, place in enumerate((0, 1 + role)):
        acc_ref[place] += count.astype(F32) * (dot(feat, in_ref[m, 0]) + dot(feat, in_ref[m, 1]))


def pair_body(mine, place_ref, count_ref, scale_ref, own_ref, rows_ref, left_ref, feat_ref, out_ref, right_ref, acc_ref, kernel_ref, list_ref, *stages):
    product_refs, weight_refs = stages[:2], stages[2:]
    found = list_cells(mine, place_ref[0, 0], count_ref, list_ref)
    own = own_ref[:, pl.ds(pl.multiple_of(mine * BLOCK, BLOCK), BLOCK)]
    own_features(own, right_ref)
    acc_ref[...] = jnp.zeros_like(acc_ref)
    kernel_ref[...] = jnp.zeros_like(kernel_ref)
    weight_refs[1][...] = jnp.zeros_like(weight_refs[1])
    products(list_ref[1], left_ref, right_ref, product_refs[0])

    def visit(i, carry):
        for u in range(2):
            now, later = u, 1 - u
            reduce_cell(list_ref[2 * i + u], feat_ref, weight_refs[later], acc_ref)
            weights(list_ref[2 * i + u + 1], rows_ref, product_refs[now], weight_refs[now], kernel_ref)
            products(list_ref[2 * i + u + 2], left_ref, right_ref, product_refs[later])
        return carry

    rounds = (found + 1) // 2
    lax.fori_loop(0, rounds, visit, 0)
    reduce_cell(list_ref[2 * rounds], feat_ref, weight_refs[1], acc_ref)

    scale = scale_ref[0, 0]
    pushing, target, source = (acc_ref[m, 0:8] + acc_ref[m, 8:16] + acc_ref[m, 16:24] for m in range(3))
    center, normal = own[0:3], own[3:6]
    weight = scale * own[6:7]
    push = center * pushing[6:7] - pushing[0:3]
    pull = normal * target[6:7] + source[3:6]
    out_ref[0:3, :] = weight * (2.0 * pull - 4.0 * push)
    out_ref[3:6, :] = 2.0 * weight * (center * target[6:7] - target[0:3])
    out_ref[6:7, :] = scale * jnp.sum(kernel_ref[...], axis=0, keepdims=True)
    out_ref[7:8, :] = jnp.zeros((1, BLOCK), F32)


def outer_kernel(place_ref, count_ref, scale_ref, own_ref, rows_ref, out_ref, edge_ref, left_ref, feat_ref, *scratch):
    core = place_ref[0, 1]
    partner_features(rows_ref, left_ref, feat_ref)
    pair_body((1 - core) * (FB_DEV - 1), place_ref, count_ref, scale_ref, own_ref, rows_ref, left_ref, feat_ref, out_ref, *scratch)
    gap = jnp.zeros((1, HALO_FACES), F32)
    tails, heads = [], []
    for c in range(3):
        tails += [out_ref[c : c + 1, BLOCK - HALO_FACES :], gap]
        heads += [gap, out_ref[c : c + 1, :HALO_FACES]]
    rest = [gap] * (2 * BLOCK // HALO_FACES - 6)
    edge_ref[...] = jnp.where(core == 0, jnp.concatenate(tails + rest, axis=1), jnp.concatenate(heads + rest, axis=1))


def inner_kernel(place_ref, *refs):
    pair_body(FB_DEV - 2 - place_ref[0, 1], place_ref, *refs)


def pair_call(body, outputs, operands, name):
    partners = operands[1].shape[0] - 1
    cells = 2 * partners * FB_DEV // 3
    in_specs = [SMEM] * 3 + [VMEM] * (len(operands) - 3)
    return pl.pallas_call(
        body,
        out_shape=outputs,
        in_specs=in_specs,
        out_specs=jax.tree.map(lambda _: VMEM, outputs),
        scratch_shapes=[
            pltpu.VMEM((3, DEPTH, BLOCK), BF16),
            pltpu.VMEM((3, 32, BLOCK), F32),
            pltpu.VMEM((8, BLOCK), F32),
            pltpu.SMEM((2 * partners * FB_DEV + 8,), jnp.int32),
        ]
        + [pltpu.VMEM((2, BLOCK, BLOCK), F32)] * 2
        + [pltpu.VMEM((2, 2, BLOCK, BLOCK), BF16)] * 2,
        compiler_params=pltpu.CompilerParams(vmem_limit_bytes=24 * 1024 * 1024),
        cost_estimate=pl.CostEstimate(
            flops=cells * BLOCK * BLOCK * 500, bytes_accessed=1 << 21, transcendentals=cells * BLOCK * BLOCK
        ),
        name=name,
    )(*operands)


def incidence_kernel(corner_ref, out_ref):
    verts, faces = out_ref.shape
    vertex = lax.broadcasted_iota(jnp.int32, (verts, 128), 0)
    for e in range(0, faces, 128):
        total = jnp.zeros((verts, 128), F32)
        for k in range(3):
            total = total + jnp.where(corner_ref[k : k + 1, e : e + 128] == vertex, 1.0, 0.0)
        out_ref[:, e : e + 128] = total.astype(BF16)


def incidence_table(corner, verts):
    faces = corner.shape[1]
    return pl.pallas_call(
        incidence_kernel,
        out_shape=jax.ShapeDtypeStruct((verts, faces), BF16),
        in_specs=[VMEM],
        out_specs=VMEM,
        compiler_params=pltpu.CompilerParams(vmem_limit_bytes=16 * 1024 * 1024),
        cost_estimate=pl.CostEstimate(flops=verts * faces * 9, bytes_accessed=verts * faces * 2, transcendentals=0),
        name="incidence",
    )(corner)


def finish_kernel(parts_ref, table_ref, vertex_ref, face_ref):
    sums = []
    for core in range(2):
        total = parts_ref[core]
        for i in range(core + 2, parts_ref.shape[0], 2):
            total = total + parts_ref[i]
        sums.append(total)
    low, high = sums[1], sums[0]
    total = jnp.concatenate([low[:, :BLOCK], low[:, BLOCK:], high[:, BLOCK:], high[:, :BLOCK]], axis=1)
    faces = total.shape[1]
    width = 2 * HALO_FACES
    face_ref[...] = total[3:7]
    edges = low[7:8] + high[7:8]
    edge = jnp.concatenate([edges[:, c * width : (c + 1) * width] for c in range(3)], axis=0)
    contract = (((1,), (1,)), ((), ()))
    out = jnp.zeros((3, vertex_ref.shape[1]), F32)
    for main, side in zip(thirds(total[0:3]), thirds(edge)):
        out = out + lax.dot_general(main.astype(BF16), table_ref[:, 0:faces], contract, preferred_element_type=F32)
        out = out + lax.dot_general(side.astype(BF16), table_ref[:, faces:], contract, preferred_element_type=F32)
    vertex_ref[...] = out / 3.0


def finish(parts, table):
    verts, faces = table.shape[0], 2 * parts.shape[2]
    return pl.pallas_call(
        finish_kernel,
        out_shape=(jax.ShapeDtypeStruct((3, verts), F32), jax.ShapeDtypeStruct((4, faces), F32)),
        in_specs=[VMEM, VMEM],
        out_specs=(VMEM, VMEM),
        compiler_params=pltpu.CompilerParams(vmem_limit_bytes=16 * 1024 * 1024),
        name="finish",
    )(parts, table)


def shards(centroids, normals, areas, cotangent, pair_code, corner_vertex):
    count, shares = lax.axis_size("blk"), lax.axis_size("pair")
    side = shares // 2
    both = ("blk", "pair")
    faces = centroids.shape[1]
    assert count == side * side
    z, x = lax.axis_index("blk") // side, lax.axis_index("blk") % side
    core = lax.axis_index("pair") % 2

    def at(z, x, y, c):
        return (z * side + x) * shares + y * 2 + c

    every = range(side)
    swap = [(at(y, x, z, c), at(z, x, y, c)) for z in every for x in every for y in every for c in range(2)]
    along = [[z * side + x for x in every] for z in every]

    code = jnp.repeat(pair_code.reshape(side, 1, side), 2, axis=1).reshape(shares, side)
    held = lax.all_to_all(code, "pair", 0, 0, tiled=True)
    tally = jnp.sum((held[:, :, None] == jnp.arange(CODES, dtype=jnp.int32)).astype(F32), axis=0).reshape(1, side * CODES)
    tally_row = jnp.pad(tally, ((0, 0), (0, faces - side * CODES)))
    own = jnp.concatenate([centroids, normals, areas[None], tally_row], axis=0)
    swapped = lax.ppermute(own, both, swap)
    copies = jnp.broadcast_to(swapped[None], (side, 8, faces))
    rows = lax.all_to_all(copies, "blk", 0, 0, axis_index_groups=along)
    counts = jnp.concatenate([rows[:, 7, : side * CODES], tally], axis=0).astype(jnp.int32)
    place = jnp.stack([x, core]).reshape(1, 2)
    scale = cotangent.reshape(1, 1)
    corner = jnp.concatenate(
        [corner_vertex[:, HALO_FACES:-HALO_FACES], corner_vertex[:, :HALO_FACES], corner_vertex[:, -HALO_FACES:]], axis=1
    )
    table = incidence_table(corner, faces // 2)

    block = jax.ShapeDtypeStruct((8, BLOCK), F32)
    row = jax.ShapeDtypeStruct((1, 2 * BLOCK), F32)
    left = jax.ShapeDtypeStruct((side * FB_DEV, DEPTH, BLOCK), BF16)
    feat = jax.ShapeDtypeStruct((side * FB_DEV, 32, BLOCK), BF16)
    outer, edge, left, feat = pair_call(
        outer_kernel, (block, row, left, feat), (place, counts, scale, own, rows), "outer_block"
    )
    hops = [(at(z, x, y, c), (at(z, x, y, c) + (shares if c == 0 else -shares)) % (count * shares))
            for z in every for x in every for y in every for c in range(2)]
    halo = lax.ppermute(edge, both, hops)
    inner = pair_call(inner_kernel, block, (place, counts, scale, own, rows, left, feat), "inner_block")
    part = jnp.concatenate([jnp.concatenate([outer, inner], axis=1)[:7], halo], axis=0)
    parts = lax.all_gather(part, "pair")
    return finish(parts, table)


def solution(mesh):
    placed = (
        P(None, "blk"),
        P(None, "blk"),
        P("blk"),
        P(),
        P("blk", "pair", None, None),
        P(None, "blk"),
    )
    return jax.shard_map(
        shards,
        mesh=mesh,
        in_specs=placed,
        out_specs=(P(None, "blk"), P(None, "blk")),
        check_vma=False,
    )
```

time: 105 us -> 96.2 us (0.916)
  blocking collectives: 48 us -> 41.4 us
  starting transfers between devices: 25.5 us -> 22.1 us
  Pallas kernels: 16.7 us -> 17.8 us
    all_gather x1, blocking collectives: 24.4 us -> 17.8 us  [shards(): parts = lax.all_gather(part, 'pair')]
    ppermute x2 -> x1, starting transfers between devices: 21.4 us -> 18 us  [shards(): halo = lax.ppermute(edge, both, hops)]
    pallas_call x2, Pallas kernels: 14.3 us -> 15.4 us  [pair_call(): pl.pallas_call(body, out_shape=outputs, in_specs=in_specs, out_specs=jax....]
  transfers between devices with their start and end apart: 4 -> 3, of which waited for: 1 -> 1; matrix products, arithmetic and copies ran while one was open for 2% -> 2% of each run, Pallas kernels for 7% -> 8%
where the time goes in v4:
time: 96.2 us; the launch traced here: 95.8 us
  blocking collectives  41.4 us (43%)
  starting transfers between devices  22.1 us (23%)
  Pallas kernels  17.8 us (19%)
  waiting for transfers between devices  7.72 us (8%)
  local copies, waits for them, and re-layouts  3.06 us (3%)
  other arithmetic  2.27 us (2%)
  between operations  1.37 us (1%)
    all_to_all x1, blocking collectives, shards(): held = lax.all_to_all(code, 'pair', 0, 0, tiled=True)  23.6 us
    ppermute x1, starting transfers between devices, shards(): halo = lax.ppermute(edge, both, hops)  18 us
    all_gather x1, blocking collectives, shards(): parts = lax.all_gather(part, 'pair')  17.8 us
    pallas_call x2, Pallas kernels, pair_call(): pl.pallas_call(body, out_shape=outputs, in_specs=in_specs, out_specs=jax....  15.4 us
    all_to_all x1, waiting for transfers between devices, shards(): rows = lax.all_to_all(copies, 'blk', 0, 0, axis_index_groups=along)  7.72 us
    all_to_all x1, starting transfers between devices, shards(): rows = lax.all_to_all(copies, 'blk', 0, 0, axis_index_groups=along)  3.41 us
  transfers between devices with their start and end apart: 3, of which 1 were waited for; matrix products, arithmetic and copies ran while one was open for 2% of the time, Pallas kernels for 8%

profile of v4, /device:TPU:1, one launch (start us, length us, event | category | flops | bytes accessed | tf_op | source)
XLA Modules:
  0.0 95.8 jit_solution(10928057229045318875)
XLA Ops:
  0.6 0.5 broadcast.19
  1.1 1.3 %reduce.3 = s32[64]{0:T(128)S(1)} reduce(s32[1,1,64,1]{2,3,1,0:T(1,128)} %param.10, s32[]{:T(128)} %broadcast.19), dimensions={0,1,3}, to_apply=%param.10.reduce_sub_computation.3 | reduce | bytes 516 | tf_op args[4]
  2.5 0.1 reshape.25
  2.5 23.6 %all_to_all.14 = s32[16,1,8]{2,1,0:T(1,128)S(1)} all-to-all(s32[16,1,8]{2,1,0:T(1,128)S(1)} %bitcast.16), channel_id=1, replica_groups=mesh['blk'=64,'pair'=16] {'pair'}, dimensions={0} | all-to-all | bytes 1024 | tf_op jit(solution)/shard_map/all_to_all | solution.py:280
  26.1 0.1 convert_reduce_fusion
  26.2 0.1 reshape.26
  26.3 0.8 select_maximum_fusion.own_ref.refs_2_
  27.1 0.7 collective-permute-start
  27.8 0.0 collective-permute-done
  27.8 0.7 broadcast_in_dim.16
  28.5 3.4 %all-to-all-start.1 = ((f32[8,8,1024]{2,1,0:T(8,128)}), f32[8,8,1024]{2,1,0:T(8,128)S(1)}, u32[]{:S(2)}, u32[]{:S(2)}) async-start(f32[8,8,1024]{2,1,0:T(8,128)} %broadcast_in_dim.16), calls=%async_computation.1 | async-start | bytes 524288 | tf_op jit(solution)/shard_map/all_to_all | solution.py:286
  32.6 0.8 slice.17
  33.4 0.8 fusion.1
  34.1 0.1 concatenate.19.corner_ref
  34.2 0.8 incidence.1.table_ref
  35.0 0.1 add_bitcast_fusion.place_ref
  35.1 7.7 %all-to-all-done.1.rows_ref.refs_3_ = f32[8,8,1024]{2,1,0:T(8,128)S(1)} async-done(((f32[8,8,1024]{2,1,0:T(8,128)}), f32[8,8,1024]{2,1,0:T(8,128)S(1)}, u32[]{:S(2)}, u32[]{:S(2)}) %all-to-all-start.1) | async-done | bytes 262176 | tf_op jit(solution)/shard_map/all_to_all | solution.py:286
  42.8 8.5 %outer_block.1 = (f32[8,256]{1,0:T(8,128)S(1)}, f32[1,512]{1,0:T(1,128)S(1)}, bf16[32,64,256]{2,1,0:T(8,128)(2,1)S(1)}, bf16[32,32,256]{2,1,0:T(8,128)(2,1)S(1)}) custom-call(s32[1,2]{1,0:T(1,128)S(1)} %add_bitcast_fusion.place_ref, s32[9,128]{1,0:T(8,128)S(1)} %maximum_convert_fusion.count_ref.refs_0_, f32[1,1]{1,0:T(1,128)} %bitcast.13.scale_ref, ...), custom_call_target="tpu_custom_call" | custom-call | flops 688128000 | bytes 2097152 | tf_op jit(solution)/shard_map/outer_block/pallas_call | solution.py:185
  51.3 18.0 %collective-permute-start.1 = (f32[1,512]{1,0:T(1,128)S(1)}, f32[1,512]{1,0:T(1,128)S(1)}, u32[]{:S(2)}, u32[]{:S(2)}) collective-permute-start(f32[1,512]{1,0:T(1,128)S(1)} %get-tuple-element.9), channel_id=1, source_target_pairs={{0,16},{1,1009},{2,18},{3,1011},{4,20},{5,1013},{6,22},{7,1015},{8... | collective-permute-start | bytes 6152 | tf_op jit(solution)/shard_map/ppermute | solution.py:304
  69.4 7.0 %inner_block.1 = f32[8,256]{1,0:T(8,128)S(1)} custom-call(s32[1,2]{1,0:T(1,128)S(1)} %add_bitcast_fusion.place_ref, s32[9,128]{1,0:T(8,128)S(1)} %maximum_convert_fusion.count_ref.refs_0_, f32[1,1]{1,0:T(1,128)} %bitcast.14.refs_1_, f32[8,1024]{1,0:T(8,128)S(1)} %select_maximum_fusion.own_ref.refs_2_, f32[8,8,1024]{2,1,0:T(8,128)S(1)} %all-to-all-done.1.rows_ref.refs_3_, ...), custom_call_target="tpu_custom_call" | custom-call | flops 688128000 | bytes 2097152 | tf_op jit(solution)/shard_map/inner_block/pallas_call | solution.py:185
  76.3 0.0 collective-permute-done.1
  76.3 17.8 %all-gather = f32[128,512]{1,0:T(8,128)S(1)} all-gather(f32[8,512]{1,0:T(8,128)S(1)} %fusion), channel_id=2, replica_groups=mesh['blk'=64,'pair'=16] {'pair'}, dimensions={0}, use_global_device_ids=true | all-gather | bytes 278528 | tf_op jit(solution)/shard_map/all_gather | solution.py:307
  94.1 1.6 %finish.1 = (f32[3,512]{1,0:T(4,128)}, f32[4,1024]{1,0:T(4,128)}) custom-call(f32[16,8,512]{2,1,0:T(8,128)S(1)} %bitcast.15, bf16[512,1152]{1,0:T(8,128)(2,1)S(1)} %incidence.1.table_ref), custom_call_target="tpu_custom_call" | custom-call | tf_op jit(solution)/shard_map/finish/pallas_call | solution.py:253
  (4 shorter events, 0.0 us)
Async XLA Ops:
  27.1 0.7 collective-permute-start
  28.5 14.3 %all-to-all-start.1 = ((f32[8,8,1024]{2,1,0:T(8,128)}), f32[8,8,1024]{2,1,0:T(8,128)S(1)}, u32[]{:S(2)}, u32[]{:S(2)}) async-start(f32[8,8,1024]{2,1,0:T(8,128)} %broadcast_in_dim.16), calls=%async_computation.1 | async-start | bytes 524288 | tf_op jit(solution)/shard_map/all_to_all | solution.py:286
  51.3 25.0 %collective-permute-start.1 = (f32[1,512]{1,0:T(1,128)S(1)}, f32[1,512]{1,0:T(1,128)S(1)}, u32[]{:S(2)}, u32[]{:S(2)}) collective-permute-start(f32[1,512]{1,0:T(1,128)S(1)} %get-tuple-element.9), channel_id=1, source_target_pairs={{0,16},{1,1009},{2,18},{3,1011},{4,20},{5,1013},{6,22},{7,1015},{8... | collective-permute-start | bytes 6152 | tf_op jit(solution)/shard_map/ppermute | solution.py:304

commit v5 on v4

v5 whole, which is shorter than its diff:
```python
import functools

import jax
import jax.numpy as jnp
from jax import lax
from jax.experimental import pallas as pl
from jax.experimental.pallas import tpu as pltpu
from jax.sharding import PartitionSpec as P

BLOCK = 256
FB_DEV = 4
HALO_FACES = 64
CODES = FB_DEV * FB_DEV
DEPTH = 64
SLICE = 128
LEFT = (0, 0, 1, 1, 0, 2)
RIGHT = (0, 1, 0, 1, 2, 0)
ONES = (0, 1, 4)
F32 = jnp.float32
BF16 = jnp.bfloat16
VMEM = pl.BlockSpec(memory_space=pltpu.VMEM)
SMEM = pl.BlockSpec(memory_space=pltpu.SMEM)
dot = functools.partial(jnp.dot, preferred_element_type=F32)


def thirds(values):
    high = values.astype(BF16).astype(F32)
    rest = values - high
    middle = rest.astype(BF16).astype(F32)
    return [high, middle, (rest - middle).astype(BF16).astype(F32)]


def square(x):
    return jnp.sum(x[0:3] * x[0:3], axis=0, keepdims=True)


def lever(x):
    return jnp.sum(x[0:3] * x[3:6], axis=0, keepdims=True)


def partner_features(rows, left_ref, feat_ref, base):
    x = jnp.concatenate(rows, axis=1)
    width = x.shape[1]
    row = lax.broadcasted_iota(jnp.int32, x.shape, 0)
    area = x[6:7]
    x = jnp.where(row >= 6, 1.0, x)
    split = thirds(x)
    extra = thirds(square(x)) + thirds(lever(x)) + [jnp.zeros((10, width), F32)]
    left = jnp.concatenate([split[i] for i in LEFT] + extra, axis=0).astype(BF16)
    feat = jnp.concatenate(thirds(x * area) + [jnp.zeros((8, width), F32)], axis=0).astype(BF16)
    for i in range(len(rows)):
        columns = slice(i * SLICE, (i + 1) * SLICE)
        left_ref[base + i] = left[:, columns]
        feat_ref[base + i] = feat[:, columns]


def own_features(x, right_ref, at):
    row = lax.broadcasted_iota(jnp.int32, (8, BLOCK), 0)
    zero = jnp.zeros((8, BLOCK), F32)
    first, second = row < 3, jnp.logical_and(row >= 3, row < 6)
    center = thirds(-2.0 * x)
    swapped = thirds(jnp.concatenate([x[3:6], x[0:3], x[6:8]], axis=0))
    distance, level = thirds(square(x) + 1.0), thirds(lever(x))
    sides = (
        [jnp.where(first, center[i], zero) for i in RIGHT],
        [jnp.where(first, -swapped[i], zero) for i in RIGHT],
        [jnp.where(second, swapped[i], zero) for i in RIGHT],
    )
    for i, g in enumerate(ONES):
        sides[0][g] = jnp.where(row == 7, distance[i], sides[0][g])
        sides[1][g] = jnp.where(row == 7, level[i], sides[1][g])
    tails = (jnp.where(first, 1.0, zero), zero, jnp.where(second, -1.0, zero))
    for m in range(3):
        right_ref[at, m] = jnp.concatenate(sides[m] + [tails[m], zero], axis=0).astype(BF16)


def own_block(core, at):
    return jnp.where(core == 0, FB_DEV - 1 - at, at)


def feature_kernel(place_ref, own_ref, rows_ref, left_ref, feat_ref, right_ref):
    for at in range(2):
        first = pl.multiple_of(own_block(place_ref[0, 0], at) * BLOCK, BLOCK)
        own_features(own_ref[:, pl.ds(first, BLOCK)], right_ref, at)
    for k in range(0, rows_ref.shape[0], 8):
        partner_features([rows_ref[k + i] for i in range(8)], left_ref, feat_ref, k)


def features(place, own, rows):
    n = rows.shape[0]
    return pl.pallas_call(
        feature_kernel,
        out_shape=(
            jax.ShapeDtypeStruct((n, DEPTH, SLICE), BF16),
            jax.ShapeDtypeStruct((n, 32, SLICE), BF16),
            jax.ShapeDtypeStruct((2, 3, DEPTH, BLOCK), BF16),
        ),
        in_specs=[SMEM, VMEM, VMEM],
        out_specs=(VMEM, VMEM, VMEM),
        compiler_params=pltpu.CompilerParams(vmem_limit_bytes=16 * 1024 * 1024),
        cost_estimate=pl.CostEstimate(flops=1 << 22, bytes_accessed=1 << 20, transcendentals=0),
        name="features",
    )(place, own, rows)


def tally_kernel(place_ref, held_ref, out_ref):
    other = place_ref[0, 1]
    held = held_ref[...]
    lane = lax.broadcasted_iota(jnp.int32, (1, held.shape[2]), 1)
    for o in range(FB_DEV):
        code = jnp.where(lane < held.shape[2] // 2, o * FB_DEV + other, other * FB_DEV + o)
        out_ref[o : o + 1, :] = jnp.sum(jnp.where(held == code[None], 1.0, 0.0), axis=0).astype(jnp.int32)


def tally(place, held):
    return pl.pallas_call(
        tally_kernel,
        out_shape=jax.ShapeDtypeStruct((FB_DEV, held.shape[2]), jnp.int32),
        in_specs=[SMEM, VMEM],
        out_specs=VMEM,
        compiler_params=pltpu.CompilerParams(vmem_limit_bytes=16 * 1024 * 1024),
        name="tally",
    )(place, held)


def list_cells(mine, count_ref, list_ref):
    list_ref[0] = 0
    list_ref[1] = 0
    found = jnp.int32(0)
    for role in range(2):

        def step(q, found):
            count = count_ref[mine, role * (count_ref.shape[1] // 2) + q]
            list_ref[found + 2] = count * 65536 + role * 256 + q
            return found + (count > 0).astype(jnp.int32)

        found = lax.fori_loop(0, count_ref.shape[1] // 2, step, found, unroll=16)
        list_ref[found + 2] = role * 256
        found = (found + 1) // 2 * 2
    for u in range(6):
        list_ref[found + 2 + u] = 0
    return found // 2


def unpack(entry):
    return entry // 65536, (entry // 256) % 256, entry % 256


def both(ref, list_ref, step):
    return jnp.concatenate([ref[list_ref[2 * step + h] % 256] for h in range(2)], axis=1)


def products(step, list_ref, left_ref, right_ref, at, out_ref):
    role = unpack(list_ref[2 * step])[1]
    left = both(left_ref, list_ref, step)
    over = (((0,), (0,)), ((), ()))
    out_ref[0] = lax.dot_general(left, right_ref[at, 0], over, preferred_element_type=F32)
    out_ref[1] = lax.dot_general(left, right_ref[at, 1 + role], over, preferred_element_type=F32)


def weights(step, list_ref, rows_ref, in_ref, out_ref, kernel_ref):
    for h in range(2):
        count, _, x = unpack(list_ref[2 * step + h])
        area = rows_ref[x].T[:, 6:7]
        here = slice(h * SLICE, (h + 1) * SLICE)
        inverse = pl.reciprocal(in_ref[0, here], approx=True)
        projected = in_ref[1, here]
        scaled = inverse * inverse * count.astype(F32)
        kernel = (projected * projected + 1.0) * scaled
        kernel_ref[...] += jnp.sum((kernel * area).reshape(SLICE // 8, 8, BLOCK), axis=0)
        for m, values in enumerate((kernel * inverse, projected * scaled)):
            high = values.astype(BF16)
            out_ref[m, 0, here] = high
            out_ref[m, 1, here] = (values - high.astype(F32)).astype(BF16)


def reduce_cells(step, list_ref, feat_ref, in_ref, acc_ref):
    role = unpack(list_ref[2 * step])[1]
    feat = both(feat_ref, list_ref, step)
    for m, place in enumerate((0, 1 + role)):
        acc_ref[place] += dot(feat, in_ref[m, 0]) + dot(feat, in_ref[m, 1])


def pair_body(at, place_ref, count_ref, scale_ref, own_ref, rows_ref, left_ref, feat_ref, right_ref, out_ref, acc_ref, kernel_ref, list_ref, *stages):
    product_refs, weight_refs = stages[:2], stages[2:]
    mine = own_block(place_ref[0, 0], at)
    steps = list_cells(mine, count_ref, list_ref)
    own = own_ref[:, pl.ds(pl.multiple_of(mine * BLOCK, BLOCK), BLOCK)]
    acc_ref[...] = jnp.zeros_like(acc_ref)
    kernel_ref[...] = jnp.zeros_like(kernel_ref)
    weight_refs[1][...] = jnp.zeros_like(weight_refs[1])
    products(1, list_ref, left_ref, right_ref, at, product_refs[0])

    def visit(i, carry):
        for u in range(2):
            now, later, step = u, 1 - u, 2 * i + u
            reduce_cells(step, list_ref, feat_ref, weight_refs[later], acc_ref)
            weights(step + 1, list_ref, rows_ref, product_refs[now], weight_refs[now], kernel_ref)
            products(step + 2, list_ref, left_ref, right_ref, at, product_refs[later])
        return carry

    rounds = (steps + 1) // 2
    lax.fori_loop(0, rounds, visit, 0)
    reduce_cells(2 * rounds, list_ref, feat_ref, weight_refs[1], acc_ref)

    scale = scale_ref[0, 0]
    pushing, target, source = (acc_ref[m, 0:8] + acc_ref[m, 8:16] + acc_ref[m, 16:24] for m in range(3))
    center, normal = own[0:3], own[3:6]
    weight = scale * own[6:7]
    push = center * pushing[6:7] - pushing[0:3]
    pull = normal * target[6:7] + source[3:6]
    out_ref[0:3, :] = weight * (2.0 * pull - 4.0 * push)
    out_ref[3:6, :] = 2.0 * weight * (center * target[6:7] - target[0:3])
    out_ref[6:7, :] = scale * jnp.sum(kernel_ref[...], axis=0, keepdims=True)
    out_ref[7:8, :] = jnp.zeros((1, BLOCK), F32)


def outer_kernel(*refs):
    place_ref, (out_ref, edge_ref), scratch = refs[0], refs[8:10], refs[10:]
    pair_body(0, *refs[:8], out_ref, *scratch)
    core = place_ref[0, 0]
    gap = jnp.zeros((1, HALO_FACES), F32)
    tails, heads = [], []
    for c in range(3):
        tails += [out_ref[c : c + 1, BLOCK - HALO_FACES :], gap]
        heads += [gap, out_ref[c : c + 1, :HALO_FACES]]
    rest = [gap] * (2 * BLOCK // HALO_FACES - 6)
    edge_ref[...] = jnp.where(core == 0, jnp.concatenate(tails + rest, axis=1), jnp.concatenate(heads + rest, axis=1))


def inner_kernel(*refs):
    pair_body(1, *refs)


def pair_call(body, outputs, operands, name):
    partners = operands[1].shape[1] // 2
    cells = partners // 3
    in_specs = [SMEM] * 3 + [VMEM] * (len(operands) - 3)
    return pl.pallas_call(
        body,
        out_shape=outputs,
        in_specs=in_specs,
        out_specs=jax.tree.map(lambda _: VMEM, outputs),
        scratch_shapes=[
            pltpu.VMEM((3, 32, BLOCK), F32),
            pltpu.VMEM((8, BLOCK), F32),
            pltpu.SMEM((2 * partners + 16,), jnp.int32),
        ]
        + [pltpu.VMEM((2, 2 * SLICE, BLOCK), F32)] * 2
        + [pltpu.VMEM((2, 2, 2 * SLICE, BLOCK), BF16)] * 2,
        compiler_params=pltpu.CompilerParams(vmem_limit_bytes=24 * 1024 * 1024),
        cost_estimate=pl.CostEstimate(
            flops=cells * BLOCK * BLOCK * 500, bytes_accessed=1 << 21, transcendentals=cells * BLOCK * BLOCK
        ),
        name=name,
    )(*operands)


def incidence_kernel(corner_ref, out_ref):
    verts, faces = out_ref.shape
    vertex = lax.broadcasted_iota(jnp.int32, (verts, 128), 0)
    for e in range(0, faces, 128):
        total = jnp.zeros((verts, 128), F32)
        for k in range(3):
            total = total + jnp.where(corner_ref[k : k + 1, e : e + 128] == vertex, 1.0, 0.0)
        out_ref[:, e : e + 128] = total.astype(BF16)


def incidence_table(corner, verts):
    faces = corner.shape[1]
    return pl.pallas_call(
        incidence_kernel,
        out_shape=jax.ShapeDtypeStruct((verts, faces), BF16),
        in_specs=[VMEM],
        out_specs=VMEM,
        compiler_params=pltpu.CompilerParams(vmem_limit_bytes=16 * 1024 * 1024),
        cost_estimate=pl.CostEstimate(flops=verts * faces * 9, bytes_accessed=verts * faces * 2, transcendentals=0),
        name="incidence",
    )(corner)


def finish_kernel(parts_ref, table_ref, vertex_ref, face_ref):
    sums = []
    for core in range(2):
        total = parts_ref[core]
        for i in range(core + 2, parts_ref.shape[0], 2):
            total = total + parts_ref[i]
        sums.append(total)
    low, high = sums[1], sums[0]
    total = jnp.concatenate([low[:, :BLOCK], low[:, BLOCK:], high[:, BLOCK:], high[:, :BLOCK]], axis=1)
    faces = total.shape[1]
    width = 2 * HALO_FACES
    face_ref[...] = total[3:7]
    edges = low[7:8] + high[7:8]
    edge = jnp.concatenate([edges[:, c * width : (c + 1) * width] for c in range(3)], axis=0)
    contract = (((1,), (1,)), ((), ()))
    out = jnp.zeros((3, vertex_ref.shape[1]), F32)
    for main, side in zip(thirds(total[0:3]), thirds(edge)):
        out = out + lax.dot_general(main.astype(BF16), table_ref[:, 0:faces], contract, preferred_element_type=F32)
        out = out + lax.dot_general(side.astype(BF16), table_ref[:, faces:], contract, preferred_element_type=F32)
    vertex_ref[...] = out / 3.0


def finish(parts, table):
    verts, faces = table.shape[0], 2 * parts.shape[2]
    return pl.pallas_call(
        finish_kernel,
        out_shape=(jax.ShapeDtypeStruct((3, verts), F32), jax.ShapeDtypeStruct((4, faces), F32)),
        in_specs=[VMEM, VMEM],
        out_specs=(VMEM, VMEM),
        compiler_params=pltpu.CompilerParams(vmem_limit_bytes=16 * 1024 * 1024),
        name="finish",
    )(parts, table)


def shards(centroids, normals, areas, cotangent, pair_code, corner_vertex):
    count, shares = lax.axis_size("blk"), lax.axis_size("pair")
    faces = centroids.shape[1]
    assert shares // 2 * SLICE == faces
    member = lax.axis_index("pair")
    core, slab = member % 2, member // 2
    other_block = slab * SLICE // BLOCK

    own = jnp.concatenate([centroids, normals, areas[None], jnp.zeros((1, faces), F32)], axis=0)
    codes = pair_code.reshape(count)
    piece = lax.dynamic_slice_in_dim(own, slab * SLICE, SLICE, axis=1)
    line = lax.broadcasted_iota(jnp.int32, (1, 8, SLICE), 1)
    chunks = jnp.where(line == 7, codes.astype(F32)[:, None, None], piece[None])
    rows = lax.all_to_all(chunks, "blk", 0, 0)

    incoming = rows[:, 7, 0].astype(jnp.int32)
    pack = jnp.concatenate([incoming, codes]).reshape(1, 1, 2 * count)
    held = lax.all_to_all(jnp.broadcast_to(pack, (shares, 1, 2 * count)), "pair", 0, 0)
    place = jnp.stack([core, other_block]).reshape(1, 2)
    counts = tally(place, held)
    scale = cotangent.reshape(1, 1)
    corner = jnp.concatenate(
        [corner_vertex[:, HALO_FACES:-HALO_FACES], corner_vertex[:, :HALO_FACES], corner_vertex[:, -HALO_FACES:]], axis=1
    )
    table = incidence_table(corner, faces // 2)

    block = jax.ShapeDtypeStruct((8, BLOCK), F32)
    edge_row = jax.ShapeDtypeStruct((1, 2 * BLOCK), F32)
    operands = (place, counts, scale, own, rows, *features(place, own, rows))
    outer, edge = pair_call(outer_kernel, (block, edge_row), operands, "outer_block")

    def neighbour(b, member):
        return (b + (1 if member % 2 == 0 else count - 1)) % count * shares + member

    hops = [(b * shares + m, neighbour(b, m)) for b in range(count) for m in range(shares)]
    halo = lax.ppermute(edge, ("blk", "pair"), hops)
    inner = pair_call(inner_kernel, block, operands, "inner_block")
    part = jnp.concatenate([jnp.concatenate([outer, inner], axis=1)[:7], halo], axis=0)
    parts = lax.all_gather(part, "pair")
    return finish(parts, table)


def solution(mesh):
    placed = (
        P(None, "blk"),
        P(None, "blk"),
        P("blk"),
        P(),
        P("blk", "pair", None, None),
        P(None, "blk"),
    )
    return jax.shard_map(
        shards,
        mesh=mesh,
        in_specs=placed,
        out_specs=(P(None, "blk"), P(None, "blk")),
        check_vma=False,
    )
```

time: 96.2 us -> 94.5 us (0.982)
  blocking collectives: 41.4 us -> 17.4 us
  starting transfers between devices: 22.1 us -> 37.3 us
  waiting for transfers between devices: 7.72 us -> 15.3 us
  other arithmetic: 2.27 us -> 4.37 us
  Pallas kernels: 17.8 us -> 15.8 us
    all_to_all x1 -> x2, starting transfers between devices: 3.41 us -> 34 us  [the longest x1 23.2 us: shards(): rows = lax.all_to_all(chunks, 'blk', 0, 0)]
    all_to_all x1 -> x0, blocking collectives: 23.6 us -> none  [shards(): held = lax.all_to_all(code, 'pair', 0, 0, tiled=True)]
    ppermute x2 -> x1, starting transfers between devices: 18.7 us -> 3.34 us  [shards(): halo = lax.ppermute(edge, ('blk', 'pair'), hops)]
    all_to_all x1 -> x2, waiting for transfers between devices: 7.72 us -> 15.3 us  [the longest x1 11.8 us: shards(): rows = lax.all_to_all(chunks, 'blk', 0, 0)]
    pallas_call x2, Pallas kernels: 15.4 us -> 11.8 us  [pair_call(): pl.pallas_call(body, out_shape=outputs, in_specs=in_specs, out_specs=jax....]
    convert_element_type x1 -> x2, other arithmetic: 0.01 us -> 1.88 us  [the longest x1 1.22 us: shards(): incoming = rows[:, 7, 0].astype(jnp.int32)]
    pallas_call x0 -> x2, Pallas kernels: none -> 1.65 us  [the longest x1 1.06 us: features(): pl.pallas_call(feature_kernel, out_shape=(jax.ShapeDtypeStruct((n, DEPTH,...]
    unnamed x1 -> x0, other arithmetic: 1.32 us -> none
  transfers between devices with their start and end apart: 3 -> 3, of which waited for: 1 -> 2; matrix products, arithmetic and copies ran while one was open for 2% -> 2% of each run, Pallas kernels for 8% -> 8%
where the time goes in v5:
time: 94.5 us; the launch traced here: 93.9 us
  starting transfers between devices  37.3 us (39%)
  blocking collectives  17.4 us (18%)
  Pallas kernels  15.8 us (17%)
  waiting for transfers between devices  15.3 us (16%)
  other arithmetic  4.37 us (5%)
  local copies, waits for them, and re-layouts  2.35 us (2%)
  between operations  1.41 us (1%)
    all_to_all x1, starting transfers between devices, shards(): rows = lax.all_to_all(chunks, 'blk', 0, 0)  23.2 us
    all_gather x1, blocking collectives, shards(): parts = lax.all_gather(part, 'pair')  17.4 us
    all_to_all x1, waiting for transfers between devices, shards(): rows = lax.all_to_all(chunks, 'blk', 0, 0)  11.8 us
    pallas_call x2, Pallas kernels, pair_call(): pl.pallas_call(body, out_shape=outputs, in_specs=in_specs, out_specs=jax....  11.8 us
    all_to_all x1, starting transfers between devices, shards(): lax.all_to_all(jnp.broadcast_to(pack, (shares, 1, 2 * count)), 'pair', 0, 0)  10.8 us
    all_to_all x1, waiting for transfers between devices, shards(): lax.all_to_all(jnp.broadcast_to(pack, (shares, 1, 2 * count)), 'pair', 0, 0)  3.49 us
    ppermute x1, starting transfers between devices, shards(): halo = lax.ppermute(edge, ('blk', 'pair'), hops)  3.34 us
  transfers between devices with their start and end apart: 3, of which 2 were waited for; matrix products, arithmetic and copies ran while one was open for 2% of the time, Pallas kernels for 8%

profile of v5, /device:TPU:1, one launch (start us, length us, event | category | flops | bytes accessed | tf_op | source)
XLA Modules:
  0.0 93.9 jit_solution(13474142681942357928)
XLA Ops:
  0.7 0.7 bitcast_convert_fusion
  1.3 0.1 pad.9.clone
  1.4 0.8 maximum_maximum_fusion.own_ref.refs_3_
  2.2 0.8 broadcast_select_fusion
  3.1 23.2 %all-to-all-start = ((f32[64,8,128]{2,1,0:T(8,128)}), f32[64,8,128]{2,1,0:T(8,128)S(1)}, u32[]{:S(2)}, u32[]{:S(2)}) async-start(f32[64,8,128]{2,1,0:T(8,128)} %broadcast_select_fusion), calls=%async_computation | async-start | bytes 524288 | tf_op jit(solution)/shard_map/all_to_all | solution.py:329
  26.3 0.8 fusion.2
  27.0 11.8 %all-to-all-done.rows_ref.refs_4_ = f32[64,8,128]{2,1,0:T(8,128)S(1)} async-done(((f32[64,8,128]{2,1,0:T(8,128)}), f32[64,8,128]{2,1,0:T(8,128)S(1)}, u32[]{:S(2)}, u32[]{:S(2)}) %all-to-all-start) | async-done | bytes 262176 | tf_op jit(solution)/shard_map/all_to_all | solution.py:329
  38.9 1.2 %fusion = s32[64]{0:T(128)S(1)} fusion(f32[64,8,128]{2,1,0:T(8,128)S(1)} %all-to-all-done.rows_ref.refs_4_), kind=kLoop, calls=%fused_computation.2 | loop fusion | flops 64 | bytes 512 | tf_op jit(solution)/shard_map/convert_element_type | solution.py:331
  40.1 0.7 pad_add_fusion
  40.9 0.6 broadcast_in_dim.42
  41.5 10.8 %all-to-all-start.1 = ((s32[16,1,128]{2,1,0:T(1,128)}), s32[16,1,128]{2,1,0:T(1,128)S(1)}, u32[]{:S(2)}, u32[]{:S(2)}) async-start(s32[16,1,128]{2,1,0:T(1,128)} %broadcast_in_dim.42), calls=%async_computation.1 | async-start | bytes 16384 | tf_op jit(solution)/shard_map/all_to_all | solution.py:333
  52.3 0.1 add_bitcast_fusion.place_ref.refs_0_
  52.3 0.8 slice.17
  53.8 0.1 concatenate.19.corner_ref
  53.9 0.8 incidence.1.table_ref
  54.6 1.1 %features.1 = (bf16[64,64,128]{2,1,0:T(8,128)(2,1)S(1)}, bf16[64,32,128]{2,1,0:T(8,128)(2,1)S(1)}, bf16[2,3,64,256]{3,2,1,0:T(8,128)(2,1)S(1)}) custom-call(s32[1,2]{1,0:T(1,128)S(1)} %add_bitcast_fusion.place_ref.refs_0_, f32[8,1024]{1,0:T(8,128)S(1)} %maximum_maximum_fusion.own_ref.refs_3_, f32[64,8,128]{2,1,0:T(8,128)S(1)} %all-to-all-done.rows_ref.refs_4_), custom_call_target="tpu_custom_call" | custom-call | flops 4194304 | bytes 1048576 | tf_op jit(solution)/shard_map/features/pallas_call | solution.py:91
  55.7 3.5 %all-to-all-done.1.held_ref = s32[16,1,128]{2,1,0:T(1,128)S(1)} async-done(((s32[16,1,128]{2,1,0:T(1,128)}), s32[16,1,128]{2,1,0:T(1,128)S(1)}, u32[]{:S(2)}, u32[]{:S(2)}) %all-to-all-start.1) | async-done | bytes 8224 | tf_op jit(solution)/shard_map/all_to_all | solution.py:333
  59.2 0.6 tally.1.refs_1_
  59.8 6.2 %outer_block.1 = (f32[8,256]{1,0:T(8,128)S(1)}, f32[1,512]{1,0:T(1,128)S(1)}) custom-call(s32[1,2]{1,0:T(1,128)S(1)} %add_bitcast_fusion.place_ref.refs_0_, s32[4,128]{1,0:T(4,128)S(1)} %tally.1.refs_1_, f32[1,1]{1,0:T(1,128)} %bitcast.10.refs_2_, f32[8,1024]{1,0:T(8,128)S(1)} %maximum_maximum_fusion.own_ref.refs_3_, ...), custom_call_target="tpu_custom_call" | custom-call | flops 688128000 | bytes 2097152 | tf_op jit(solution)/shard_map/outer_block/pallas_call | solution.py:239
  66.0 3.3 %collective-permute-start = (f32[1,512]{1,0:T(1,128)S(1)}, f32[1,512]{1,0:T(1,128)S(1)}, u32[]{:S(2)}, u32[]{:S(2)}) collective-permute-start(f32[1,512]{1,0:T(1,128)S(1)} %get-tuple-element.11), channel_id=1, source_target_pairs={{0,16},{1,1009},{2,18},{3,1011},{4,20},{5,1013},{6,22},{7,1015},{8... | collective-permute-start | bytes 6152 | tf_op jit(solution)/shard_map/ppermute | solution.py:351
  69.3 5.6 %inner_block.1 = f32[8,256]{1,0:T(8,128)S(1)} custom-call(s32[1,2]{1,0:T(1,128)S(1)} %add_bitcast_fusion.place_ref.refs_0_, s32[4,128]{1,0:T(4,128)S(1)} %tally.1.refs_1_, f32[1,1]{1,0:T(1,128)} %bitcast.11.refs_2_, f32[8,1024]{1,0:T(8,128)S(1)} %maximum_maximum_fusion.own_ref.refs_3_, f32[64,8,128]{2,1,0:T(8,128)S(1)} %all-to-all-done.rows_ref.refs_4_, ...), custom_call_target="tpu_custom_call" | custom-call | flops 688128000 | bytes 2097152 | tf_op jit(solution)/shard_map/inner_block/pallas_call | solution.py:239
  74.9 0.0 collective-permute-done
  74.9 17.4 %all-gather = f32[128,512]{1,0:T(8,128)S(1)} all-gather(f32[8,512]{1,0:T(8,128)S(1)} %fusion.1), channel_id=2, replica_groups=mesh['blk'=64,'pair'=16] {'pair'}, dimensions={0}, use_global_device_ids=true | all-gather | bytes 278528 | tf_op jit(solution)/shard_map/all_gather | solution.py:354
  92.3 1.6 %finish.1 = (f32[3,512]{1,0:T(4,128)}, f32[4,1024]{1,0:T(4,128)}) custom-call(f32[16,8,512]{2,1,0:T(8,128)S(1)} %bitcast.12, bf16[512,1152]{1,0:T(8,128)(2,1)S(1)} %incidence.1.table_ref), custom_call_target="tpu_custom_call" | custom-call | tf_op jit(solution)/shard_map/finish/pallas_call | solution.py:306
  (3 shorter events, 0.0 us)
Async XLA Ops:
  3.1 35.8 %all-to-all-start = ((f32[64,8,128]{2,1,0:T(8,128)}), f32[64,8,128]{2,1,0:T(8,128)S(1)}, u32[]{:S(2)}, u32[]{:S(2)}) async-start(f32[64,8,128]{2,1,0:T(8,128)} %broadcast_select_fusion), calls=%async_computation | async-start | bytes 524288 | tf_op jit(solution)/shard_map/all_to_all | solution.py:329
  41.5 17.7 %all-to-all-start.1 = ((s32[16,1,128]{2,1,0:T(1,128)}), s32[16,1,128]{2,1,0:T(1,128)S(1)}, u32[]{:S(2)}, u32[]{:S(2)}) async-start(s32[16,1,128]{2,1,0:T(1,128)} %broadcast_in_dim.42), calls=%async_computation.1 | async-start | bytes 16384 | tf_op jit(solution)/shard_map/all_to_all | solution.py:333
  66.0 9.0 %collective-permute-start = (f32[1,512]{1,0:T(1,128)S(1)}, f32[1,512]{1,0:T(1,128)S(1)}, u32[]{:S(2)}, u32[]{:S(2)}) collective-permute-start(f32[1,512]{1,0:T(1,128)S(1)} %get-tuple-element.11), channel_id=1, source_target_pairs={{0,16},{1,1009},{2,18},{3,1011},{4,20},{5,1013},{6,22},{7,1015},{8... | collective-permute-start | bytes 6152 | tf_op jit(solution)/shard_map/ppermute | solution.py:351

commit v6 on v5

--- a/solution.py
+++ b/solution.py
@@ -106,16 +106,36 @@
 def tally_kernel(place_ref, held_ref, out_ref):
     other = place_ref[0, 1]
     held = held_ref[...]
-    lane = lax.broadcasted_iota(jnp.int32, (1, held.shape[2]), 1)
+    lanes = held.shape[2]
+    half = lanes // 2
+    lane = lax.broadcasted_iota(jnp.int32, (1, lanes), 1)
+    rows = []
     for o in range(FB_DEV):
-        code = jnp.where(lane < held.shape[2] // 2, o * FB_DEV + other, other * FB_DEV + o)
-        out_ref[o : o + 1, :] = jnp.sum(jnp.where(held == code[None], 1.0, 0.0), axis=0).astype(jnp.int32)
+        code = jnp.where(lane < half, o * FB_DEV + other, other * FB_DEV + o)
+        rows.append(jnp.sum(jnp.where(held == code[None], 1.0, 0.0), axis=0))
+    counts = jnp.concatenate(rows + [jnp.zeros((8 - FB_DEV, lanes), F32)], axis=0).T
+    active = counts > 0.0
+    at, before = (lax.broadcasted_iota(jnp.int32, (lanes, lanes), i) for i in range(2))
+    upto = jnp.logical_and(before <= at, (before < half) == (at < half))
+    order = dot(jnp.where(upto, 1.0, 0.0).astype(BF16), jnp.where(active, 1.0, 0.0).astype(BF16)).astype(jnp.int32)
+    place = jnp.where(active, order - 1, -1)
+    index = lax.broadcasted_iota(jnp.int32, counts.shape, 0) % half
+    value = counts.astype(jnp.int32) * 256 + index
+    slot = lax.broadcasted_iota(jnp.int32, (half, 128), 1)
+    for o in range(FB_DEV):
+        for role in range(2):
+            mine = slice(role * half, (role + 1) * half)
+            hit = slot == place[mine, o : o + 1]
+            entries = jnp.sum(jnp.where(hit, value[mine, o : o + 1].astype(F32), 0.0), axis=0, keepdims=True)
+            total = order[(role + 1) * half - 1 : (role + 1) * half, o : o + 1].astype(F32)
+            entries = jnp.where(slot[0:1] == 127, total, entries)
+            out_ref[o : o + 1, role * 128 : (role + 1) * 128] = entries.astype(jnp.int32)
 
 
 def tally(place, held):
     return pl.pallas_call(
         tally_kernel,
-        out_shape=jax.ShapeDtypeStruct((FB_DEV, held.shape[2]), jnp.int32),
+        out_shape=jax.ShapeDtypeStruct((FB_DEV, 256), jnp.int32),
         in_specs=[SMEM, VMEM],
         out_specs=VMEM,
         compiler_params=pltpu.CompilerParams(vmem_limit_bytes=16 * 1024 * 1024),
@@ -123,44 +143,77 @@
     )(place, held)
 
 
-def list_cells(mine, count_ref, list_ref):
-    list_ref[0] = 0
-    list_ref[1] = 0
-    found = jnp.int32(0)
-    for role in range(2):
-
-        def step(q, found):
-            count = count_ref[mine, role * (count_ref.shape[1] // 2) + q]
-            list_ref[found + 2] = count * 65536 + role * 256 + q
-            return found + (count > 0).astype(jnp.int32)
-
-        found = lax.fori_loop(0, count_ref.shape[1] // 2, step, found, unroll=16)
-        list_ref[found + 2] = role * 256
-        found = (found + 1) // 2 * 2
-    for u in range(6):
-        list_ref[found + 2 + u] = 0
-    return found // 2
-
-
-def unpack(entry):
-    return entry // 65536, (entry // 256) % 256, entry % 256
-
-
-def both(ref, list_ref, step):
-    return jnp.concatenate([ref[list_ref[2 * step + h] % 256] for h in range(2)], axis=1)
-
-
-def products(step, list_ref, left_ref, right_ref, at, out_ref):
-    role = unpack(list_ref[2 * step])[1]
-    left = both(left_ref, list_ref, step)
+def prepare_kernel(place_ref, code_ref, center_ref, normal_ref, area_ref, own_ref, chunk_ref):
+    own_ref[0:3, :] = center_ref[...]
+    own_ref[3:6, :] = normal_ref[...]
+    own_ref[6:7, :] = area_ref[...]
+    own_ref[7:8, :] = jnp.zeros_like(area_ref)
+    piece = own_ref[:, pl.ds(pl.multiple_of(place_ref[0, 2] * SLICE, SLICE), SLICE)]
+    last = lax.broadcasted_iota(jnp.int32, piece.shape, 0) == 7
+    for b in range(chunk_ref.shape[0]):
+        chunk_ref[b] = jnp.where(last, code_ref[0, b].astype(F32), piece)
+
+
+def prepare(place, codes, centroids, normals, areas):
+    count, faces = codes.shape[1], centroids.shape[1]
+    return pl.pallas_call(
+        prepare_kernel,
+        out_shape=(jax.ShapeDtypeStruct((8, faces), F32), jax.ShapeDtypeStruct((count, 8, SLICE), F32)),
+        in_specs=[SMEM, SMEM, VMEM, VMEM, VMEM],
+        out_specs=(VMEM, VMEM),
+        compiler_params=pltpu.CompilerParams(vmem_limit_bytes=16 * 1024 * 1024),
+        name="prepare",
+    )(place, codes, centroids, normals, areas)
+
+
+def pack_kernel(code_ref, rows_ref, out_ref):
+    values = rows_ref[:, 7, :]
+    count = values.shape[0]
+    lane, row = (lax.broadcasted_iota(jnp.int32, values.shape, i) for i in (1, 0))
+    incoming = jnp.sum(jnp.where(lane == row, values, 0.0), axis=0, keepdims=True)
+    both_ways = jnp.concatenate([incoming[:, :count], code_ref[...].astype(F32)], axis=1).astype(jnp.int32)
+    out_ref[...] = jnp.broadcast_to(both_ways[None], out_ref.shape)
+
+
+def pack_codes(codes, rows, shares):
+    return pl.pallas_call(
+        pack_kernel,
+        out_shape=jax.ShapeDtypeStruct((shares, 1, 2 * codes.shape[1]), jnp.int32),
+        in_specs=[VMEM, VMEM],
+        out_specs=VMEM,
+        compiler_params=pltpu.CompilerParams(vmem_limit_bytes=16 * 1024 * 1024),
+        name="pack_codes",
+    )(codes, rows)
+
+
+class Steps:
+    def __init__(self, mine, list_ref):
+        self.mine, self.list_ref = mine, list_ref
+        self.first = (list_ref[mine, 127] + 1) // 2
+        self.number = self.first + (list_ref[mine, 255] + 1) // 2
+
+    def role(self, step):
+        return (step >= self.first).astype(jnp.int32)
+
+    def entry(self, step, h):
+        role = self.role(step)
+        entry = self.list_ref[self.mine, role * 128 + 2 * (step - role * self.first) + h]
+        return entry // 256, entry % 256
+
+    def beside(self, step, ref):
+        return jnp.concatenate([ref[self.entry(step, h)[1]] for h in range(2)], axis=1)
+
+
+def products(step, steps, left_ref, right_ref, at, out_ref):
+    left = steps.beside(step, left_ref)
     over = (((0,), (0,)), ((), ()))
     out_ref[0] = lax.dot_general(left, right_ref[at, 0], over, preferred_element_type=F32)
-    out_ref[1] = lax.dot_general(left, right_ref[at, 1 + role], over, preferred_element_type=F32)
-
-
-def weights(step, list_ref, rows_ref, in_ref, out_ref, kernel_ref):
+    out_ref[1] = lax.dot_general(left, right_ref[at, 1 + steps.role(step)], over, preferred_element_type=F32)
+
+
+def weights(step, steps, rows_ref, in_ref, out_ref, kernel_ref):
     for h in range(2):
-        count, _, x = unpack(list_ref[2 * step + h])
+        count, x = steps.entry(step, h)
         area = rows_ref[x].T[:, 6:7]
         here = slice(h * SLICE, (h + 1) * SLICE)
         inverse = pl.reciprocal(in_ref[0, here], approx=True)
@@ -174,34 +227,33 @@
             out_ref[m, 1, here] = (values - high.astype(F32)).astype(BF16)
 
 
-def reduce_cells(step, list_ref, feat_ref, in_ref, acc_ref):
-    role = unpack(list_ref[2 * step])[1]
-    feat = both(feat_ref, list_ref, step)
-    for m, place in enumerate((0, 1 + role)):
+def reduce_cells(step, steps, feat_ref, in_ref, acc_ref):
+    feat = steps.beside(step, feat_ref)
+    for m, place in enumerate((0, 1 + steps.role(step))):
         acc_ref[place] += dot(feat, in_ref[m, 0]) + dot(feat, in_ref[m, 1])
 
 
-def pair_body(at, place_ref, count_ref, scale_ref, own_ref, rows_ref, left_ref, feat_ref, right_ref, out_ref, acc_ref, kernel_ref, list_ref, *stages):
+def pair_body(at, place_ref, list_ref, scale_ref, own_ref, rows_ref, left_ref, feat_ref, right_ref, out_ref, acc_ref, kernel_ref, *stages):
     product_refs, weight_refs = stages[:2], stages[2:]
     mine = own_block(place_ref[0, 0], at)
-    steps = list_cells(mine, count_ref, list_ref)
+    steps = Steps(mine, list_ref)
     own = own_ref[:, pl.ds(pl.multiple_of(mine * BLOCK, BLOCK), BLOCK)]
     acc_ref[...] = jnp.zeros_like(acc_ref)
     kernel_ref[...] = jnp.zeros_like(kernel_ref)
     weight_refs[1][...] = jnp.zeros_like(weight_refs[1])
-    products(1, list_ref, left_ref, right_ref, at, product_refs[0])
+    products(0, steps, left_ref, right_ref, at, product_refs[0])
 
     def visit(i, carry):
         for u in range(2):
             now, later, step = u, 1 - u, 2 * i + u
-            reduce_cells(step, list_ref, feat_ref, weight_refs[later], acc_ref)
-            weights(step + 1, list_ref, rows_ref, product_refs[now], weight_refs[now], kernel_ref)
-            products(step + 2, list_ref, left_ref, right_ref, at, product_refs[later])
+            reduce_cells(jnp.maximum(step - 1, 0), steps, feat_ref, weight_refs[later], acc_ref)
+            weights(step, steps, rows_ref, product_refs[now], weight_refs[now], kernel_ref)
+            products(step + 1, steps, left_ref, right_ref, at, product_refs[later])
         return carry
 
-    rounds = (steps + 1) // 2
+    rounds = (steps.number + 1) // 2
     lax.fori_loop(0, rounds, visit, 0)
-    reduce_cells(2 * rounds, list_ref, feat_ref, weight_refs[1], acc_ref)
+    reduce_cells(jnp.maximum(2 * rounds - 1, 0), steps, feat_ref, weight_refs[1], acc_ref)
 
     scale = scale_ref[0, 0]
     pushing, target, source = (acc_ref[m, 0:8] + acc_ref[m, 8:16] + acc_ref[m, 16:24] for m in range(3))
@@ -233,8 +285,7 @@
 
 
 def pair_call(body, outputs, operands, name):
-    partners = operands[1].shape[1] // 2
-    cells = partners // 3
+    cells = operands[4].shape[0] // 3
     in_specs = [SMEM] * 3 + [VMEM] * (len(operands) - 3)
     return pl.pallas_call(
         body,
@@ -244,7 +295,6 @@
         scratch_shapes=[
             pltpu.VMEM((3, 32, BLOCK), F32),
             pltpu.VMEM((8, BLOCK), F32),
-            pltpu.SMEM((2 * partners + 16,), jnp.int32),
         ]
         + [pltpu.VMEM((2, 2 * SLICE, BLOCK), F32)] * 2
         + [pltpu.VMEM((2, 2, 2 * SLICE, BLOCK), BF16)] * 2,
@@ -321,17 +371,12 @@
     core, slab = member % 2, member // 2
     other_block = slab * SLICE // BLOCK
 
-    own = jnp.concatenate([centroids, normals, areas[None], jnp.zeros((1, faces), F32)], axis=0)
-    codes = pair_code.reshape(count)
-    piece = lax.dynamic_slice_in_dim(own, slab * SLICE, SLICE, axis=1)
-    line = lax.broadcasted_iota(jnp.int32, (1, 8, SLICE), 1)
-    chunks = jnp.where(line == 7, codes.astype(F32)[:, None, None], piece[None])
+    place = jnp.stack([core, other_block, slab]).reshape(1, 3)
+    codes = pair_code.transpose(0, 1, 3, 2).reshape(1, count)
+    own, chunks = prepare(place, codes, centroids, normals, areas.reshape(1, faces))
     rows = lax.all_to_all(chunks, "blk", 0, 0)
 
-    incoming = rows[:, 7, 0].astype(jnp.int32)
-    pack = jnp.concatenate([incoming, codes]).reshape(1, 1, 2 * count)
-    held = lax.all_to_all(jnp.broadcast_to(pack, (shares, 1, 2 * count)), "pair", 0, 0)
-    place = jnp.stack([core, other_block]).reshape(1, 2)
+    held = lax.all_to_all(pack_codes(codes, rows, shares), "pair", 0, 0)
     counts = tally(place, held)
     scale = cotangent.reshape(1, 1)
     corner = jnp.concatenate(
@@ -351,7 +396,7 @@
     halo = lax.ppermute(edge, ("blk", "pair"), hops)
     inner = pair_call(inner_kernel, block, operands, "inner_block")
     part = jnp.concatenate([jnp.concatenate([outer, inner], axis=1)[:7], halo], axis=0)
-    parts = lax.all_gather(part, "pair")
+    parts = lax.all_to_all(jnp.broadcast_to(part[None], (shares, *part.shape)), "pair", 0, 0)
     return finish(parts, table)
 
 

time: 94.5 us -> 94.1 us (level)
  starting transfers between devices: 37.3 us -> 19 us
  blocking collectives: 17.4 us -> 35.6 us
  other arithmetic: 4.37 us -> 0.09 us
  local copies, waits for them, and re-layouts: 2.35 us -> 3.75 us
  Pallas kernels: 15.8 us -> 17.2 us
    all_to_all x0 -> x1, blocking collectives: none -> 35.6 us  [shards(): rows = lax.all_to_all(chunks, 'blk', 0, 0)]
    all_to_all x2, starting transfers between devices: 34 us -> 15.7 us  [the longest x1 10.8 us: shards(): held = lax.all_to_all(pack_codes(codes, rows, shares), 'pair', 0, 0)]
    all_gather x1 -> x0, blocking collectives: 17.4 us -> none  [shards(): parts = lax.all_gather(part, 'pair')]
    unnamed x0 -> x10, local copies, waits for them, and re-layouts: none -> 2.78 us
    convert_element_type x2 -> x0, other arithmetic: 1.88 us -> none  [the longest x1 1.22 us: shards(): incoming = rows[:, 7, 0].astype(jnp.int32)]
    pallas_call x1 -> x3, Pallas kernels: 0.59 us -> 2.25 us  [the longest x1 0.99 us: tally(): pl.pallas_call(tally_kernel, out_shape=jax.ShapeDtypeStruct((FB_DEV, 256)...]
    concatenate x2 -> x0, other arithmetic: 1.56 us -> none  [the longest x1 0.82 us: shards(): jnp.concatenate([centroids, normals, areas[None], jnp.zeros((1, faces), F...]
  transfers between devices with their start and end apart: 3 -> 3, of which waited for: 2 -> 2; matrix products, arithmetic and copies ran while one was open for 2% -> 0% of each run, Pallas kernels for 8% -> 9%
where the time goes in v6:
time: 94.1 us; the launch traced here: 93.2 us
  blocking collectives  35.6 us (38%)
  starting transfers between devices  19 us (20%)
  Pallas kernels  17.2 us (18%)
  waiting for transfers between devices  16.1 us (17%)
  local copies, waits for them, and re-layouts  3.75 us (4%)
  between operations  1.4 us (1%)
    all_to_all x1, blocking collectives, shards(): rows = lax.all_to_all(chunks, 'blk', 0, 0)  35.6 us
    pallas_call x2, Pallas kernels, pair_call(): pl.pallas_call(body, out_shape=outputs, in_specs=in_specs, out_specs=jax....  11.5 us
    all_to_all x1, waiting for transfers between devices, shards(): lax.all_to_all(jnp.broadcast_to(part[None], (shares, *part.shape)), 'pair...  10.8 us
    all_to_all x1, starting transfers between devices, shards(): held = lax.all_to_all(pack_codes(codes, rows, shares), 'pair', 0, 0)  10.8 us
    all_to_all x1, waiting for transfers between devices, shards(): held = lax.all_to_all(pack_codes(codes, rows, shares), 'pair', 0, 0)  5.23 us
    all_to_all x1, starting transfers between devices, shards(): lax.all_to_all(jnp.broadcast_to(part[None], (shares, *part.shape)), 'pair...  4.89 us
    ppermute x1, starting transfers between devices, shards(): halo = lax.ppermute(edge, ('blk', 'pair'), hops)  3.35 us
    unnamed x10, local copies, waits for them, and re-layouts  2.78 us
  transfers between devices with their start and end apart: 3, of which 2 were waited for; matrix products, arithmetic and copies ran while one was open for 0% of the time, Pallas kernels for 9%

profile of v6, /device:TPU:1, one launch (start us, length us, event | category | flops | bytes accessed | tf_op | source)
XLA Modules:
  0.0 93.2 jit_solution(3576190686029260845)
XLA Ops:
  0.7 0.1 add_bitcast_fusion.place_ref.refs_0_
  0.7 0.7 copy-done
  1.5 0.7 copy-done.1
  2.2 0.7 copy-done.2
  2.9 0.7 copy-done.3
  3.5 0.6 prepare.1
  4.1 35.6 %all_to_all.15.rows_ref.refs_4_ = f32[64,8,128]{2,1,0:T(8,128)S(1)} all-to-all(f32[64,8,128]{2,1,0:T(8,128)S(1)} %get-tuple-element.9), channel_id=1, replica_groups=mesh['blk'=64,'pair'=16] {'blk'}, dimensions={0} | all-to-all | bytes 524288 | tf_op jit(solution)/shard_map/all_to_all | solution.py:377
  39.7 0.7 pack_codes.1
  40.4 10.8 %all-to-all-start.1 = ((s32[16,1,128]{2,1,0:T(1,128)}), s32[16,1,128]{2,1,0:T(1,128)S(1)}, u32[]{:S(2)}, u32[]{:S(2)}) async-start(s32[16,1,128]{2,1,0:T(1,128)} %pack_codes.1), calls=%async_computation.1 | async-start | bytes 16384 | tf_op jit(solution)/shard_map/all_to_all | solution.py:379
  51.9 1.1 %features.1 = (bf16[64,64,128]{2,1,0:T(8,128)(2,1)S(1)}, bf16[64,32,128]{2,1,0:T(8,128)(2,1)S(1)}, bf16[2,3,64,256]{3,2,1,0:T(8,128)(2,1)S(1)}) custom-call(s32[1,3]{1,0:T(1,128)S(1)} %add_bitcast_fusion.place_ref.refs_0_, f32[8,1024]{1,0:T(8,128)S(1)} %get-tuple-element.10.own_ref.refs_3_, f32[64,8,128]{2,1,0:T(8,128)S(1)} %all_to_all.15.rows_ref.refs_4_), custom_call_target="tpu_custom_call" | custom-call | flops 4194304 | bytes 1048576 | tf_op jit(solution)/shard_map/features/pallas_call | solution.py:91
  52.9 5.2 %all-to-all-done.1.held_ref = s32[16,1,128]{2,1,0:T(1,128)S(1)} async-done(((s32[16,1,128]{2,1,0:T(1,128)}), s32[16,1,128]{2,1,0:T(1,128)S(1)}, u32[]{:S(2)}, u32[]{:S(2)}) %all-to-all-start.1) | async-done | bytes 8224 | tf_op jit(solution)/shard_map/all_to_all | solution.py:379
  58.1 1.0 %tally.1.refs_1_ = s32[4,256]{1,0:T(4,128)S(1)} custom-call(s32[1,3]{1,0:T(1,128)S(1)} %add_bitcast_fusion.place_ref.refs_0_, s32[16,1,128]{2,1,0:T(1,128)S(1)} %all-to-all-done.1.held_ref), custom_call_target="tpu_custom_call" | custom-call | tf_op jit(solution)/shard_map/tally/pallas_call | solution.py:136
  59.1 5.1 %outer_block.1 = (f32[8,256]{1,0:T(8,128)S(1)}, f32[1,512]{1,0:T(1,128)S(1)}) custom-call(s32[1,3]{1,0:T(1,128)S(1)} %add_bitcast_fusion.place_ref.refs_0_, s32[4,256]{1,0:T(4,128)S(1)} %tally.1.refs_1_, f32[1,1]{1,0:T(1,128)} %bitcast.8.refs_2_, f32[8,1024]{1,0:T(8,128)S(1)} %get-tuple-element.10.own_ref.refs_3_, ...), custom_call_target="tpu_custom_call" | custom-call | flops 688128000 | bytes 2097152 | tf_op jit(solution)/shard_map/outer_block/pallas_call | solution.py:290
  64.2 3.4 %collective-permute-start = (f32[1,512]{1,0:T(1,128)S(1)}, f32[1,512]{1,0:T(1,128)S(1)}, u32[]{:S(2)}, u32[]{:S(2)}) collective-permute-start(f32[1,512]{1,0:T(1,128)S(1)} %get-tuple-element.15), channel_id=1, source_target_pairs={{0,16},{1,1009},{2,18},{3,1011},{4,20},{5,1013},{6,22},{7,1015},{8... | collective-permute-start | bytes 6152 | tf_op jit(solution)/shard_map/ppermute | solution.py:396
  67.6 0.0 copy-start.4
  67.6 6.4 %inner_block.1 = f32[8,256]{1,0:T(8,128)S(1)} custom-call(s32[1,3]{1,0:T(1,128)S(1)} %add_bitcast_fusion.place_ref.refs_0_, s32[4,256]{1,0:T(4,128)S(1)} %tally.1.refs_1_, f32[1,1]{1,0:T(1,128)} %bitcast.9.refs_2_, f32[8,1024]{1,0:T(8,128)S(1)} %get-tuple-element.10.own_ref.refs_3_, f32[64,8,128]{2,1,0:T(8,128)S(1)} %all_to_all.15.rows_ref.refs_4_, ...), custom_call_target="tpu_custom_call" | custom-call | flops 688128000 | bytes 2097152 | tf_op jit(solution)/shard_map/inner_block/pallas_call | solution.py:290
  74.1 0.7 broadcast_in_dim.2
  74.8 4.9 %all-to-all-start.2 = ((f32[16,8,512]{2,1,0:T(8,128)}), f32[16,8,512]{2,1,0:T(8,128)S(1)}, u32[]{:S(2)}, u32[]{:S(2)}) async-start(f32[16,8,512]{2,1,0:T(8,128)} %broadcast_in_dim.2), calls=%async_computation.2 | async-start | bytes 524288 | tf_op jit(solution)/shard_map/all_to_all | solution.py:399
  79.7 0.1 slice.13
  79.8 0.1 fusion.1
  79.8 0.1 concatenate.11.corner_ref
  79.9 0.8 incidence.1.table_ref
  80.7 10.8 %all-to-all-done.2.parts_ref = f32[16,8,512]{2,1,0:T(8,128)S(1)} async-done(((f32[16,8,512]{2,1,0:T(8,128)}), f32[16,8,512]{2,1,0:T(8,128)S(1)}, u32[]{:S(2)}, u32[]{:S(2)}) %all-to-all-start.2) | async-done | bytes 262176 | tf_op jit(solution)/shard_map/all_to_all | solution.py:399
  91.6 1.6 %finish.1 = (f32[3,512]{1,0:T(4,128)}, f32[4,1024]{1,0:T(4,128)}) custom-call(f32[16,8,512]{2,1,0:T(8,128)S(1)} %all-to-all-done.2.parts_ref, bf16[512,1152]{1,0:T(8,128)(2,1)S(1)} %incidence.1.table_ref), custom_call_target="tpu_custom_call" | custom-call | tf_op jit(solution)/shard_map/finish/pallas_call | solution.py:356
  (7 shorter events, 0.0 us)
Async XLA Ops:
  0.7 0.7 copy-start
  1.5 0.7 copy-start.1
  2.2 0.7 copy-start.2
  2.9 0.7 copy-start.3
  40.4 17.7 %all-to-all-start.1 = ((s32[16,1,128]{2,1,0:T(1,128)}), s32[16,1,128]{2,1,0:T(1,128)S(1)}, u32[]{:S(2)}, u32[]{:S(2)}) async-start(s32[16,1,128]{2,1,0:T(1,128)} %pack_codes.1), calls=%async_computation.1 | async-start | bytes 16384 | tf_op jit(solution)/shard_map/all_to_all | solution.py:379
  64.2 9.8 %collective-permute-start = (f32[1,512]{1,0:T(1,128)S(1)}, f32[1,512]{1,0:T(1,128)S(1)}, u32[]{:S(2)}, u32[]{:S(2)}) collective-permute-start(f32[1,512]{1,0:T(1,128)S(1)} %get-tuple-element.15), channel_id=1, source_target_pairs={{0,16},{1,1009},{2,18},{3,1011},{4,20},{5,1013},{6,22},{7,1015},{8... | collective-permute-start | bytes 6152 | tf_op jit(solution)/shard_map/ppermute | solution.py:396
  67.6 12.1 %copy-start.4 = (s32[3,1152]{1,0:T(4,128)S(1)}, s32[3,1152]{1,0:T(4,128)}, u32[]{:S(2)}) copy-start(s32[3,1152]{1,0:T(4,128)} %param.11) | copy-start | bytes 41476
  74.8 16.8 %all-to-all-start.2 = ((f32[16,8,512]{2,1,0:T(8,128)}), f32[16,8,512]{2,1,0:T(8,128)S(1)}, u32[]{:S(2)}, u32[]{:S(2)}) async-start(f32[16,8,512]{2,1,0:T(8,128)} %broadcast_in_dim.2), calls=%async_computation.2 | async-start | bytes 524288 | tf_op jit(solution)/shard_map/all_to_all | solution.py:399

commit v7 on v6

--- a/solution.py
+++ b/solution.py
@@ -161,7 +161,7 @@
         out_shape=(jax.ShapeDtypeStruct((8, faces), F32), jax.ShapeDtypeStruct((count, 8, SLICE), F32)),
         in_specs=[SMEM, SMEM, VMEM, VMEM, VMEM],
         out_specs=(VMEM, VMEM),
-        compiler_params=pltpu.CompilerParams(vmem_limit_bytes=16 * 1024 * 1024),
+        compiler_params=pltpu.CompilerParams(vmem_limit_bytes=60 * 1024 * 1024),
         name="prepare",
     )(place, codes, centroids, normals, areas)
 
@@ -344,11 +344,11 @@
     edges = low[7:8] + high[7:8]
     edge = jnp.concatenate([edges[:, c * width : (c + 1) * width] for c in range(3)], axis=0)
     contract = (((1,), (1,)), ((), ()))
-    out = jnp.zeros((3, vertex_ref.shape[1]), F32)
-    for main, side in zip(thirds(total[0:3]), thirds(edge)):
-        out = out + lax.dot_general(main.astype(BF16), table_ref[:, 0:faces], contract, preferred_element_type=F32)
-        out = out + lax.dot_general(side.astype(BF16), table_ref[:, faces:], contract, preferred_element_type=F32)
-    vertex_ref[...] = out / 3.0
+    main = jnp.concatenate(thirds(total[0:3]), axis=0).astype(BF16)
+    side = jnp.concatenate(thirds(edge), axis=0).astype(BF16)
+    out = lax.dot_general(main, table_ref[:, 0:faces], contract, preferred_element_type=F32)
+    out = out + lax.dot_general(side, table_ref[:, faces:], contract, preferred_element_type=F32)
+    vertex_ref[...] = (out[0:3] + out[3:6] + out[6:9]) / 3.0
 
 
 def finish(parts, table):
@@ -396,7 +396,7 @@
     halo = lax.ppermute(edge, ("blk", "pair"), hops)
     inner = pair_call(inner_kernel, block, operands, "inner_block")
     part = jnp.concatenate([jnp.concatenate([outer, inner], axis=1)[:7], halo], axis=0)
-    parts = lax.all_to_all(jnp.broadcast_to(part[None], (shares, *part.shape)), "pair", 0, 0)
+    parts = lax.all_gather(part, "pair")
     return finish(parts, table)
 
 

time: 94.1 us -> 93.1 us (0.989)
  blocking collectives: 35.6 us -> 52.3 us
  waiting for transfers between devices: 16.1 us -> 2.78 us
  starting transfers between devices: 19 us -> 12.7 us
  Pallas kernels: 17.2 us -> 20.5 us
  local copies, waits for them, and re-layouts: 3.75 us -> 2.32 us
    all_gather x0 -> x1, blocking collectives: none -> 16.4 us  [shards(): parts = lax.all_gather(part, 'pair')]
    all_to_all x1 -> x0, waiting for transfers between devices: 10.8 us -> none  [shards(): lax.all_to_all(jnp.broadcast_to(part[None], (shares, *part.shape)), 'pair...]
    all_to_all x1 -> x0, starting transfers between devices: 4.89 us -> none  [shards(): lax.all_to_all(jnp.broadcast_to(part[None], (shares, *part.shape)), 'pair...]
    pallas_call x2, Pallas kernels: 11.5 us -> 14.4 us  [pair_call(): pl.pallas_call(body, out_shape=outputs, in_specs=in_specs, out_specs=jax....]
    all_to_all x1, waiting for transfers between devices: 5.23 us -> 2.78 us  [shards(): held = lax.all_to_all(pack_codes(codes, rows, shares), 'pair', 0, 0)]
    unnamed x10 -> x6, local copies, waits for them, and re-layouts: 2.78 us -> 0.66 us
    ppermute x1, starting transfers between devices: 3.35 us -> 1.92 us  [shards(): halo = lax.ppermute(edge, ('blk', 'pair'), hops)]
    pallas_call x1, Pallas kernels: 0.59 us -> 1.56 us  [prepare(): pl.pallas_call(prepare_kernel, out_shape=(jax.ShapeDtypeStruct((8, faces)...]
  transfers between devices with their start and end apart: 3 -> 2, of which waited for: 2 -> 1; matrix products, arithmetic and copies ran while one was open for 0% -> 2% of each run, Pallas kernels for 9% -> 9%
where the time goes in v7:
time: 93.1 us; the launch traced here: 92.7 us
  blocking collectives  52.3 us (56%)
  Pallas kernels  20.5 us (22%)
  starting transfers between devices  12.7 us (14%)
  waiting for transfers between devices  2.78 us (3%)
  local copies, waits for them, and re-layouts  2.32 us (2%)
  between operations  1.39 us (1%)
    all_to_all x1, blocking collectives, shards(): rows = lax.all_to_all(chunks, 'blk', 0, 0)  35.9 us
    all_gather x1, blocking collectives, shards(): parts = lax.all_gather(part, 'pair')  16.4 us
    pallas_call x2, Pallas kernels, pair_call(): pl.pallas_call(body, out_shape=outputs, in_specs=in_specs, out_specs=jax....  14.4 us
    all_to_all x1, starting transfers between devices, shards(): held = lax.all_to_all(pack_codes(codes, rows, shares), 'pair', 0, 0)  10.8 us
    all_to_all x1, waiting for transfers between devices, shards(): held = lax.all_to_all(pack_codes(codes, rows, shares), 'pair', 0, 0)  2.78 us
    ppermute x1, starting transfers between devices, shards(): halo = lax.ppermute(edge, ('blk', 'pair'), hops)  1.92 us
  transfers between devices with their start and end apart: 2, of which 1 were waited for; matrix products, arithmetic and copies ran while one was open for 2% of the time, Pallas kernels for 9%

profile of v7, /device:TPU:1, one launch (start us, length us, event | category | flops | bytes accessed | tf_op | source)
XLA Modules:
  0.0 92.7 jit_solution(5921850548756353940)
XLA Ops:
  0.7 0.7 add_bitcast_fusion.place_ref.refs_0_
  1.3 0.0 copy-start.1
  1.3 1.6 %prepare.1 = (f32[8,1024]{1,0:T(8,128)}, f32[64,8,128]{2,1,0:T(8,128)}) custom-call(s32[1,3]{1,0:T(1,128)} %add_bitcast_fusion.place_ref.refs_0_, s32[1,64]{1,0:T(1,128)} %bitcast.12, f32[3,1024]{1,0:T(4,128)} %center_ref.1, f32[3,1024]{1,0:T(4,128)} %normal_ref.1, f32[1,1024]{1,0:T(1,128)} %bitcast.14), custom_call_target="tpu_custom_call" | custom-call | tf_op jit(solution)/shard_map/prepare/pallas_call | solution.py:159
  2.9 0.0 copy-start
  2.9 35.9 %all_to_all.10.rows_ref.refs_4_ = f32[64,8,128]{2,1,0:T(8,128)S(1)} all-to-all(f32[64,8,128]{2,1,0:T(8,128)} %get-tuple-element.9), channel_id=1, replica_groups=mesh['blk'=64,'pair'=16] {'blk'}, dimensions={0} | all-to-all | bytes 524288 | tf_op jit(solution)/shard_map/all_to_all | solution.py:377
  38.8 0.0 copy-start.2
  38.8 0.7 copy-done.2
  39.5 0.7 pack_codes.1
  40.2 10.8 %all-to-all-start.1 = ((s32[16,1,128]{2,1,0:T(1,128)}), s32[16,1,128]{2,1,0:T(1,128)S(1)}, u32[]{:S(2)}, u32[]{:S(2)}) async-start(s32[16,1,128]{2,1,0:T(1,128)} %pack_codes.1), calls=%async_computation.1 | async-start | bytes 16384 | tf_op jit(solution)/shard_map/all_to_all | solution.py:379
  51.0 0.8 fusion.1
  51.7 0.8 slice.13
  53.2 0.1 concatenate.11.corner_ref
  53.3 0.8 incidence.1.table_ref
  54.0 0.0 copy-done.1
  54.0 0.0 copy-done
  54.1 1.1 %features.1 = (bf16[64,64,128]{2,1,0:T(8,128)(2,1)S(1)}, bf16[64,32,128]{2,1,0:T(8,128)(2,1)S(1)}, bf16[2,3,64,256]{3,2,1,0:T(8,128)(2,1)S(1)}) custom-call(s32[1,3]{1,0:T(1,128)S(1)} %copy-done.1, f32[8,1024]{1,0:T(8,128)S(1)} %copy-done, f32[64,8,128]{2,1,0:T(8,128)S(1)} %all_to_all.10.rows_ref.refs_4_), custom_call_target="tpu_custom_call" | custom-call | flops 4194304 | bytes 1048576 | tf_op jit(solution)/shard_map/features/pallas_call | solution.py:91
  55.1 2.8 %all-to-all-done.1.held_ref = s32[16,1,128]{2,1,0:T(1,128)S(1)} async-done(((s32[16,1,128]{2,1,0:T(1,128)}), s32[16,1,128]{2,1,0:T(1,128)S(1)}, u32[]{:S(2)}, u32[]{:S(2)}) %all-to-all-start.1) | async-done | bytes 8224 | tf_op jit(solution)/shard_map/all_to_all | solution.py:379
  57.9 1.0 %tally.1.refs_1_ = s32[4,256]{1,0:T(4,128)S(1)} custom-call(s32[1,3]{1,0:T(1,128)S(1)} %copy-done.1, s32[16,1,128]{2,1,0:T(1,128)S(1)} %all-to-all-done.1.held_ref), custom_call_target="tpu_custom_call" | custom-call | tf_op jit(solution)/shard_map/tally/pallas_call | solution.py:136
  58.9 7.5 %outer_block.1 = (f32[8,256]{1,0:T(8,128)S(1)}, f32[1,512]{1,0:T(1,128)S(1)}) custom-call(s32[1,3]{1,0:T(1,128)S(1)} %copy-done.1, s32[4,256]{1,0:T(4,128)S(1)} %tally.1.refs_1_, f32[1,1]{1,0:T(1,128)} %bitcast.9.refs_2_, f32[8,1024]{1,0:T(8,128)S(1)} %copy-done, f32[64,8,128]{2,1,0:T(8,128)S(1)} %all_to_all.10.rows_ref.refs_4_, ...), custom_call_target="tpu_custom_call" | custom-call | flops 688128000 | bytes 2097152 | tf_op jit(solution)/shard_map/outer_block/pallas_call | solution.py:290
  66.4 1.9 %collective-permute-start = (f32[1,512]{1,0:T(1,128)S(1)}, f32[1,512]{1,0:T(1,128)S(1)}, u32[]{:S(2)}, u32[]{:S(2)}) collective-permute-start(f32[1,512]{1,0:T(1,128)S(1)} %get-tuple-element.15), channel_id=1, source_target_pairs={{0,16},{1,1009},{2,18},{3,1011},{4,20},{5,1013},{6,22},{7,1015},{8... | collective-permute-start | bytes 6152 | tf_op jit(solution)/shard_map/ppermute | solution.py:396
  68.3 6.9 %inner_block.1 = f32[8,256]{1,0:T(8,128)S(1)} custom-call(s32[1,3]{1,0:T(1,128)S(1)} %copy-done.1, s32[4,256]{1,0:T(4,128)S(1)} %tally.1.refs_1_, f32[1,1]{1,0:T(1,128)} %bitcast.10.refs_2_, f32[8,1024]{1,0:T(8,128)S(1)} %copy-done, f32[64,8,128]{2,1,0:T(8,128)S(1)} %all_to_all.10.rows_ref.refs_4_, bf16[64,64,128]{2,1,0:T(8,128)(2,1)S(1)} %get-tuple-element.11.refs_5_, ...), custom_call_target="tpu_custom_call" | custom-call | flops 688128000 | bytes 2097152 | tf_op jit(solution)/shard_map/inner_block/pallas_call | solution.py:290
  75.2 0.0 collective-permute-done
  75.3 16.4 %all-gather = f32[128,512]{1,0:T(8,128)S(1)} all-gather(f32[8,512]{1,0:T(8,128)S(1)} %fusion), channel_id=2, replica_groups=mesh['blk'=64,'pair'=16] {'pair'}, dimensions={0}, use_global_device_ids=true | all-gather | bytes 278528 | tf_op jit(solution)/shard_map/all_gather | solution.py:399
  91.6 1.0 %finish.1 = (f32[3,512]{1,0:T(4,128)}, f32[4,1024]{1,0:T(4,128)}) custom-call(f32[16,8,512]{2,1,0:T(8,128)S(1)} %bitcast.11, bf16[512,1152]{1,0:T(8,128)(2,1)S(1)} %incidence.1.table_ref), custom_call_target="tpu_custom_call" | custom-call | tf_op jit(solution)/shard_map/finish/pallas_call | solution.py:356
  (1 shorter events, 0.0 us)
Async XLA Ops:
  1.3 52.7 %copy-start.1 = (s32[1,3]{1,0:T(1,128)S(1)}, s32[1,3]{1,0:T(1,128)}, u32[]{:S(2)}) copy-start(s32[1,3]{1,0:T(1,128)} %add_bitcast_fusion.place_ref.refs_0_) | copy-start | bytes 40
  2.9 51.2 %copy-start = (f32[8,1024]{1,0:T(8,128)S(1)}, f32[8,1024]{1,0:T(8,128)}, u32[]{:S(2)}) copy-start(f32[8,1024]{1,0:T(8,128)} %get-tuple-element.10.own_ref.refs_3_) | copy-start | bytes 98308
  38.8 0.7 copy-start.2
  40.2 17.7 %all-to-all-start.1 = ((s32[16,1,128]{2,1,0:T(1,128)}), s32[16,1,128]{2,1,0:T(1,128)S(1)}, u32[]{:S(2)}, u32[]{:S(2)}) async-start(s32[16,1,128]{2,1,0:T(1,128)} %pack_codes.1), calls=%async_computation.1 | async-start | bytes 16384 | tf_op jit(solution)/shard_map/all_to_all | solution.py:379
  66.4 8.9 %collective-permute-start = (f32[1,512]{1,0:T(1,128)S(1)}, f32[1,512]{1,0:T(1,128)S(1)}, u32[]{:S(2)}, u32[]{:S(2)}) collective-permute-start(f32[1,512]{1,0:T(1,128)S(1)} %get-tuple-element.15), channel_id=1, source_target_pairs={{0,16},{1,1009},{2,18},{3,1011},{4,20},{5,1013},{6,22},{7,1015},{8... | collective-permute-start | bytes 6152 | tf_op jit(solution)/shard_map/ppermute | solution.py:396

commit v8 on v7

--- a/solution.py
+++ b/solution.py
@@ -143,11 +143,12 @@
     )(place, held)
 
 
-def prepare_kernel(place_ref, code_ref, center_ref, normal_ref, area_ref, own_ref, chunk_ref):
+def prepare_kernel(place_ref, code_ref, center_ref, normal_ref, area_ref, row_ref, own_ref, chunk_ref):
     own_ref[0:3, :] = center_ref[...]
     own_ref[3:6, :] = normal_ref[...]
     own_ref[6:7, :] = area_ref[...]
     own_ref[7:8, :] = jnp.zeros_like(area_ref)
+    own_ref[7:8, : row_ref.shape[1]] = row_ref[...].astype(F32)
     piece = own_ref[:, pl.ds(pl.multiple_of(place_ref[0, 2] * SLICE, SLICE), SLICE)]
     last = lax.broadcasted_iota(jnp.int32, piece.shape, 0) == 7
     for b in range(chunk_ref.shape[0]):
@@ -159,31 +160,31 @@
     return pl.pallas_call(
         prepare_kernel,
         out_shape=(jax.ShapeDtypeStruct((8, faces), F32), jax.ShapeDtypeStruct((count, 8, SLICE), F32)),
-        in_specs=[SMEM, SMEM, VMEM, VMEM, VMEM],
+        in_specs=[SMEM, SMEM, VMEM, VMEM, VMEM, VMEM],
         out_specs=(VMEM, VMEM),
         compiler_params=pltpu.CompilerParams(vmem_limit_bytes=60 * 1024 * 1024),
         name="prepare",
-    )(place, codes, centroids, normals, areas)
-
-
-def pack_kernel(code_ref, rows_ref, out_ref):
+    )(place, codes, centroids, normals, areas, codes)
+
+
+def pack_kernel(own_ref, rows_ref, out_ref):
     values = rows_ref[:, 7, :]
     count = values.shape[0]
     lane, row = (lax.broadcasted_iota(jnp.int32, values.shape, i) for i in (1, 0))
     incoming = jnp.sum(jnp.where(lane == row, values, 0.0), axis=0, keepdims=True)
-    both_ways = jnp.concatenate([incoming[:, :count], code_ref[...].astype(F32)], axis=1).astype(jnp.int32)
+    both_ways = jnp.concatenate([incoming[:, :count], own_ref[7:8, :count]], axis=1).astype(jnp.int32)
     out_ref[...] = jnp.broadcast_to(both_ways[None], out_ref.shape)
 
 
-def pack_codes(codes, rows, shares):
+def pack_codes(own, rows, shares):
     return pl.pallas_call(
         pack_kernel,
-        out_shape=jax.ShapeDtypeStruct((shares, 1, 2 * codes.shape[1]), jnp.int32),
+        out_shape=jax.ShapeDtypeStruct((shares, 1, 2 * rows.shape[0]), jnp.int32),
         in_specs=[VMEM, VMEM],
         out_specs=VMEM,
         compiler_params=pltpu.CompilerParams(vmem_limit_bytes=16 * 1024 * 1024),
         name="pack_codes",
-    )(codes, rows)
+    )(own, rows)
 
 
 class Steps:
@@ -309,10 +310,13 @@
 def incidence_kernel(corner_ref, out_ref):
     verts, faces = out_ref.shape
     vertex = lax.broadcasted_iota(jnp.int32, (verts, 128), 0)
+    window = corner_ref[...]
+    inside, ends = window[:, HALO_FACES:-HALO_FACES], (window[:, :HALO_FACES], window[:, -HALO_FACES:])
+    corner = jnp.concatenate([inside, *ends], axis=1)
     for e in range(0, faces, 128):
         total = jnp.zeros((verts, 128), F32)
         for k in range(3):
-            total = total + jnp.where(corner_ref[k : k + 1, e : e + 128] == vertex, 1.0, 0.0)
+            total = total + jnp.where(corner[k : k + 1, e : e + 128] == vertex, 1.0, 0.0)
         out_ref[:, e : e + 128] = total.astype(BF16)
 
 
@@ -376,13 +380,10 @@
     own, chunks = prepare(place, codes, centroids, normals, areas.reshape(1, faces))
     rows = lax.all_to_all(chunks, "blk", 0, 0)
 
-    held = lax.all_to_all(pack_codes(codes, rows, shares), "pair", 0, 0)
+    held = lax.all_to_all(pack_codes(own, rows, shares), "pair", 0, 0)
     counts = tally(place, held)
     scale = cotangent.reshape(1, 1)
-    corner = jnp.concatenate(
-        [corner_vertex[:, HALO_FACES:-HALO_FACES], corner_vertex[:, :HALO_FACES], corner_vertex[:, -HALO_FACES:]], axis=1
-    )
-    table = incidence_table(corner, faces // 2)
+    table = incidence_table(corner_vertex, faces // 2)
 
     block = jax.ShapeDtypeStruct((8, BLOCK), F32)
     edge_row = jax.ShapeDtypeStruct((1, 2 * BLOCK), F32)

time: 93.1 us -> 93.3 us (level)
  starting transfers between devices: 12.7 us -> 15.6 us
  Pallas kernels: 20.5 us -> 18.9 us
    ppermute x1, starting transfers between devices: 1.92 us -> 4.82 us  [shards(): halo = lax.ppermute(edge, ('blk', 'pair'), hops)]
    pallas_call x2, Pallas kernels: 14.4 us -> 12 us  [pair_call(): pl.pallas_call(body, out_shape=outputs, in_specs=in_specs, out_specs=jax....]
    slice x2 -> x0, local copies, waits for them, and re-layouts: 1.56 us -> none  [the longest x1 0.79 us: shards(): corner_vertex[:, HALO_FACES:-HALO_FACES]]
  transfers between devices with their start and end apart: 2 -> 2, of which waited for: 1 -> 1; matrix products, arithmetic and copies ran while one was open for 2% -> 0% of each run, Pallas kernels for 9% -> 10%
where the time goes in v8:
time: 93.3 us; the launch traced here: 92.8 us
  blocking collectives  51.8 us (56%)
  Pallas kernels  18.9 us (20%)
  starting transfers between devices  15.6 us (17%)
  waiting for transfers between devices  2.9 us (3%)
  local copies, waits for them, and re-layouts  1.48 us (2%)
  between operations  1.4 us (2%)
    all_to_all x1, blocking collectives, shards(): rows = lax.all_to_all(chunks, 'blk', 0, 0)  35.9 us
    all_gather x1, blocking collectives, shards(): parts = lax.all_gather(part, 'pair')  15.9 us
    pallas_call x2, Pallas kernels, pair_call(): pl.pallas_call(body, out_shape=outputs, in_specs=in_specs, out_specs=jax....  12 us
    all_to_all x1, starting transfers between devices, shards(): held = lax.all_to_all(pack_codes(own, rows, shares), 'pair', 0, 0)  10.8 us
    ppermute x1, starting transfers between devices, shards(): halo = lax.ppermute(edge, ('blk', 'pair'), hops)  4.82 us
    all_to_all x1, waiting for transfers between devices, shards(): held = lax.all_to_all(pack_codes(own, rows, shares), 'pair', 0, 0)  2.89 us
  transfers between devices with their start and end apart: 2, of which 1 were waited for; matrix products, arithmetic and copies ran while one was open for 0% of the time, Pallas kernels for 10%

profile of v8, /device:TPU:1, one launch (start us, length us, event | category | flops | bytes accessed | tf_op | source)
XLA Modules:
  0.0 92.8 jit_solution(12094667396732953420)
XLA Ops:
  0.7 0.7 add_bitcast_fusion.place_ref.refs_0_
  1.3 0.0 copy-start.3
  1.3 1.6 %prepare.1 = (f32[8,1024]{1,0:T(8,128)}, f32[64,8,128]{2,1,0:T(8,128)}) custom-call(s32[1,3]{1,0:T(1,128)} %add_bitcast_fusion.place_ref.refs_0_, s32[1,64]{1,0:T(1,128)} %bitcast.13, f32[3,1024]{1,0:T(4,128)} %center_ref.1, f32[3,1024]{1,0:T(4,128)} %normal_ref.1, f32[1,1024]{1,0:T(1,128)} %bitcast.12, s32[1,64]{1,0:T(1,128)} %bitcast.14), custom_call_target="tpu_custom_call" | custom-call | tf_op jit(solution)/shard_map/prepare/pallas_call | solution.py:160
  2.9 0.0 copy-start.1
  2.9 35.9 %all_to_all.10.rows_ref.refs_4_ = f32[64,8,128]{2,1,0:T(8,128)S(1)} all-to-all(f32[64,8,128]{2,1,0:T(8,128)} %get-tuple-element.10), channel_id=1, replica_groups=mesh['blk'=64,'pair'=16] {'blk'}, dimensions={0} | all-to-all | bytes 524288 | tf_op jit(solution)/shard_map/all_to_all | solution.py:381
  38.8 0.0 copy-start
  38.8 0.8 copy-done
  39.6 0.7 pack_codes.1
  40.3 10.8 %all-to-all-start.1 = ((s32[16,1,128]{2,1,0:T(1,128)}), s32[16,1,128]{2,1,0:T(1,128)S(1)}, u32[]{:S(2)}, u32[]{:S(2)}) async-start(s32[16,1,128]{2,1,0:T(1,128)} %pack_codes.1), calls=%async_computation.1 | async-start | bytes 16384 | tf_op jit(solution)/shard_map/all_to_all | solution.py:383
  51.7 0.0 copy-start.2
  51.7 0.7 copy-done.2
  52.4 1.6 %incidence.1.table_ref = bf16[512,1152]{1,0:T(8,128)(2,1)S(1)} custom-call(s32[3,1152]{1,0:T(4,128)S(1)} %copy-done.2), custom_call_target="tpu_custom_call" | custom-call | flops 5308416 | bytes 1179648 | tf_op jit(solution)/shard_map/incidence/pallas_call | solution.py:325
  54.0 0.0 copy-done.3
  54.0 0.0 copy-done.1
  54.0 1.1 %features.1 = (bf16[64,64,128]{2,1,0:T(8,128)(2,1)S(1)}, bf16[64,32,128]{2,1,0:T(8,128)(2,1)S(1)}, bf16[2,3,64,256]{3,2,1,0:T(8,128)(2,1)S(1)}) custom-call(s32[1,3]{1,0:T(1,128)S(1)} %copy-done.3, f32[8,1024]{1,0:T(8,128)S(1)} %copy-done.1, f32[64,8,128]{2,1,0:T(8,128)S(1)} %all_to_all.10.rows_ref.refs_4_), custom_call_target="tpu_custom_call" | custom-call | flops 4194304 | bytes 1048576 | tf_op jit(solution)/shard_map/features/pallas_call | solution.py:91
  55.1 2.9 %all-to-all-done.1.held_ref = s32[16,1,128]{2,1,0:T(1,128)S(1)} async-done(((s32[16,1,128]{2,1,0:T(1,128)}), s32[16,1,128]{2,1,0:T(1,128)S(1)}, u32[]{:S(2)}, u32[]{:S(2)}) %all-to-all-start.1) | async-done | bytes 8224 | tf_op jit(solution)/shard_map/all_to_all | solution.py:383
  58.0 1.0 %tally.1.refs_1_ = s32[4,256]{1,0:T(4,128)S(1)} custom-call(s32[1,3]{1,0:T(1,128)S(1)} %copy-done.3, s32[16,1,128]{2,1,0:T(1,128)S(1)} %all-to-all-done.1.held_ref), custom_call_target="tpu_custom_call" | custom-call | tf_op jit(solution)/shard_map/tally/pallas_call | solution.py:136
  59.0 5.1 %outer_block.1 = (f32[8,256]{1,0:T(8,128)S(1)}, f32[1,512]{1,0:T(1,128)S(1)}) custom-call(s32[1,3]{1,0:T(1,128)S(1)} %copy-done.3, s32[4,256]{1,0:T(4,128)S(1)} %tally.1.refs_1_, f32[1,1]{1,0:T(1,128)} %bitcast.9.refs_2_, f32[8,1024]{1,0:T(8,128)S(1)} %copy-done.1, f32[64,8,128]{2,1,0:T(8,128)S(1)} %all_to_all.10.rows_ref.refs_4_, ...), custom_call_target="tpu_custom_call" | custom-call | flops 688128000 | bytes 2097152 | tf_op jit(solution)/shard_map/outer_block/pallas_call | solution.py:291
  64.1 4.8 %collective-permute-start = (f32[1,512]{1,0:T(1,128)S(1)}, f32[1,512]{1,0:T(1,128)S(1)}, u32[]{:S(2)}, u32[]{:S(2)}) collective-permute-start(f32[1,512]{1,0:T(1,128)S(1)} %get-tuple-element.15), channel_id=1, source_target_pairs={{0,16},{1,1009},{2,18},{3,1011},{4,20},{5,1013},{6,22},{7,1015},{8... | collective-permute-start | bytes 6152 | tf_op jit(solution)/shard_map/ppermute | solution.py:397
  68.9 6.9 %inner_block.1 = f32[8,256]{1,0:T(8,128)S(1)} custom-call(s32[1,3]{1,0:T(1,128)S(1)} %copy-done.3, s32[4,256]{1,0:T(4,128)S(1)} %tally.1.refs_1_, f32[1,1]{1,0:T(1,128)} %bitcast.10.refs_2_, f32[8,1024]{1,0:T(8,128)S(1)} %copy-done.1, f32[64,8,128]{2,1,0:T(8,128)S(1)} %all_to_all.10.rows_ref.refs_4_, bf16[64,64,128]{2,1,0:T(8,128)(2,1)S(1)} %get-tuple-element.11.refs_5_, ...), custom_call_target="tpu_custom_call" | custom-call | flops 688128000 | bytes 2097152 | tf_op jit(solution)/shard_map/inner_block/pallas_call | solution.py:291
  75.8 0.0 collective-permute-done
  75.9 15.9 %all-gather = f32[128,512]{1,0:T(8,128)S(1)} all-gather(f32[8,512]{1,0:T(8,128)S(1)} %fusion), channel_id=2, replica_groups=mesh['blk'=64,'pair'=16] {'pair'}, dimensions={0}, use_global_device_ids=true | all-gather | bytes 278528 | tf_op jit(solution)/shard_map/all_gather | solution.py:400
  91.8 1.0 %finish.1 = (f32[3,512]{1,0:T(4,128)}, f32[4,1024]{1,0:T(4,128)}) custom-call(f32[16,8,512]{2,1,0:T(8,128)S(1)} %bitcast.11, bf16[512,1152]{1,0:T(8,128)(2,1)S(1)} %incidence.1.table_ref), custom_call_target="tpu_custom_call" | custom-call | tf_op jit(solution)/shard_map/finish/pallas_call | solution.py:360
  (1 shorter events, 0.0 us)
Async XLA Ops:
  1.3 52.7 %copy-start.3 = (s32[1,3]{1,0:T(1,128)S(1)}, s32[1,3]{1,0:T(1,128)}, u32[]{:S(2)}) copy-start(s32[1,3]{1,0:T(1,128)} %add_bitcast_fusion.place_ref.refs_0_) | copy-start | bytes 40
  2.9 51.1 %copy-start.1 = (f32[8,1024]{1,0:T(8,128)S(1)}, f32[8,1024]{1,0:T(8,128)}, u32[]{:S(2)}) copy-start(f32[8,1024]{1,0:T(8,128)} %get-tuple-element.9.own_ref.refs_3_) | copy-start | bytes 98308
  38.8 0.8 copy-start
  40.3 17.7 %all-to-all-start.1 = ((s32[16,1,128]{2,1,0:T(1,128)}), s32[16,1,128]{2,1,0:T(1,128)S(1)}, u32[]{:S(2)}, u32[]{:S(2)}) async-start(s32[16,1,128]{2,1,0:T(1,128)} %pack_codes.1), calls=%async_computation.1 | async-start | bytes 16384 | tf_op jit(solution)/shard_map/all_to_all | solution.py:383
  51.7 0.7 copy-start.2
  64.1 11.8 %collective-permute-start = (f32[1,512]{1,0:T(1,128)S(1)}, f32[1,512]{1,0:T(1,128)S(1)}, u32[]{:S(2)}, u32[]{:S(2)}) collective-permute-start(f32[1,512]{1,0:T(1,128)S(1)} %get-tuple-element.15), channel_id=1, source_target_pairs={{0,16},{1,1009},{2,18},{3,1011},{4,20},{5,1013},{6,22},{7,1015},{8... | collective-permute-start | bytes 6152 | tf_op jit(solution)/shard_map/ppermute | solution.py:397

commit v9 on v8

--- a/solution.py
+++ b/solution.py
@@ -143,28 +143,28 @@
     )(place, held)
 
 
-def prepare_kernel(place_ref, code_ref, center_ref, normal_ref, area_ref, row_ref, own_ref, chunk_ref):
+def prepare_kernel(code_ref, center_ref, normal_ref, area_ref, row_ref, own_ref, chunk_ref):
     own_ref[0:3, :] = center_ref[...]
     own_ref[3:6, :] = normal_ref[...]
     own_ref[6:7, :] = area_ref[...]
     own_ref[7:8, :] = jnp.zeros_like(area_ref)
     own_ref[7:8, : row_ref.shape[1]] = row_ref[...].astype(F32)
-    piece = own_ref[:, pl.ds(pl.multiple_of(place_ref[0, 2] * SLICE, SLICE), SLICE)]
+    piece = own_ref[:, pl.ds(pl.multiple_of(lax.axis_index("pair") // 2 * SLICE, SLICE), SLICE)]
     last = lax.broadcasted_iota(jnp.int32, piece.shape, 0) == 7
     for b in range(chunk_ref.shape[0]):
         chunk_ref[b] = jnp.where(last, code_ref[0, b].astype(F32), piece)
 
 
-def prepare(place, codes, centroids, normals, areas):
+def prepare(codes, centroids, normals, areas):
     count, faces = codes.shape[1], centroids.shape[1]
     return pl.pallas_call(
         prepare_kernel,
         out_shape=(jax.ShapeDtypeStruct((8, faces), F32), jax.ShapeDtypeStruct((count, 8, SLICE), F32)),
-        in_specs=[SMEM, SMEM, VMEM, VMEM, VMEM, VMEM],
+        in_specs=[SMEM, VMEM, VMEM, VMEM, VMEM],
         out_specs=(VMEM, VMEM),
         compiler_params=pltpu.CompilerParams(vmem_limit_bytes=60 * 1024 * 1024),
         name="prepare",
-    )(place, codes, centroids, normals, areas, codes)
+    )(codes, centroids, normals, areas, codes)
 
 
 def pack_kernel(own_ref, rows_ref, out_ref):
@@ -375,9 +375,9 @@
     core, slab = member % 2, member // 2
     other_block = slab * SLICE // BLOCK
 
-    place = jnp.stack([core, other_block, slab]).reshape(1, 3)
+    place = jnp.stack([core, other_block]).reshape(1, 2)
     codes = pair_code.transpose(0, 1, 3, 2).reshape(1, count)
-    own, chunks = prepare(place, codes, centroids, normals, areas.reshape(1, faces))
+    own, chunks = prepare(codes, centroids, normals, areas.reshape(1, faces))
     rows = lax.all_to_all(chunks, "blk", 0, 0)
 
     held = lax.all_to_all(pack_codes(own, rows, shares), "pair", 0, 0)

time: 93.3 us -> 92.3 us (0.989)
  blocking collectives: 51.8 us -> 16.7 us
  starting transfers between devices: 15.6 us -> 36 us
  waiting for transfers between devices: 2.9 us -> 15.4 us
  Pallas kernels: 18.9 us -> 19.9 us
    all_to_all x1 -> x0, blocking collectives: 35.9 us -> none  [shards(): rows = lax.all_to_all(chunks, 'blk', 0, 0)]
    all_to_all x0 -> x1, starting transfers between devices: none -> 23.3 us  [shards(): rows = lax.all_to_all(chunks, 'blk', 0, 0)]
    all_to_all x0 -> x1, waiting for transfers between devices: none -> 12.6 us  [shards(): rows = lax.all_to_all(chunks, 'blk', 0, 0)]
    ppermute x1, starting transfers between devices: 4.82 us -> 1.92 us  [shards(): halo = lax.ppermute(edge, ('blk', 'pair'), hops)]
    pallas_call x2, Pallas kernels: 12 us -> 13 us  [pair_call(): pl.pallas_call(body, out_shape=outputs, in_specs=in_specs, out_specs=jax....]
  transfers between devices with their start and end apart: 2 -> 3, of which waited for: 1 -> 2; matrix products, arithmetic and copies ran while one was open for 0% -> 0% of each run, Pallas kernels for 10% -> 9%
where the time goes in v9:
time: 92.3 us; the launch traced here: 91.1 us
  starting transfers between devices  36 us (39%)
  Pallas kernels  19.9 us (22%)
  blocking collectives  16.7 us (18%)
  waiting for transfers between devices  15.4 us (17%)
  local copies, waits for them, and re-layouts  1.48 us (2%)
  between operations  1.4 us (2%)
    all_to_all x1, starting transfers between devices, shards(): rows = lax.all_to_all(chunks, 'blk', 0, 0)  23.3 us
    all_gather x1, blocking collectives, shards(): parts = lax.all_gather(part, 'pair')  16.7 us
    pallas_call x2, Pallas kernels, pair_call(): pl.pallas_call(body, out_shape=outputs, in_specs=in_specs, out_specs=jax....  13 us
    all_to_all x1, waiting for transfers between devices, shards(): rows = lax.all_to_all(chunks, 'blk', 0, 0)  12.6 us
    all_to_all x1, starting transfers between devices, shards(): held = lax.all_to_all(pack_codes(own, rows, shares), 'pair', 0, 0)  10.8 us
    all_to_all x1, waiting for transfers between devices, shards(): held = lax.all_to_all(pack_codes(own, rows, shares), 'pair', 0, 0)  2.83 us
    ppermute x1, starting transfers between devices, shards(): halo = lax.ppermute(edge, ('blk', 'pair'), hops)  1.92 us
  transfers between devices with their start and end apart: 3, of which 2 were waited for; matrix products, arithmetic and copies ran while one was open for 0% of the time, Pallas kernels for 9%

profile of v9, /device:TPU:1, one launch (start us, length us, event | category | flops | bytes accessed | tf_op | source)
XLA Modules:
  0.0 91.1 jit_solution(10035645556218768880)
XLA Ops:
  0.6 1.6 %prepare.1 = (f32[8,1024]{1,0:T(8,128)}, f32[64,8,128]{2,1,0:T(8,128)}) custom-call(s32[1,64]{1,0:T(1,128)} %bitcast.12, f32[3,1024]{1,0:T(4,128)} %center_ref.1, f32[3,1024]{1,0:T(4,128)} %normal_ref.1, f32[1,1024]{1,0:T(1,128)} %bitcast.11, s32[1,64]{1,0:T(1,128)} %bitcast.13), custom_call_target="tpu_custom_call" | custom-call | tf_op jit(solution)/shard_map/prepare/pallas_call | solution.py:160
  2.2 0.0 copy-start.1
  2.2 23.3 %all-to-all-start = ((f32[64,8,128]{2,1,0:T(8,128)}), f32[64,8,128]{2,1,0:T(8,128)S(1)}, u32[]{:S(2)}, u32[]{:S(2)}) async-start(f32[64,8,128]{2,1,0:T(8,128)} %get-tuple-element.10), calls=%async_computation | async-start | bytes 524288 | tf_op jit(solution)/shard_map/all_to_all | solution.py:381
  25.5 12.6 %all-to-all-done.rows_ref.refs_4_ = f32[64,8,128]{2,1,0:T(8,128)S(1)} async-done(((f32[64,8,128]{2,1,0:T(8,128)}), f32[64,8,128]{2,1,0:T(8,128)S(1)}, u32[]{:S(2)}, u32[]{:S(2)}) %all-to-all-start) | async-done | bytes 262176 | tf_op jit(solution)/shard_map/all_to_all | solution.py:381
  38.2 0.0 copy-start
  38.2 0.8 copy-done
  38.9 0.7 pack_codes.1
  39.6 10.8 %all-to-all-start.1 = ((s32[16,1,128]{2,1,0:T(1,128)}), s32[16,1,128]{2,1,0:T(1,128)S(1)}, u32[]{:S(2)}, u32[]{:S(2)}) async-start(s32[16,1,128]{2,1,0:T(1,128)} %pack_codes.1), calls=%async_computation.1 | async-start | bytes 16384 | tf_op jit(solution)/shard_map/all_to_all | solution.py:383
  50.4 0.1 add_bitcast_fusion.place_ref.refs_0_
  51.1 0.0 copy-start.2
  51.1 0.7 copy-done.2
  51.8 1.6 %incidence.1.table_ref = bf16[512,1152]{1,0:T(8,128)(2,1)S(1)} custom-call(s32[3,1152]{1,0:T(4,128)S(1)} %copy-done.2), custom_call_target="tpu_custom_call" | custom-call | flops 5308416 | bytes 1179648 | tf_op jit(solution)/shard_map/incidence/pallas_call | solution.py:325
  53.4 0.0 copy-done.1
  53.4 1.1 %features.1 = (bf16[64,64,128]{2,1,0:T(8,128)(2,1)S(1)}, bf16[64,32,128]{2,1,0:T(8,128)(2,1)S(1)}, bf16[2,3,64,256]{3,2,1,0:T(8,128)(2,1)S(1)}) custom-call(s32[1,2]{1,0:T(1,128)S(1)} %add_bitcast_fusion.place_ref.refs_0_, f32[8,1024]{1,0:T(8,128)S(1)} %copy-done.1, f32[64,8,128]{2,1,0:T(8,128)S(1)} %all-to-all-done.rows_ref.refs_4_), custom_call_target="tpu_custom_call" | custom-call | flops 4194304 | bytes 1048576 | tf_op jit(solution)/shard_map/features/pallas_call | solution.py:91
  54.5 2.8 %all-to-all-done.1.held_ref = s32[16,1,128]{2,1,0:T(1,128)S(1)} async-done(((s32[16,1,128]{2,1,0:T(1,128)}), s32[16,1,128]{2,1,0:T(1,128)S(1)}, u32[]{:S(2)}, u32[]{:S(2)}) %all-to-all-start.1) | async-done | bytes 8224 | tf_op jit(solution)/shard_map/all_to_all | solution.py:383
  57.3 1.0 %tally.1.refs_1_ = s32[4,256]{1,0:T(4,128)S(1)} custom-call(s32[1,2]{1,0:T(1,128)S(1)} %add_bitcast_fusion.place_ref.refs_0_, s32[16,1,128]{2,1,0:T(1,128)S(1)} %all-to-all-done.1.held_ref), custom_call_target="tpu_custom_call" | custom-call | tf_op jit(solution)/shard_map/tally/pallas_call | solution.py:136
  58.3 7.5 %outer_block.1 = (f32[8,256]{1,0:T(8,128)S(1)}, f32[1,512]{1,0:T(1,128)S(1)}) custom-call(s32[1,2]{1,0:T(1,128)S(1)} %add_bitcast_fusion.place_ref.refs_0_, s32[4,256]{1,0:T(4,128)S(1)} %tally.1.refs_1_, f32[1,1]{1,0:T(1,128)} %bitcast.8.refs_2_, f32[8,1024]{1,0:T(8,128)S(1)} %copy-done.1, f32[64,8,128]{2,1,0:T(8,128)S(1)} %all-to-all-done.rows_ref.refs_4_, ...), custom_call_target="tpu_custom_call" | custom-call | flops 688128000 | bytes 2097152 | tf_op jit(solution)/shard_map/outer_block/pallas_call | solution.py:291
  65.8 1.9 %collective-permute-start = (f32[1,512]{1,0:T(1,128)S(1)}, f32[1,512]{1,0:T(1,128)S(1)}, u32[]{:S(2)}, u32[]{:S(2)}) collective-permute-start(f32[1,512]{1,0:T(1,128)S(1)} %get-tuple-element.15), channel_id=1, source_target_pairs={{0,16},{1,1009},{2,18},{3,1011},{4,20},{5,1013},{6,22},{7,1015},{8... | collective-permute-start | bytes 6152 | tf_op jit(solution)/shard_map/ppermute | solution.py:397
  67.7 5.5 %inner_block.1 = f32[8,256]{1,0:T(8,128)S(1)} custom-call(s32[1,2]{1,0:T(1,128)S(1)} %add_bitcast_fusion.place_ref.refs_0_, s32[4,256]{1,0:T(4,128)S(1)} %tally.1.refs_1_, f32[1,1]{1,0:T(1,128)} %bitcast.9.refs_2_, f32[8,1024]{1,0:T(8,128)S(1)} %copy-done.1, f32[64,8,128]{2,1,0:T(8,128)S(1)} %all-to-all-done.rows_ref.refs_4_, ...), custom_call_target="tpu_custom_call" | custom-call | flops 688128000 | bytes 2097152 | tf_op jit(solution)/shard_map/inner_block/pallas_call | solution.py:291
  73.3 0.0 collective-permute-done
  73.3 16.7 %all-gather = f32[128,512]{1,0:T(8,128)S(1)} all-gather(f32[8,512]{1,0:T(8,128)S(1)} %fusion), channel_id=2, replica_groups=mesh['blk'=64,'pair'=16] {'pair'}, dimensions={0}, use_global_device_ids=true | all-gather | bytes 278528 | tf_op jit(solution)/shard_map/all_gather | solution.py:400
  90.0 1.0 %finish.1 = (f32[3,512]{1,0:T(4,128)}, f32[4,1024]{1,0:T(4,128)}) custom-call(f32[16,8,512]{2,1,0:T(8,128)S(1)} %bitcast.10, bf16[512,1152]{1,0:T(8,128)(2,1)S(1)} %incidence.1.table_ref), custom_call_target="tpu_custom_call" | custom-call | tf_op jit(solution)/shard_map/finish/pallas_call | solution.py:360
  (1 shorter events, 0.0 us)
Async XLA Ops:
  2.2 51.2 %copy-start.1 = (f32[8,1024]{1,0:T(8,128)S(1)}, f32[8,1024]{1,0:T(8,128)}, u32[]{:S(2)}) copy-start(f32[8,1024]{1,0:T(8,128)} %get-tuple-element.9.own_ref.refs_3_) | copy-start | bytes 98308
  2.2 36.0 %all-to-all-start = ((f32[64,8,128]{2,1,0:T(8,128)}), f32[64,8,128]{2,1,0:T(8,128)S(1)}, u32[]{:S(2)}, u32[]{:S(2)}) async-start(f32[64,8,128]{2,1,0:T(8,128)} %get-tuple-element.10), calls=%async_computation | async-start | bytes 524288 | tf_op jit(solution)/shard_map/all_to_all | solution.py:381
  38.2 0.8 copy-start
  39.6 17.7 %all-to-all-start.1 = ((s32[16,1,128]{2,1,0:T(1,128)}), s32[16,1,128]{2,1,0:T(1,128)S(1)}, u32[]{:S(2)}, u32[]{:S(2)}) async-start(s32[16,1,128]{2,1,0:T(1,128)} %pack_codes.1), calls=%async_computation.1 | async-start | bytes 16384 | tf_op jit(solution)/shard_map/all_to_all | solution.py:383
  51.1 0.7 copy-start.2
  65.8 7.4 %collective-permute-start = (f32[1,512]{1,0:T(1,128)S(1)}, f32[1,512]{1,0:T(1,128)S(1)}, u32[]{:S(2)}, u32[]{:S(2)}) collective-permute-start(f32[1,512]{1,0:T(1,128)S(1)} %get-tuple-element.15), channel_id=1, source_target_pairs={{0,16},{1,1009},{2,18},{3,1011},{4,20},{5,1013},{6,22},{7,1015},{8... | collective-permute-start | bytes 6152 | tf_op jit(solution)/shard_map/ppermute | solution.py:397
